TPU v7x, 512 devices: a whole 4x4x16 slice. The times are simulated.
512 devices in a mesh: gx: 16 (over x, y), gy: 32 (over z, core).
Axes of the slice: x: 4, y: 4, z: 16, core: 2. Of those that a mesh axis runs over, the one named last changes fastest.
Arguments:
- pressure_rhs: float32 [128, 256, 256], P('gx', 'gy'), may hold values from -6 to 6
- storage_fine: float32 [128, 256, 256], P('gx', 'gy'), may hold values from 0.003 to 0.03
- mobility_fine: float32 [3, 128, 256, 256], P(None, 'gx', 'gy'), may hold values from 0.1 to 10
- storage_mid: float32 [64, 128, 128], P('gx', 'gy'), may hold values from 0.024 to 0.24
- mobility_mid: float32 [3, 64, 128, 128], P(None, 'gx', 'gy'), may hold values from 0.4 to 40
- storage_coarse: float32 [32, 64, 64], P('gx', 'gy'), may hold values from 0.19 to 1.9
- mobility_coarse: float32 [3, 32, 64, 64], P(None, 'gx', 'gy'), may hold values from 1.6 to 160
Outputs:
- pressure: float32 [128, 256, 256], P('gx', 'gy')
- residual: float32 [128, 256, 256], P('gx', 'gy')
All inputs are finite; a program needn't handle non-finite values.
Results may differ from a plain program's by a relative error of at most 0.0002.
Values sent between devices are 32-bit elements; how exact they have to be, the bound alone decides.
A program may use at most 192 MiB of HBM per device.

v0:
```python
import jax
import jax.numpy as jnp
from jax import lax
from jax.sharding import PartitionSpec as P

NU = 2
KC = 6
GROUP = 8


damping = 2.0 / 3.0


def padded_2(cells, sides, width):
    for axis, dim in sides:
        count = lax.axis_size(axis)
        ends = count - 1
        head = lax.slice_in_dim(cells, 0, width, axis=dim)
        tail = lax.slice_in_dim(cells, cells.shape[dim] - width, cells.shape[dim], axis=dim)
        cells = jnp.concatenate(
            [
                lax.ppermute(tail, axis, [(i, (i + 1) % count) for i in range(ends)]),
                cells,
                lax.ppermute(head, axis, [((i + 1) % count, i) for i in range(ends)]),
            ],
            axis=dim,
        )
    return cells


def harmonic(left, right):
    return 2.0 * left * right / (left + right)


def shifted(values, dim, upward):
    n = values.shape[dim]
    edge = jnp.zeros_like(lax.slice_in_dim(values, 0, 1, axis=dim))
    if upward:
        return jnp.concatenate([lax.slice_in_dim(values, 1, n, axis=dim), edge], axis=dim)
    return jnp.concatenate([edge, lax.slice_in_dim(values, 0, n - 1, axis=dim)], axis=dim)


def zero_padded(values, dim):
    widths = [(0, 0), (0, 0), (0, 0)]
    widths[dim] = (1, 1)
    return jnp.pad(values, widths)


def parts_from_padded(storage, padded_list):
    uppers = []
    lowers = []
    for dim in range(3):
        padded = padded_list[dim]
        n = padded.shape[dim]
        centre = lax.slice_in_dim(padded, 1, n - 1, axis=dim)
        uppers.append(harmonic(centre, lax.slice_in_dim(padded, 2, n, axis=dim)))
        lowers.append(harmonic(lax.slice_in_dim(padded, 0, n - 2, axis=dim), centre))
    diagonal = storage + (uppers[0] + lowers[0]) + (uppers[1] + lowers[1]) + (uppers[2] + lowers[2])
    return (uppers, lowers, diagonal)


def spread_parts(storage, mobility):
    rim_pads = padded_2(mobility[0:2], (("gx", 1), ("gy", 2)), 1)
    first_pad = rim_pads[0][:, 1:-1]
    second_pad = rim_pads[1][1:-1, :]
    return parts_from_padded(storage, [first_pad, second_pad, zero_padded(mobility[2], 2)])


def field_neighbours(values):
    padded = padded_2(values, (("gx", 0), ("gy", 1)), 1)
    nexts = (padded[2:, 1:-1], padded[1:-1, 2:], shifted(values, 2, True))
    prevs = (padded[:-2, 1:-1], padded[1:-1, :-2], shifted(values, 2, False))
    return (nexts, prevs)


def apply_operator(values, parts):
    uppers, lowers, diagonal = parts
    nexts, prevs = field_neighbours(values)
    total = diagonal * values
    for dim in range(3):
        total = total - uppers[dim] * nexts[dim] - lowers[dim] * prevs[dim]
    return total


def smooth(values, source, parts, sweeps):
    for turn in range(sweeps):
        values = values + damping * (source - apply_operator(values, parts)) / parts[2]
    return values


def smooth_zero(source, parts):
    values = damping * source / parts[2]
    return smooth(values, source, parts, NU - 1)


def restrict(values):
    a, b, c = values.shape
    return values.reshape(a // 2, 2, b // 2, 2, c // 2, 2).sum(axis=(1, 3, 5))


def prolong(values):
    return jnp.repeat(jnp.repeat(jnp.repeat(values, 2, axis=0), 2, axis=1), 2, axis=2)


def line_solve(lower_band, diagonal, upper_band, source):
    return lax.linalg.tridiagonal_solve(lower_band, diagonal, upper_band, source[..., None])[..., 0]


def coarse_sweeps(source, parts, lateral):
    uppers, lowers, diagonal = parts
    lower_band = -lowers[2]
    upper_band = -uppers[2]
    answer = line_solve(lower_band, diagonal, upper_band, source)
    for turn in range(KC - 1):
        nexts, prevs = lateral(answer)
        push = source + uppers[0] * nexts[0] + lowers[0] * prevs[0]
        push = push + uppers[1] * nexts[1] + lowers[1] * prevs[1]
        answer = line_solve(lower_band, diagonal, upper_band, push)
    return answer


def coarse_halo(values):
    return padded_2(values, (("gy", 1),), 1)


def coarse_correction(coarse_source, storage_coarse, mobility_coarse):
    position = (lax.axis_index("gy") - 2) % GROUP
    second_rims = coarse_halo(mobility_coarse[1])
    lower_rim = jnp.where(position > 0, second_rims[:, :1], jnp.zeros_like(second_rims[:, :1]))
    upper_rim = jnp.where(
        position < GROUP - 1, second_rims[:, -1:], jnp.zeros_like(second_rims[:, -1:])
    )
    second_pad = jnp.concatenate([lower_rim, mobility_coarse[1], upper_rim], axis=1)
    block_parts = parts_from_padded(
        storage_coarse,
        [zero_padded(mobility_coarse[0], 0), second_pad, zero_padded(mobility_coarse[2], 2)],
    )

    def spread_lateral(values):
        padded = coarse_halo(values)
        return (
            (shifted(values, 0, True), padded[:, 2:]),
            (shifted(values, 0, False), padded[:, :-2]),
        )

    return coarse_sweeps(coarse_source, block_parts, spread_lateral)


def local(
    pressure_rhs,
    storage_fine,
    mobility_fine,
    storage_mid,
    mobility_mid,
    storage_coarse,
    mobility_coarse,
):
    fine_parts = spread_parts(storage_fine, mobility_fine)
    fine_x = smooth_zero(pressure_rhs, fine_parts)
    fine_res = pressure_rhs - apply_operator(fine_x, fine_parts)
    mid_source = restrict(fine_res)
    mid_parts = spread_parts(storage_mid, mobility_mid)
    mid_y = smooth_zero(mid_source, mid_parts)
    mid_res = mid_source - apply_operator(mid_y, mid_parts)
    coarse_source = restrict(mid_res)
    coarse_z = coarse_correction(coarse_source, storage_coarse, mobility_coarse)
    mid_y = smooth(mid_y + prolong(coarse_z), mid_source, mid_parts, NU)
    fine_x = smooth(fine_x + prolong(mid_y), pressure_rhs, fine_parts, NU)
    residual = pressure_rhs - apply_operator(fine_x, fine_parts)
    return (fine_x, residual)


def solution(mesh):
    placed = (
        P("gx", "gy", None),
        P("gx", "gy", None),
        P(None, "gx", "gy", None),
        P("gx", "gy", None),
        P(None, "gx", "gy", None),
        P("gx", "gy", None),
        P(None, "gx", "gy", None),
    )
    return jax.shard_map(
        local,
        mesh=mesh,
        in_specs=placed,
        out_specs=(P("gx", "gy", None), P("gx", "gy", None)),
        check_vma=False,
    )
```

profile of v0, /device:TPU:231, one launch (start us, length us, event | category | flops | bytes accessed | tf_op | source)
XLA Modules:
  0.0 281.1 jit_solution(4894933371719632903)
XLA Ops:
  1.4 3.2 %collective-permute-start = (f32[2,1,8,256]{3,2,1,0:T(8,128)S(1)}, f32[2,1,8,256]{3,2,1,0:T(8,128)S(1)}, u32[]{:S(2)}, u32[]{:S(2)}) collective-permute-start(f32[2,1,8,256]{3,2,1,0:T(8,128)S(1)} %get-tuple-element.1048), channel_id=1, source_target_pairs={{0,32},{32,64},{64,96},{96,128},{128,160},{160,192},{192,224},{224... | collective-permute-start | bytes 49160 | tf_op jit(solution)/shard_map/ppermute | solution.py:22
  4.6 4.2 %collective-permute-start.1 = (f32[2,1,8,256]{3,2,1,0:T(8,128)S(1)}, f32[2,1,8,256]{3,2,1,0:T(8,128)S(1)}, u32[]{:S(2)}, u32[]{:S(2)}) collective-permute-start(f32[2,1,8,256]{3,2,1,0:T(8,128)S(1)} %get-tuple-element.1049), channel_id=1, source_target_pairs={{32,0},{64,32},{96,64},{128,96},{160,128},{192,160},{224,192},{256... | collective-permute-start | bytes 49160 | tf_op jit(solution)/shard_map/ppermute | solution.py:24
  11.5 5.5 %collective-permute-start.13 = (f32[2,1,4,128]{3,2,1,0:T(4,128)S(1)}, f32[2,1,4,128]{3,2,1,0:T(4,128)S(1)}, u32[]{:S(2)}, u32[]{:S(2)}) collective-permute-start(f32[2,1,4,128]{3,2,1,0:T(4,128)S(1)} %get-tuple-element.1110), channel_id=1, source_target_pairs={{32,0},{64,32},{96,64},{128,96},{160,128},{192,160},{224,192},{256... | collective-permute-start | bytes 12296 | tf_op jit(solution)/shard_map/ppermute | solution.py:24
  17.9 6.4 %collective-permute-start.25 = (f32[2,1,64]{1,0,2:T(2,128)S(1)}, f32[2,1,64]{1,0,2:T(2,128)S(1)}, u32[]{:S(2)}, u32[]{:S(2)}) collective-permute-start(f32[2,1,64]{1,0,2:T(2,128)S(1)} %get-tuple-element.1097), channel_id=1, source_target_pairs={{0,1},{1,2},{2,3},{3,4},{4,5},{5,6},{6,7},{7,8},{8,9},{9,10},{10,1... | collective-permute-start | bytes 1544 | tf_op jit(solution)/shard_map/ppermute | solution.py:22
  30.4 4.9 %collective-permute-start.14 = (f32[2,6,1,128]{3,0,2,1:T(2,128)S(1)}, f32[2,6,1,128]{3,0,2,1:T(2,128)S(1)}, u32[]{:S(2)}, u32[]{:S(2)}) collective-permute-start(f32[2,6,1,128]{3,0,2,1:T(2,128)S(1)} %copy.7464), channel_id=1, source_target_pairs={{0,1},{1,2},{2,3},{3,4},{4,5},{5,6},{6,7},{7,8},{8,9},{9,10},{10,1... | collective-permute-start | bytes 18440 | tf_op jit(solution)/shard_map/ppermute | solution.py:22
  37.3 4.2 %collective-permute-done.15 = f32[2,6,1,128]{3,0,2,1:T(2,128)S(1)} collective-permute-done((f32[2,6,1,128]{3,0,2,1:T(2,128)S(1)}, f32[2,6,1,128]{3,0,2,1:T(2,128)S(1)}, u32[]{:S(2)}, u32[]{:S(2)}) %collective-permute-start.15) | collective-permute-done | bytes 6176 | tf_op jit(solution)/shard_map/ppermute | solution.py:24
  46.0 3.9 %collective-permute-done.3 = f32[2,10,1,256]{3,0,2,1:T(2,128)S(1)} collective-permute-done((f32[2,10,1,256]{3,0,2,1:T(2,128)S(1)}, f32[2,10,1,256]{3,0,2,1:T(2,128)S(1)}, u32[]{:S(2)}, u32[]{:S(2)}) %collective-permute-start.3) | collective-permute-done | bytes 20512 | tf_op jit(solution)/shard_map/ppermute | solution.py:24
  52.9 3.4 %collective-permute-start.5 = (f32[1,8,256]{2,1,0:T(8,128)S(1)}, f32[1,8,256]{2,1,0:T(8,128)S(1)}, u32[]{:S(2)}, u32[]{:S(2)}) collective-permute-start(f32[1,8,256]{2,1,0:T(8,128)S(1)} %get-tuple-element.1105), channel_id=1, source_target_pairs={{0,32},{32,64},{64,96},{96,128},{128,160},{160,192},{192,224},{224... | collective-permute-start | bytes 24584 | tf_op jit(solution)/shard_map/ppermute | solution.py:22
  61.4 4.9 %collective-permute-start.7 = (f32[10,1,256]{2,1,0:T(1,128)S(1)}, f32[10,1,256]{2,1,0:T(1,128)S(1)}, u32[]{:S(2)}, u32[]{:S(2)}) collective-permute-start(f32[10,1,256]{2,1,0:T(1,128)S(1)} %get-tuple-element.1061), channel_id=1, source_target_pairs={{0,1},{1,2},{2,3},{3,4},{4,5},{5,6},{6,7},{7,8},{8,9},{9,10},{10,1... | collective-permute-start | bytes 30728 | tf_op jit(solution)/shard_map/ppermute | solution.py:22
  69.0 3.4 %collective-permute-start.9 = (f32[1,8,256]{2,1,0:T(8,128)S(1)}, f32[1,8,256]{2,1,0:T(8,128)S(1)}, u32[]{:S(2)}, u32[]{:S(2)}) collective-permute-start(f32[1,8,256]{2,1,0:T(8,128)S(1)} %get-tuple-element.1101), channel_id=1, source_target_pairs={{0,32},{32,64},{64,96},{96,128},{128,160},{160,192},{192,224},{224... | collective-permute-start | bytes 24584 | tf_op jit(solution)/shard_map/ppermute | solution.py:22
  77.5 6.6 %collective-permute-start.11 = (f32[10,1,256]{2,1,0:T(1,128)S(1)}, f32[10,1,256]{2,1,0:T(1,128)S(1)}, u32[]{:S(2)}, u32[]{:S(2)}) collective-permute-start(f32[10,1,256]{2,1,0:T(1,128)S(1)} %get-tuple-element.1059), channel_id=1, source_target_pairs={{0,1},{1,2},{2,3},{3,4},{4,5},{5,6},{6,7},{7,8},{8,9},{9,10},{10,1... | collective-permute-start | bytes 30728 | tf_op jit(solution)/shard_map/ppermute | solution.py:22
  85.0 5.5 %reshape.6212 = f32[4,2,4,2,128,2]{5,4,3,2,1,0:T(8,128)} reshape(f32[8,8,256]{2,1,0:T(8,128)S(1)} %fusion.73) | data formatting | bytes 131072 | tf_op jit(solution)/shard_map/reshape | solution.py:98
  95.1 3.4 %collective-permute-start.17 = (f32[1,4,128]{2,1,0:T(4,128)S(1)}, f32[1,4,128]{2,1,0:T(4,128)S(1)}, u32[]{:S(2)}, u32[]{:S(2)}) collective-permute-start(f32[1,4,128]{2,1,0:T(4,128)S(1)} %get-tuple-element.1133), channel_id=1, source_target_pairs={{0,32},{32,64},{64,96},{96,128},{128,160},{160,192},{192,224},{224... | collective-permute-start | bytes 6152 | tf_op jit(solution)/shard_map/ppermute | solution.py:22
  103.5 6.6 %collective-permute-start.19 = (f32[6,1,128]{2,1,0:T(1,128)S(1)}, f32[6,1,128]{2,1,0:T(1,128)S(1)}, u32[]{:S(2)}, u32[]{:S(2)}) collective-permute-start(f32[6,1,128]{2,1,0:T(1,128)S(1)} %get-tuple-element.1118), channel_id=1, source_target_pairs={{0,1},{1,2},{2,3},{3,4},{4,5},{5,6},{6,7},{7,8},{8,9},{9,10},{10,1... | collective-permute-start | bytes 9224 | tf_op jit(solution)/shard_map/ppermute | solution.py:22
  112.8 3.4 %collective-permute-start.21 = (f32[1,4,128]{2,1,0:T(4,128)S(1)}, f32[1,4,128]{2,1,0:T(4,128)S(1)}, u32[]{:S(2)}, u32[]{:S(2)}) collective-permute-start(f32[1,4,128]{2,1,0:T(4,128)S(1)} %get-tuple-element.1129), channel_id=1, source_target_pairs={{0,32},{32,64},{64,96},{96,128},{128,160},{160,192},{192,224},{224... | collective-permute-start | bytes 6152 | tf_op jit(solution)/shard_map/ppermute | solution.py:22
  121.1 6.5 %collective-permute-start.23 = (f32[6,1,128]{2,1,0:T(1,128)S(1)}, f32[6,1,128]{2,1,0:T(1,128)S(1)}, u32[]{:S(2)}, u32[]{:S(2)}) collective-permute-start(f32[6,1,128]{2,1,0:T(1,128)S(1)} %get-tuple-element.1116), channel_id=1, source_target_pairs={{0,1},{1,2},{2,3},{3,4},{4,5},{5,6},{6,7},{7,8},{8,9},{9,10},{10,1... | collective-permute-start | bytes 9224 | tf_op jit(solution)/shard_map/ppermute | solution.py:22
  133.9 5.4 %collective-permute-start.27 = (f32[2,1,64]{1,0,2:T(2,128)S(1)}, f32[2,1,64]{1,0,2:T(2,128)S(1)}, u32[]{:S(2)}, u32[]{:S(2)}) collective-permute-start(f32[2,1,64]{1,0,2:T(2,128)S(1)} %get-tuple-element.1093), channel_id=1, source_target_pairs={{0,1},{1,2},{2,3},{3,4},{4,5},{5,6},{6,7},{7,8},{8,9},{9,10},{10,1... | collective-permute-start | bytes 1544 | tf_op jit(solution)/shard_map/ppermute | solution.py:22
  144.4 5.5 %collective-permute-start.29 = (f32[2,1,64]{1,0,2:T(2,128)S(1)}, f32[2,1,64]{1,0,2:T(2,128)S(1)}, u32[]{:S(2)}, u32[]{:S(2)}) collective-permute-start(f32[2,1,64]{1,0,2:T(2,128)S(1)} %get-tuple-element.1089), channel_id=1, source_target_pairs={{0,1},{1,2},{2,3},{3,4},{4,5},{5,6},{6,7},{7,8},{8,9},{9,10},{10,1... | collective-permute-start | bytes 1544 | tf_op jit(solution)/shard_map/ppermute | solution.py:22
  154.9 5.7 %collective-permute-start.31 = (f32[2,1,64]{1,0,2:T(2,128)S(1)}, f32[2,1,64]{1,0,2:T(2,128)S(1)}, u32[]{:S(2)}, u32[]{:S(2)}) collective-permute-start(f32[2,1,64]{1,0,2:T(2,128)S(1)} %get-tuple-element.1085), channel_id=1, source_target_pairs={{0,1},{1,2},{2,3},{3,4},{4,5},{5,6},{6,7},{7,8},{8,9},{9,10},{10,1... | collective-permute-start | bytes 1544 | tf_op jit(solution)/shard_map/ppermute | solution.py:22
  165.4 5.5 %collective-permute-start.33 = (f32[2,1,64]{1,0,2:T(2,128)S(1)}, f32[2,1,64]{1,0,2:T(2,128)S(1)}, u32[]{:S(2)}, u32[]{:S(2)}) collective-permute-start(f32[2,1,64]{1,0,2:T(2,128)S(1)} %get-tuple-element.1081), channel_id=1, source_target_pairs={{0,1},{1,2},{2,3},{3,4},{4,5},{5,6},{6,7},{7,8},{8,9},{9,10},{10,1... | collective-permute-start | bytes 1544 | tf_op jit(solution)/shard_map/ppermute | solution.py:22
  176.0 5.5 %collective-permute-start.35 = (f32[2,1,64]{1,0,2:T(2,128)S(1)}, f32[2,1,64]{1,0,2:T(2,128)S(1)}, u32[]{:S(2)}, u32[]{:S(2)}) collective-permute-start(f32[2,1,64]{1,0,2:T(2,128)S(1)} %get-tuple-element.1077), channel_id=1, source_target_pairs={{0,1},{1,2},{2,3},{3,4},{4,5},{5,6},{6,7},{7,8},{8,9},{9,10},{10,1... | collective-permute-start | bytes 1544 | tf_op jit(solution)/shard_map/ppermute | solution.py:22
  192.8 3.4 %collective-permute-start.37 = (f32[1,4,128]{2,1,0:T(4,128)S(1)}, f32[1,4,128]{2,1,0:T(4,128)S(1)}, u32[]{:S(2)}, u32[]{:S(2)}) collective-permute-start(f32[1,4,128]{2,1,0:T(4,128)S(1)} %get-tuple-element.1125), channel_id=1, source_target_pairs={{0,32},{32,64},{64,96},{96,128},{128,160},{160,192},{192,224},{224... | collective-permute-start | bytes 6152 | tf_op jit(solution)/shard_map/ppermute | solution.py:22
  201.1 6.6 %collective-permute-start.39 = (f32[6,1,128]{2,1,0:T(1,128)S(1)}, f32[6,1,128]{2,1,0:T(1,128)S(1)}, u32[]{:S(2)}, u32[]{:S(2)}) collective-permute-start(f32[6,1,128]{2,1,0:T(1,128)S(1)} %get-tuple-element.1114), channel_id=1, source_target_pairs={{0,1},{1,2},{2,3},{3,4},{4,5},{5,6},{6,7},{7,8},{8,9},{9,10},{10,1... | collective-permute-start | bytes 9224 | tf_op jit(solution)/shard_map/ppermute | solution.py:22
  210.5 3.4 %collective-permute-start.41 = (f32[1,4,128]{2,1,0:T(4,128)S(1)}, f32[1,4,128]{2,1,0:T(4,128)S(1)}, u32[]{:S(2)}, u32[]{:S(2)}) collective-permute-start(f32[1,4,128]{2,1,0:T(4,128)S(1)} %get-tuple-element.1121), channel_id=1, source_target_pairs={{0,32},{32,64},{64,96},{96,128},{128,160},{160,192},{192,224},{224... | collective-permute-start | bytes 6152 | tf_op jit(solution)/shard_map/ppermute | solution.py:22
  218.9 6.5 %collective-permute-start.43 = (f32[6,1,128]{2,1,0:T(1,128)S(1)}, f32[6,1,128]{2,1,0:T(1,128)S(1)}, u32[]{:S(2)}, u32[]{:S(2)}) collective-permute-start(f32[6,1,128]{2,1,0:T(1,128)S(1)} %get-tuple-element.1112), channel_id=1, source_target_pairs={{0,1},{1,2},{2,3},{3,4},{4,5},{5,6},{6,7},{7,8},{8,9},{9,10},{10,1... | collective-permute-start | bytes 9224 | tf_op jit(solution)/shard_map/ppermute | solution.py:22
  228.9 3.4 %collective-permute-start.45 = (f32[1,8,256]{2,1,0:T(8,128)S(1)}, f32[1,8,256]{2,1,0:T(8,128)S(1)}, u32[]{:S(2)}, u32[]{:S(2)}) collective-permute-start(f32[1,8,256]{2,1,0:T(8,128)S(1)} %get-tuple-element.1072), channel_id=1, source_target_pairs={{0,32},{32,64},{64,96},{96,128},{128,160},{160,192},{192,224},{224... | collective-permute-start | bytes 24584 | tf_op jit(solution)/shard_map/ppermute | solution.py:22
  232.3 3.1 %collective-permute-done.45 = f32[1,8,256]{2,1,0:T(8,128)S(1)} collective-permute-done((f32[1,8,256]{2,1,0:T(8,128)S(1)}, f32[1,8,256]{2,1,0:T(8,128)S(1)}, u32[]{:S(2)}, u32[]{:S(2)}) %collective-permute-start.45) | collective-permute-done | bytes 8224 | tf_op jit(solution)/shard_map/ppermute | solution.py:22
  237.4 6.5 %collective-permute-start.47 = (f32[10,1,256]{2,1,0:T(1,128)S(1)}, f32[10,1,256]{2,1,0:T(1,128)S(1)}, u32[]{:S(2)}, u32[]{:S(2)}) collective-permute-start(f32[10,1,256]{2,1,0:T(1,128)S(1)} %get-tuple-element.1057), channel_id=1, source_target_pairs={{0,1},{1,2},{2,3},{3,4},{4,5},{5,6},{6,7},{7,8},{8,9},{9,10},{10,1... | collective-permute-start | bytes 30728 | tf_op jit(solution)/shard_map/ppermute | solution.py:22
  246.7 3.4 %collective-permute-start.49 = (f32[1,8,256]{2,1,0:T(8,128)S(1)}, f32[1,8,256]{2,1,0:T(8,128)S(1)}, u32[]{:S(2)}, u32[]{:S(2)}) collective-permute-start(f32[1,8,256]{2,1,0:T(8,128)S(1)} %get-tuple-element.1068), channel_id=1, source_target_pairs={{0,32},{32,64},{64,96},{96,128},{128,160},{160,192},{192,224},{224... | collective-permute-start | bytes 24584 | tf_op jit(solution)/shard_map/ppermute | solution.py:22
  255.2 6.6 %collective-permute-start.51 = (f32[10,1,256]{2,1,0:T(1,128)S(1)}, f32[10,1,256]{2,1,0:T(1,128)S(1)}, u32[]{:S(2)}, u32[]{:S(2)}) collective-permute-start(f32[10,1,256]{2,1,0:T(1,128)S(1)} %get-tuple-element.1055), channel_id=1, source_target_pairs={{0,1},{1,2},{2,3},{3,4},{4,5},{5,6},{6,7},{7,8},{8,9},{9,10},{10,1... | collective-permute-start | bytes 30728 | tf_op jit(solution)/shard_map/ppermute | solution.py:22
  264.6 3.4 %collective-permute-start.53 = (f32[1,8,256]{2,1,0:T(8,128)S(1)}, f32[1,8,256]{2,1,0:T(8,128)S(1)}, u32[]{:S(2)}, u32[]{:S(2)}) collective-permute-start(f32[1,8,256]{2,1,0:T(8,128)S(1)} %get-tuple-element.1064), channel_id=1, source_target_pairs={{0,32},{32,64},{64,96},{96,128},{128,160},{160,192},{192,224},{224... | collective-permute-start | bytes 24584 | tf_op jit(solution)/shard_map/ppermute | solution.py:22
  273.1 6.6 %collective-permute-start.55 = (f32[10,1,256]{2,1,0:T(1,128)S(1)}, f32[10,1,256]{2,1,0:T(1,128)S(1)}, u32[]{:S(2)}, u32[]{:S(2)}) collective-permute-start(f32[10,1,256]{2,1,0:T(1,128)S(1)} %get-tuple-element.1053), channel_id=1, source_target_pairs={{0,1},{1,2},{2,3},{3,4},{4,5},{5,6},{6,7},{7,8},{8,9},{9,10},{10,1... | collective-permute-start | bytes 30728 | tf_op jit(solution)/shard_map/ppermute | solution.py:22
  (643 shorter events, 122.4 us)
Async XLA Ops:
  1.4 40.0 %collective-permute-start = (f32[2,1,8,256]{3,2,1,0:T(8,128)S(1)}, f32[2,1,8,256]{3,2,1,0:T(8,128)S(1)}, u32[]{:S(2)}, u32[]{:S(2)}) collective-permute-start(f32[2,1,8,256]{3,2,1,0:T(8,128)S(1)} %get-tuple-element.1048), channel_id=1, source_target_pairs={{0,32},{32,64},{64,96},{96,128},{128,160},{160,192},{192,224},{224... | collective-permute-start | bytes 49160 | tf_op jit(solution)/shard_map/ppermute | solution.py:22
  4.6 36.8 %collective-permute-start.1 = (f32[2,1,8,256]{3,2,1,0:T(8,128)S(1)}, f32[2,1,8,256]{3,2,1,0:T(8,128)S(1)}, u32[]{:S(2)}, u32[]{:S(2)}) collective-permute-start(f32[2,1,8,256]{3,2,1,0:T(8,128)S(1)} %get-tuple-element.1049), channel_id=1, source_target_pairs={{32,0},{64,32},{96,64},{128,96},{160,128},{192,160},{224,192},{256... | collective-permute-start | bytes 49160 | tf_op jit(solution)/shard_map/ppermute | solution.py:24
  9.5 20.8 %collective-permute-start.12 = (f32[2,1,4,128]{3,2,1,0:T(4,128)S(1)}, f32[2,1,4,128]{3,2,1,0:T(4,128)S(1)}, u32[]{:S(2)}, u32[]{:S(2)}) collective-permute-start(f32[2,1,4,128]{3,2,1,0:T(4,128)S(1)} %get-tuple-element.1109), channel_id=1, source_target_pairs={{0,32},{32,64},{64,96},{96,128},{128,160},{160,192},{192,224},{224... | collective-permute-start | bytes 12296 | tf_op jit(solution)/shard_map/ppermute | solution.py:22
  11.5 18.9 %collective-permute-start.13 = (f32[2,1,4,128]{3,2,1,0:T(4,128)S(1)}, f32[2,1,4,128]{3,2,1,0:T(4,128)S(1)}, u32[]{:S(2)}, u32[]{:S(2)}) collective-permute-start(f32[2,1,4,128]{3,2,1,0:T(4,128)S(1)} %get-tuple-element.1110), channel_id=1, source_target_pairs={{32,0},{64,32},{96,64},{128,96},{160,128},{192,160},{224,192},{256... | collective-permute-start | bytes 12296 | tf_op jit(solution)/shard_map/ppermute | solution.py:24
  17.9 10.5 %collective-permute-start.25 = (f32[2,1,64]{1,0,2:T(2,128)S(1)}, f32[2,1,64]{1,0,2:T(2,128)S(1)}, u32[]{:S(2)}, u32[]{:S(2)}) collective-permute-start(f32[2,1,64]{1,0,2:T(2,128)S(1)} %get-tuple-element.1097), channel_id=1, source_target_pairs={{0,1},{1,2},{2,3},{3,4},{4,5},{5,6},{6,7},{7,8},{8,9},{9,10},{10,1... | collective-permute-start | bytes 1544 | tf_op jit(solution)/shard_map/ppermute | solution.py:22
  28.4 8.8 %collective-permute-start.24 = (f32[2,1,64]{1,0,2:T(2,128)S(1)}, f32[2,1,64]{1,0,2:T(2,128)S(1)}, u32[]{:S(2)}, u32[]{:S(2)}) collective-permute-start(f32[2,1,64]{1,0,2:T(2,128)S(1)} %get-tuple-element.1096), channel_id=1, source_target_pairs={{1,0},{2,1},{3,2},{4,3},{5,4},{6,5},{7,6},{8,7},{9,8},{10,9},{11,1... | collective-permute-start | bytes 1544 | tf_op jit(solution)/shard_map/ppermute | solution.py:24
  30.4 6.9 %collective-permute-start.14 = (f32[2,6,1,128]{3,0,2,1:T(2,128)S(1)}, f32[2,6,1,128]{3,0,2,1:T(2,128)S(1)}, u32[]{:S(2)}, u32[]{:S(2)}) collective-permute-start(f32[2,6,1,128]{3,0,2,1:T(2,128)S(1)} %copy.7464), channel_id=1, source_target_pairs={{0,1},{1,2},{2,3},{3,4},{4,5},{5,6},{6,7},{7,8},{8,9},{9,10},{10,1... | collective-permute-start | bytes 18440 | tf_op jit(solution)/shard_map/ppermute | solution.py:22
  59.4 6.9 %collective-permute-start.6 = (f32[10,1,256]{2,1,0:T(1,128)S(1)}, f32[10,1,256]{2,1,0:T(1,128)S(1)}, u32[]{:S(2)}, u32[]{:S(2)}) collective-permute-start(f32[10,1,256]{2,1,0:T(1,128)S(1)} %get-tuple-element.1060), channel_id=1, source_target_pairs={{1,0},{2,1},{3,2},{4,3},{5,4},{6,5},{7,6},{8,7},{9,8},{10,9},{11,1... | collective-permute-start | bytes 30728 | tf_op jit(solution)/shard_map/ppermute | solution.py:24
  75.6 8.6 %collective-permute-start.10 = (f32[10,1,256]{2,1,0:T(1,128)S(1)}, f32[10,1,256]{2,1,0:T(1,128)S(1)}, u32[]{:S(2)}, u32[]{:S(2)}) collective-permute-start(f32[10,1,256]{2,1,0:T(1,128)S(1)} %get-tuple-element.1058), channel_id=1, source_target_pairs={{1,0},{2,1},{3,2},{4,3},{5,4},{6,5},{7,6},{8,7},{9,8},{10,9},{11,1... | collective-permute-start | bytes 30728 | tf_op jit(solution)/shard_map/ppermute | solution.py:24
  77.5 7.4 %collective-permute-start.11 = (f32[10,1,256]{2,1,0:T(1,128)S(1)}, f32[10,1,256]{2,1,0:T(1,128)S(1)}, u32[]{:S(2)}, u32[]{:S(2)}) collective-permute-start(f32[10,1,256]{2,1,0:T(1,128)S(1)} %get-tuple-element.1059), channel_id=1, source_target_pairs={{0,1},{1,2},{2,3},{3,4},{4,5},{5,6},{6,7},{7,8},{8,9},{9,10},{10,1... | collective-permute-start | bytes 30728 | tf_op jit(solution)/shard_map/ppermute | solution.py:22
  101.5 8.6 %collective-permute-start.18 = (f32[6,1,128]{2,1,0:T(1,128)S(1)}, f32[6,1,128]{2,1,0:T(1,128)S(1)}, u32[]{:S(2)}, u32[]{:S(2)}) collective-permute-start(f32[6,1,128]{2,1,0:T(1,128)S(1)} %get-tuple-element.1117), channel_id=1, source_target_pairs={{1,0},{2,1},{3,2},{4,3},{5,4},{6,5},{7,6},{8,7},{9,8},{10,9},{11,1... | collective-permute-start | bytes 9224 | tf_op jit(solution)/shard_map/ppermute | solution.py:24
  103.5 7.3 %collective-permute-start.19 = (f32[6,1,128]{2,1,0:T(1,128)S(1)}, f32[6,1,128]{2,1,0:T(1,128)S(1)}, u32[]{:S(2)}, u32[]{:S(2)}) collective-permute-start(f32[6,1,128]{2,1,0:T(1,128)S(1)} %get-tuple-element.1118), channel_id=1, source_target_pairs={{0,1},{1,2},{2,3},{3,4},{4,5},{5,6},{6,7},{7,8},{8,9},{9,10},{10,1... | collective-permute-start | bytes 9224 | tf_op jit(solution)/shard_map/ppermute | solution.py:22
  119.2 8.6 %collective-permute-start.22 = (f32[6,1,128]{2,1,0:T(1,128)S(1)}, f32[6,1,128]{2,1,0:T(1,128)S(1)}, u32[]{:S(2)}, u32[]{:S(2)}) collective-permute-start(f32[6,1,128]{2,1,0:T(1,128)S(1)} %get-tuple-element.1115), channel_id=1, source_target_pairs={{1,0},{2,1},{3,2},{4,3},{5,4},{6,5},{7,6},{8,7},{9,8},{10,9},{11,1... | collective-permute-start | bytes 9224 | tf_op jit(solution)/shard_map/ppermute | solution.py:24
  121.1 7.3 %collective-permute-start.23 = (f32[6,1,128]{2,1,0:T(1,128)S(1)}, f32[6,1,128]{2,1,0:T(1,128)S(1)}, u32[]{:S(2)}, u32[]{:S(2)}) collective-permute-start(f32[6,1,128]{2,1,0:T(1,128)S(1)} %get-tuple-element.1116), channel_id=1, source_target_pairs={{0,1},{1,2},{2,3},{3,4},{4,5},{5,6},{6,7},{7,8},{8,9},{9,10},{10,1... | collective-permute-start | bytes 9224 | tf_op jit(solution)/shard_map/ppermute | solution.py:22
  132.0 7.5 %collective-permute-start.26 = (f32[2,1,64]{1,0,2:T(2,128)S(1)}, f32[2,1,64]{1,0,2:T(2,128)S(1)}, u32[]{:S(2)}, u32[]{:S(2)}) collective-permute-start(f32[2,1,64]{1,0,2:T(2,128)S(1)} %get-tuple-element.1092), channel_id=1, source_target_pairs={{1,0},{2,1},{3,2},{4,3},{5,4},{6,5},{7,6},{8,7},{9,8},{10,9},{11,1... | collective-permute-start | bytes 1544 | tf_op jit(solution)/shard_map/ppermute | solution.py:24
  142.4 7.5 %collective-permute-start.28 = (f32[2,1,64]{1,0,2:T(2,128)S(1)}, f32[2,1,64]{1,0,2:T(2,128)S(1)}, u32[]{:S(2)}, u32[]{:S(2)}) collective-permute-start(f32[2,1,64]{1,0,2:T(2,128)S(1)} %get-tuple-element.1088), channel_id=1, source_target_pairs={{1,0},{2,1},{3,2},{4,3},{5,4},{6,5},{7,6},{8,7},{9,8},{10,9},{11,1... | collective-permute-start | bytes 1544 | tf_op jit(solution)/shard_map/ppermute | solution.py:24
  144.4 6.8 %collective-permute-start.29 = (f32[2,1,64]{1,0,2:T(2,128)S(1)}, f32[2,1,64]{1,0,2:T(2,128)S(1)}, u32[]{:S(2)}, u32[]{:S(2)}) collective-permute-start(f32[2,1,64]{1,0,2:T(2,128)S(1)} %get-tuple-element.1089), channel_id=1, source_target_pairs={{0,1},{1,2},{2,3},{3,4},{4,5},{5,6},{6,7},{7,8},{8,9},{9,10},{10,1... | collective-permute-start | bytes 1544 | tf_op jit(solution)/shard_map/ppermute | solution.py:22
  153.0 7.7 %collective-permute-start.30 = (f32[2,1,64]{1,0,2:T(2,128)S(1)}, f32[2,1,64]{1,0,2:T(2,128)S(1)}, u32[]{:S(2)}, u32[]{:S(2)}) collective-permute-start(f32[2,1,64]{1,0,2:T(2,128)S(1)} %get-tuple-element.1084), channel_id=1, source_target_pairs={{1,0},{2,1},{3,2},{4,3},{5,4},{6,5},{7,6},{8,7},{9,8},{10,9},{11,1... | collective-permute-start | bytes 1544 | tf_op jit(solution)/shard_map/ppermute | solution.py:24
  154.9 6.8 %collective-permute-start.31 = (f32[2,1,64]{1,0,2:T(2,128)S(1)}, f32[2,1,64]{1,0,2:T(2,128)S(1)}, u32[]{:S(2)}, u32[]{:S(2)}) collective-permute-start(f32[2,1,64]{1,0,2:T(2,128)S(1)} %get-tuple-element.1085), channel_id=1, source_target_pairs={{0,1},{1,2},{2,3},{3,4},{4,5},{5,6},{6,7},{7,8},{8,9},{9,10},{10,1... | collective-permute-start | bytes 1544 | tf_op jit(solution)/shard_map/ppermute | solution.py:22
  163.5 7.5 %collective-permute-start.32 = (f32[2,1,64]{1,0,2:T(2,128)S(1)}, f32[2,1,64]{1,0,2:T(2,128)S(1)}, u32[]{:S(2)}, u32[]{:S(2)}) collective-permute-start(f32[2,1,64]{1,0,2:T(2,128)S(1)} %get-tuple-element.1080), channel_id=1, source_target_pairs={{1,0},{2,1},{3,2},{4,3},{5,4},{6,5},{7,6},{8,7},{9,8},{10,9},{11,1... | collective-permute-start | bytes 1544 | tf_op jit(solution)/shard_map/ppermute | solution.py:24
  165.4 6.8 %collective-permute-start.33 = (f32[2,1,64]{1,0,2:T(2,128)S(1)}, f32[2,1,64]{1,0,2:T(2,128)S(1)}, u32[]{:S(2)}, u32[]{:S(2)}) collective-permute-start(f32[2,1,64]{1,0,2:T(2,128)S(1)} %get-tuple-element.1081), channel_id=1, source_target_pairs={{0,1},{1,2},{2,3},{3,4},{4,5},{5,6},{6,7},{7,8},{8,9},{9,10},{10,1... | collective-permute-start | bytes 1544 | tf_op jit(solution)/shard_map/ppermute | solution.py:22
  174.0 7.5 %collective-permute-start.34 = (f32[2,1,64]{1,0,2:T(2,128)S(1)}, f32[2,1,64]{1,0,2:T(2,128)S(1)}, u32[]{:S(2)}, u32[]{:S(2)}) collective-permute-start(f32[2,1,64]{1,0,2:T(2,128)S(1)} %get-tuple-element.1076), channel_id=1, source_target_pairs={{1,0},{2,1},{3,2},{4,3},{5,4},{6,5},{7,6},{8,7},{9,8},{10,9},{11,1... | collective-permute-start | bytes 1544 | tf_op jit(solution)/shard_map/ppermute | solution.py:24
  199.2 8.6 %collective-permute-start.38 = (f32[6,1,128]{2,1,0:T(1,128)S(1)}, f32[6,1,128]{2,1,0:T(1,128)S(1)}, u32[]{:S(2)}, u32[]{:S(2)}) collective-permute-start(f32[6,1,128]{2,1,0:T(1,128)S(1)} %get-tuple-element.1113), channel_id=1, source_target_pairs={{1,0},{2,1},{3,2},{4,3},{5,4},{6,5},{7,6},{8,7},{9,8},{10,9},{11,1... | collective-permute-start | bytes 9224 | tf_op jit(solution)/shard_map/ppermute | solution.py:24
  201.1 7.4 %collective-permute-start.39 = (f32[6,1,128]{2,1,0:T(1,128)S(1)}, f32[6,1,128]{2,1,0:T(1,128)S(1)}, u32[]{:S(2)}, u32[]{:S(2)}) collective-permute-start(f32[6,1,128]{2,1,0:T(1,128)S(1)} %get-tuple-element.1114), channel_id=1, source_target_pairs={{0,1},{1,2},{2,3},{3,4},{4,5},{5,6},{6,7},{7,8},{8,9},{9,10},{10,1... | collective-permute-start | bytes 9224 | tf_op jit(solution)/shard_map/ppermute | solution.py:22
  216.9 8.6 %collective-permute-start.42 = (f32[6,1,128]{2,1,0:T(1,128)S(1)}, f32[6,1,128]{2,1,0:T(1,128)S(1)}, u32[]{:S(2)}, u32[]{:S(2)}) collective-permute-start(f32[6,1,128]{2,1,0:T(1,128)S(1)} %get-tuple-element.1111), channel_id=1, source_target_pairs={{1,0},{2,1},{3,2},{4,3},{5,4},{6,5},{7,6},{8,7},{9,8},{10,9},{11,1... | collective-permute-start | bytes 9224 | tf_op jit(solution)/shard_map/ppermute | solution.py:24
  218.9 7.3 %collective-permute-start.43 = (f32[6,1,128]{2,1,0:T(1,128)S(1)}, f32[6,1,128]{2,1,0:T(1,128)S(1)}, u32[]{:S(2)}, u32[]{:S(2)}) collective-permute-start(f32[6,1,128]{2,1,0:T(1,128)S(1)} %get-tuple-element.1112), channel_id=1, source_target_pairs={{0,1},{1,2},{2,3},{3,4},{4,5},{5,6},{6,7},{7,8},{8,9},{9,10},{10,1... | collective-permute-start | bytes 9224 | tf_op jit(solution)/shard_map/ppermute | solution.py:22
  235.4 8.6 %collective-permute-start.46 = (f32[10,1,256]{2,1,0:T(1,128)S(1)}, f32[10,1,256]{2,1,0:T(1,128)S(1)}, u32[]{:S(2)}, u32[]{:S(2)}) collective-permute-start(f32[10,1,256]{2,1,0:T(1,128)S(1)} %get-tuple-element.1056), channel_id=1, source_target_pairs={{1,0},{2,1},{3,2},{4,3},{5,4},{6,5},{7,6},{8,7},{9,8},{10,9},{11,1... | collective-permute-start | bytes 30728 | tf_op jit(solution)/shard_map/ppermute | solution.py:24
  237.4 7.3 %collective-permute-start.47 = (f32[10,1,256]{2,1,0:T(1,128)S(1)}, f32[10,1,256]{2,1,0:T(1,128)S(1)}, u32[]{:S(2)}, u32[]{:S(2)}) collective-permute-start(f32[10,1,256]{2,1,0:T(1,128)S(1)} %get-tuple-element.1057), channel_id=1, source_target_pairs={{0,1},{1,2},{2,3},{3,4},{4,5},{5,6},{6,7},{7,8},{8,9},{9,10},{10,1... | collective-permute-start | bytes 30728 | tf_op jit(solution)/shard_map/ppermute | solution.py:22
  253.3 8.6 %collective-permute-start.50 = (f32[10,1,256]{2,1,0:T(1,128)S(1)}, f32[10,1,256]{2,1,0:T(1,128)S(1)}, u32[]{:S(2)}, u32[]{:S(2)}) collective-permute-start(f32[10,1,256]{2,1,0:T(1,128)S(1)} %get-tuple-element.1054), channel_id=1, source_target_pairs={{1,0},{2,1},{3,2},{4,3},{5,4},{6,5},{7,6},{8,7},{9,8},{10,9},{11,1... | collective-permute-start | bytes 30728 | tf_op jit(solution)/shard_map/ppermute | solution.py:24
  255.2 7.4 %collective-permute-start.51 = (f32[10,1,256]{2,1,0:T(1,128)S(1)}, f32[10,1,256]{2,1,0:T(1,128)S(1)}, u32[]{:S(2)}, u32[]{:S(2)}) collective-permute-start(f32[10,1,256]{2,1,0:T(1,128)S(1)} %get-tuple-element.1055), channel_id=1, source_target_pairs={{0,1},{1,2},{2,3},{3,4},{4,5},{5,6},{6,7},{7,8},{8,9},{9,10},{10,1... | collective-permute-start | bytes 30728 | tf_op jit(solution)/shard_map/ppermute | solution.py:22
  271.1 8.6 %collective-permute-start.54 = (f32[10,1,256]{2,1,0:T(1,128)S(1)}, f32[10,1,256]{2,1,0:T(1,128)S(1)}, u32[]{:S(2)}, u32[]{:S(2)}) collective-permute-start(f32[10,1,256]{2,1,0:T(1,128)S(1)} %get-tuple-element.1052), channel_id=1, source_target_pairs={{1,0},{2,1},{3,2},{4,3},{5,4},{6,5},{7,6},{8,7},{9,8},{10,9},{11,1... | collective-permute-start | bytes 30728 | tf_op jit(solution)/shard_map/ppermute | solution.py:24
  273.1 7.4 %collective-permute-start.55 = (f32[10,1,256]{2,1,0:T(1,128)S(1)}, f32[10,1,256]{2,1,0:T(1,128)S(1)}, u32[]{:S(2)}, u32[]{:S(2)}) collective-permute-start(f32[10,1,256]{2,1,0:T(1,128)S(1)} %get-tuple-element.1053), channel_id=1, source_target_pairs={{0,1},{1,2},{2,3},{3,4},{4,5},{5,6},{6,7},{7,8},{8,9},{9,10},{10,1... | collective-permute-start | bytes 30728 | tf_op jit(solution)/shard_map/ppermute | solution.py:22
  (29 other events, 333.3 us)
where the time goes:
time: 283 us; the launch traced here: 281 us
  starting transfers between devices  193 us (68%)
  waiting for transfers between devices  47.1 us (17%)
  local copies, waits for them, and re-layouts  24.3 us (9%)
  other arithmetic  13.5 us (5%)
    ppermute x28, starting transfers between devices, padded_2(): lax.ppermute(tail, axis, [(i, (i + 1) % count) for i in range(ends)])  133 us
    ppermute x28, starting transfers between devices, padded_2(): lax.ppermute(head, axis, [((i + 1) % count, i) for i in range(ends)])  60 us
    ppermute x28, waiting for transfers between devices, padded_2(): lax.ppermute(tail, axis, [(i, (i + 1) % count) for i in range(ends)])  39 us
    ppermute x28, waiting for transfers between devices, padded_2(): lax.ppermute(head, axis, [((i + 1) % count, i) for i in range(ends)])  8.08 us
    broadcast_in_dim x64, local copies, waits for them, and re-layouts, line_solve(): lax.linalg.tridiagonal_solve(lower_band, diagonal, upper_band, source[......  6.38 us
    reshape x2, local copies, waits for them, and re-layouts, restrict(): return values.reshape(a // 2, 2, b // 2, 2, c // 2, 2).sum(axis=(1, 3, 5))  5.98 us
  transfers between devices with their start and end apart: 56, of which 25 were waited for; matrix products, arithmetic and copies ran while one was open for 3% of the time, Pallas kernels for 0%

commit v1 on v0

v1 whole, which is shorter than its diff:
```python
import functools

import jax
import jax.numpy as jnp
from jax import lax
from jax.experimental import pallas as pl
from jax.experimental.pallas import tpu as pltpu
from jax.sharding import PartitionSpec as P

KC = 6
GROUP = 8
DAMPING = 2.0 / 3.0

MESH = pl.DeviceIdType.MESH

O = 4
ROWS = 16
NEIGHBOURS = ((1, 0), (-1, 0), (1, 1), (1, -1), (-1, 1), (-1, -1), (0, 1), (0, -1))


def reciprocal(values):
    guess = pl.reciprocal(values, approx=True)
    return guess * (2.0 - values * guess)


def harmonic(left, right):
    return 2.0 * left * right * reciprocal(left + right)


def next_of(values, axis):
    return pltpu.roll(values, values.shape[axis] - 1, axis)


def prev_of(values, axis):
    return pltpu.roll(values, 1, axis)


def swapped(values):
    return jnp.concatenate([values[1:2], values[0:1]], axis=0)


def next_z(values):
    moved = next_of(values, values.ndim - 1)
    if values.ndim == 2:
        return moved
    lane = lax.broadcasted_iota(jnp.int32, values.shape, 2)
    return jnp.where(lane == 127, swapped(moved), moved)


def prev_z(values):
    moved = prev_of(values, values.ndim - 1)
    if values.ndim == 2:
        return moved
    lane = lax.broadcasted_iota(jnp.int32, values.shape, 2)
    return jnp.where(lane == 0, swapped(moved), moved)


def next_y(values):
    return next_of(values, values.ndim - 2)


def prev_y(values):
    return prev_of(values, values.ndim - 2)


def one_hot(shape, test):
    row = lax.broadcasted_iota(jnp.int32, shape, 0)
    column = lax.broadcasted_iota(jnp.int32, shape, 1)
    return jnp.where(test(row, column), 1.0, 0.0).astype(jnp.bfloat16)


def thirds(values):
    head = values.astype(jnp.bfloat16)
    rest = values - head.astype(jnp.float32)
    middle = rest.astype(jnp.bfloat16)
    tail = (rest - middle.astype(jnp.float32)).astype(jnp.bfloat16)
    return [head, middle, tail]


def times_one_hot(values, matrix):
    rows = values.shape[0]
    product = jnp.dot(jnp.concatenate(thirds(values), axis=0), matrix, preferred_element_type=jnp.float32)
    return product[:rows] + product[rows : 2 * rows] + product[2 * rows :]


def source_span(step, n, width):
    return (n - width, n) if step > 0 else (0, width) if step < 0 else (0, n)


def target_span(step, n, width):
    return (O - width, O) if step > 0 else (O + n, O + n + width) if step < 0 else (O, O + n)


def face_weights(level, field, own, rows, keep_x, keep_y, keep_z):
    wx, wyu, wyd, wzu, wzd, diag, damp = level
    first, last = rows

    def along_x(x, _):
        wx[x] = harmonic(field[0, x], field[0, x + 1])
        return 0

    lax.fori_loop(first - 1, last, along_x, 0, unroll=True)
    wx[O - 1] = wx[O - 1] * keep_x[0]
    wx[O + own - 1] = wx[O + own - 1] * keep_x[1]

    def rest(x, _):
        second = field[1, x]
        third = field[2, x]
        up_y = harmonic(second, next_y(second)) * keep_y
        up_z = harmonic(third, next_z(third)) * keep_z
        down_y = prev_y(up_y)
        down_z = prev_z(up_z)
        wyu[x] = up_y
        wyd[x] = down_y
        wzu[x] = up_z
        wzd[x] = down_z
        total = field[3, x] + (wx[x] + wx[x - 1]) + (up_y + down_y) + (up_z + down_z)
        diag[x] = total
        damp[x] = DAMPING * reciprocal(total)
        return 0

    lax.fori_loop(first, last, rest, 0, unroll=True)


def row_residual(level, source, field, x):
    wx, wyu, wyd, wzu, wzd, diag, damp = level
    v = field[x]
    left = source[x] - diag[x] * v
    left = left + (wx[x] * field[x + 1] + wx[x - 1] * field[x - 1])
    left = left + (wyu[x] * next_y(v) + wyd[x] * prev_y(v))
    left = left + (wzu[x] * next_z(v) + wzd[x] * prev_z(v))
    return left


def sweep(level, source, field, result, rows):
    damp = level[6]

    def body(x, _):
        result[x] = field[x] + damp[x] * row_residual(level, source, field, x)
        return 0

    lax.fori_loop(rows[0], rows[1], body, 0, unroll=True)


def start_sweep(level, source, result, rows):
    damp = level[6]

    def body(x, _):
        result[x] = damp[x] * source[x]
        return 0

    lax.fori_loop(rows[0], rows[1], body, 0, unroll=True)


def kernel(
    count_x,
    count_y,
    rhs_h,
    store_f_h,
    mob_f_h,
    store_m_h,
    mob_m_h,
    store_c_h,
    mob_c_h,
    pressure_h,
    residual_h,
    f_in,
    f_wx,
    f_wyu,
    f_wyd,
    f_wzu,
    f_wzd,
    f_diag,
    f_damp,
    f_a,
    f_b,
    f_x,
    m_in,
    m_src,
    m_wx,
    m_wyu,
    m_wyd,
    m_wzu,
    m_wzd,
    m_diag,
    m_damp,
    m_a,
    m_b,
    m_y,
    m_fold,
    f_spread,
    c_coef,
    c_src,
    c_ext,
    c_spread,
    c_weights,
    c_alpha,
    c_gamma,
    local_sem,
    send_sem,
    recv_sem,
):
    gx = lax.axis_index("gx")
    gy = lax.axis_index("gy")
    place = lax.rem(gy + (2 * GROUP - 2), GROUP)
    leader = gy - place + count_y

    def beside(sx, sy):
        return {
            "gx": lax.rem(gx + (sx + count_x), count_x),
            "gy": lax.rem(gy + (sy + count_y), count_y),
        }

    def member(d):
        return {"gx": gx, "gy": lax.rem(leader + lax.rem(place + d, GROUP), count_y)}

    c_coef[...] = jnp.ones_like(c_coef)
    c_src[...] = jnp.zeros_like(c_src)

    barrier = pltpu.get_barrier_semaphore()
    for sx, sy in NEIGHBOURS:
        pl.semaphore_signal(barrier, inc=1, device_id=beside(sx, sy), device_id_type=MESH)
    for d in range(1, GROUP):
        pl.semaphore_signal(barrier, inc=1, device_id=member(d), device_id_type=MESH)

    locals_ = []

    def bring(source, target):
        copy = pltpu.make_async_copy(source, target, local_sem.at[len(locals_)])
        copy.start()
        locals_.append(copy)
        return copy

    sends = []

    def push(source, target, device):
        at = len(sends)
        copy = pltpu.make_async_remote_copy(
            src_ref=source,
            dst_ref=target,
            send_sem=send_sem.at[at],
            recv_sem=recv_sem.at[at],
            device_id=device,
            device_id_type=MESH,
        )
        copy.start()
        sends.append(copy)
        return copy

    own8 = slice(O, O + 8)
    own4 = slice(O, O + 4)
    fine_in = []
    for half in range(2):
        z = slice(128 * half, 128 * half + 128)
        fine_in.append(bring(mob_f_h.at[:, :, :, z], f_in.at[0:3, own8, half, own8, :]))
        fine_in.append(bring(store_f_h.at[:, :, z], f_in.at[3, own8, half, own8, :]))
        fine_in.append(bring(rhs_h.at[:, :, z], f_in.at[4, own8, half, own8, :]))
    coarse_in = []
    for iy in range(2):
        coarse_in.append(bring(store_c_h.at[:, iy, :], c_coef.at[0, iy, 0:2, :]))
        coarse_in.append(bring(mob_c_h.at[:, :, iy, :], c_coef.at[1:4, iy, 0:2, :]))
    mid_in = [
        bring(mob_m_h, m_in.at[0:3, own4, own4, :]),
        bring(store_m_h, m_in.at[3, own4, own4, :]),
    ]
    f_src = f_in.at[4]

    def spans(sx, sy, n, wide_x, wide_y):
        ax, ay = source_span(sx, n, wide_x), source_span(sy, n, wide_y)
        return (
            slice(ax[0] + O, ax[1] + O),
            slice(ay[0] + O, ay[1] + O),
            slice(*target_span(sx, n, wide_x)),
            slice(*target_span(sy, n, wide_y)),
        )

    faces_x = [step for step in NEIGHBOURS if step[1] == 0]
    faces_y = [step for step in NEIGHBOURS if step[0] == 0]
    corners = [step for step in NEIGHBOURS if step[0] != 0 and step[1] != 0]

    for copy in fine_in:
        copy.wait()
    pl.semaphore_wait(barrier, len(NEIGHBOURS) + GROUP - 1)

    fine_halo = []

    def push_fine(fields, step, wide):
        ax, ay, bx, by = spans(*step, 8, wide, wide)
        fine_halo.append(push(f_in.at[fields, ax, :, ay, :], f_in.at[fields, bx, :, by, :], beside(*step)))

    for step in faces_x:
        push_fine(slice(0, 1), step, 3)
        push_fine(slice(1, 5), step, 2)
    for step in corners:
        push_fine(slice(0, 5), step, 2)
    for copy in coarse_in:
        copy.wait()
    coarse_halo = [
        push(c_coef.at[:, 0:2, 0:2, :], c_coef.at[:, 2 * d : 2 * d + 2, 0:2, :], member(GROUP - d))
        for d in range(1, GROUP)
    ]
    for step in faces_y:
        push_fine(slice(0, 5), step, 3)

    for copy in mid_in:
        copy.wait()
    mid_halo = []
    for step in NEIGHBOURS:
        wide = 3 if step in corners else 4
        ax, ay, bx, by = spans(*step, 4, wide, wide)
        mid_halo.append(push(m_in.at[:, ax, ay, :], m_in.at[:, bx, by, :], beside(*step)))

    one = jnp.float32(1.0)
    nil = jnp.float32(0.0)
    keep_x = (jnp.where(gx == 0, nil, one), jnp.where(gx == count_x - 1, nil, one))

    def keep_yz(own, shape):
        row = lax.broadcasted_iota(jnp.int32, shape, len(shape) - 2)
        column = lax.broadcasted_iota(jnp.int32, shape, len(shape) - 1)
        if len(shape) == 3:
            column = column + 128 * lax.broadcasted_iota(jnp.int32, shape, 0)
        columns = 128 * (len(shape) - 1)
        end = jnp.where(gy == 0, O - 1, -1)
        other = jnp.where(gy == count_y - 1, O + own - 1, -1)
        keep_y = jnp.where((row == end) | (row == other), 0.0, 1.0)
        keep_z = jnp.where(column == columns - 1, 0.0, 1.0)
        return keep_y, keep_z

    half_f = one_hot((256, 128), lambda row, column: row // 2 == column)
    half_m = one_hot((64, 128), lambda row, column: row == column // 2)

    for copy in coarse_halo:
        copy.wait_recv()
    coef = [c_coef[k].reshape(128, 64).T for k in range(4)]
    column = lax.broadcasted_iota(jnp.int32, (64, 128), 1)
    level_row = lax.broadcasted_iota(jnp.int32, (64, 128), 0)
    cell_y = column // 8
    holder = lax.rem(place + cell_y // 2, GROUP)
    last_cell = (holder == GROUP - 1) | (lax.rem(leader + holder, count_y) == count_y - 1)
    shut = last_cell & (lax.rem(cell_y, 2) == 1)
    up_x = jnp.where(lax.rem(column, 8) == 0, harmonic(coef[1], next_of(coef[1], 1)), 0.0)
    down_x = prev_of(up_x, 1)
    up_y = jnp.where(shut, 0.0, harmonic(coef[2], pltpu.roll(coef[2], 120, 1)))
    down_y = pltpu.roll(up_y, 8, 1)
    up_z = jnp.where(level_row == 63, 0.0, harmonic(coef[3], next_of(coef[3], 0)))
    down_z = prev_of(up_z, 0)
    c_weights[0] = up_x
    c_weights[1] = down_x
    c_weights[2] = up_y
    c_weights[3] = down_y
    main = coef[0] + (up_x + down_x) + (up_y + down_y) + (up_z + down_z)
    low, high = -down_z, -up_z
    for step in range(6):
        far = 1 << step
        inverse = reciprocal(main)
        alpha = -low * pltpu.roll(inverse, far, 0)
        gamma = -high * pltpu.roll(inverse, 64 - far, 0)
        c_alpha[step] = alpha
        c_gamma[step] = gamma
        main = main + alpha * pltpu.roll(high, far, 0) + gamma * pltpu.roll(low, 64 - far, 0)
        low, high = alpha * pltpu.roll(low, far, 0), gamma * pltpu.roll(high, 64 - far, 0)
    c_weights[4] = reciprocal(main)

    def lines(values):
        for step in range(6):
            far = 1 << step
            lower = pltpu.roll(values, far, 0)
            upper = pltpu.roll(values, 64 - far, 0)
            values = values + c_alpha[step] * lower + c_gamma[step] * upper
        return values * c_weights[4]

    fine = (f_wx, f_wyu, f_wyd, f_wzu, f_wzd, f_diag, f_damp)
    for copy in fine_halo:
        copy.wait_recv()
    keep_y, keep_z = keep_yz(8, (2, ROWS, 128))
    face_weights(fine, f_in, 8, (O - 2, O + 10), keep_x, keep_y, keep_z)
    start_sweep(fine, f_src, f_a, (O - 2, O + 10))
    sweep(fine, f_src, f_a, f_b, (O - 1, O + 9))

    def folded(x, _):
        first = row_residual(fine, f_src, f_b, O + 2 * x)
        f_spread[x] = first + row_residual(fine, f_src, f_b, O + 2 * x + 1)
        return 0

    lax.fori_loop(0, 4, folded, 0, unroll=True)
    halves = [f_spread[0:4, half].reshape(4 * ROWS, 128) for half in range(2)]
    m_fold[0:4] = times_one_hot(jnp.concatenate(halves, axis=1), half_f).reshape(4, ROWS, 128)

    def pairs(x, _):
        even = m_fold[x, pl.ds(O, 4, stride=2), :]
        m_src[O + x, O : O + 4, :] = even + m_fold[x, pl.ds(O + 1, 4, stride=2), :]
        return 0

    lax.fori_loop(0, 4, pairs, 0, unroll=True)

    mid_source = []
    for sx, sy in NEIGHBOURS:
        wide = 2 if sx != 0 and sy != 0 else 3
        ax, ay, bx, by = spans(sx, sy, 4, wide, wide)
        mid_source.append(push(m_src.at[ax, ay, :], m_src.at[bx, by, :], beside(sx, sy)))

    def keep_fine(x, _):
        f_x[x, :, O : O + 8, :] = f_b[x, :, O : O + 8, :]
        return 0

    lax.fori_loop(O, O + 8, keep_fine, 0, unroll=True)
    fine_iterate = []
    for sx, sy in NEIGHBOURS:
        wide = 2 if sx != 0 and sy != 0 else 3
        ax, ay, bx, by = spans(sx, sy, 8, wide, wide)
        fine_iterate.append(push(f_x.at[ax, :, ay, :], f_x.at[bx, :, by, :], beside(sx, sy)))

    for copy in fine_halo + coarse_halo + mid_halo:
        copy.wait_send()

    mid = (m_wx, m_wyu, m_wyd, m_wzu, m_wzd, m_diag, m_damp)
    for copy in mid_halo:
        copy.wait_recv()
    keep_y, keep_z = keep_yz(4, (ROWS, 128))
    face_weights(mid, m_in, 4, (O - 3, O + 7), keep_x, keep_y, keep_z)
    for copy in mid_source:
        copy.wait_recv()
    start_sweep(mid, m_src, m_a, (O - 2, O + 6))
    sweep(mid, m_src, m_a, m_b, (O - 1, O + 5))
    for ix in range(2):
        fold = row_residual(mid, m_src, m_b, O + 2 * ix) + row_residual(mid, m_src, m_b, O + 2 * ix + 1)
        for iy in range(2):
            c_src[iy, ix : ix + 1, :] = fold[O + 2 * iy : O + 2 * iy + 1] + fold[O + 2 * iy + 1 : O + 2 * iy + 2]
    coarse_source = [
        push(c_src.at[0:2, 0:2, :], c_src.at[2 * d : 2 * d + 2, 0:2, :], member(GROUP - d))
        for d in range(1, GROUP)
    ]

    def keep_mid(x, _):
        m_y[x, O : O + 4, :] = m_b[x, O : O + 4, :]
        return 0

    lax.fori_loop(O, O + 4, keep_mid, 0, unroll=True)
    mid_iterate = []
    for sx, sy in NEIGHBOURS:
        wide = 3 if sx != 0 and sy != 0 else 4
        ax, ay, bx, by = spans(sx, sy, 4, wide, wide)
        mid_iterate.append(push(m_y.at[ax, ay, :], m_y.at[bx, by, :], beside(sx, sy)))

    for copy in coarse_source:
        copy.wait_recv()
    source = lax.dot_general(
        jnp.concatenate([half_m] * 3, axis=1),
        jnp.concatenate(thirds(c_src[...].reshape(128, 128)), axis=1),
        (((1,), (1,)), ((), ())),
        preferred_element_type=jnp.float32,
    )

    def turn(_, z):
        pushed = source + (c_weights[0] * next_of(z, 1) + c_weights[1] * prev_of(z, 1))
        pushed = pushed + (c_weights[2] * pltpu.roll(z, 120, 1) + c_weights[3] * pltpu.roll(z, 8, 1))
        return lines(pushed)

    z = lax.fori_loop(0, KC - 1, turn, lines(source))
    spread = times_one_hot(z.T[0:16], half_m)
    for ix in range(2):
        for iy in range(2):
            c_ext[2 + ix, 2 + iy : 3 + iy, :] = spread[8 * iy + ix : 8 * iy + ix + 1]
    coarse_iterate = []
    for sx, sy in NEIGHBOURS:
        target = c_ext.at[2 - 2 * sx : 4 - 2 * sx, 2 - 2 * sy : 4 - 2 * sy, :]
        coarse_iterate.append(push(c_ext.at[2:4, 2:4, :], target, beside(sx, sy)))

    for copy in mid_source + fine_iterate + coarse_source + mid_iterate:
        copy.wait_send()

    for copy in mid_iterate:
        copy.wait_recv()
    for copy in coarse_iterate:
        copy.wait_recv()

    def raise_mid(x, _):
        rows = c_ext[x]
        c_spread[x, pl.ds(0, 8, stride=2), :] = rows
        c_spread[x, pl.ds(1, 8, stride=2), :] = rows
        doubled = c_spread[x]
        m_a[2 * x] = m_y[2 * x] + doubled
        m_a[2 * x + 1] = m_y[2 * x + 1] + doubled
        return 0

    lax.fori_loop(0, 6, raise_mid, 0, unroll=True)
    sweep(mid, m_src, m_a, m_b, (O - 3, O + 7))
    sweep(mid, m_src, m_b, m_a, (O - 2, O + 6))

    def raise_rows(x, _):
        rows = m_a[O - 2 + x, O - 2 : O + 6, :]
        m_fold[x, pl.ds(0, 8, stride=2), :] = rows
        m_fold[x, pl.ds(1, 8, stride=2), :] = rows
        return 0

    lax.fori_loop(0, 8, raise_rows, 0, unroll=True)
    double_f = one_hot((128, 256), lambda row, column: row == column // 2)
    doubled_z = times_one_hot(m_fold[...].reshape(8 * ROWS, 128), double_f)
    for half in range(2):
        f_spread[:, half] = doubled_z[:, 128 * half : 128 * half + 128].reshape(8, ROWS, 128)
    for copy in fine_iterate:
        copy.wait_recv()

    def raise_fine(x, _):
        f_a[2 * x] = f_x[2 * x] + f_spread[x]
        f_a[2 * x + 1] = f_x[2 * x + 1] + f_spread[x]
        return 0

    lax.fori_loop(0, 8, raise_fine, 0, unroll=True)
    sweep(fine, f_src, f_a, f_b, (O - 2, O + 10))
    sweep(fine, f_src, f_b, f_a, (O - 1, O + 9))
    outs = [
        bring(f_a.at[own8, half, own8, :], pressure_h.at[:, :, 128 * half : 128 * half + 128])
        for half in range(2)
    ]

    def last(x, _):
        f_b[x] = row_residual(fine, f_src, f_a, x)
        return 0

    lax.fori_loop(O, O + 8, last, 0, unroll=True)
    for half in range(2):
        outs.append(bring(f_b.at[own8, half, own8, :], residual_h.at[:, :, 128 * half : 128 * half + 128]))
    for copy in coarse_iterate:
        copy.wait_send()
    for copy in outs:
        copy.wait()


def local(pressure_rhs, storage_fine, mobility_fine, storage_mid, mobility_mid, storage_coarse, mobility_coarse):
    count_x = lax.axis_size("gx")
    count_y = lax.axis_size("gy")
    f32 = jnp.float32
    fine = pltpu.VMEM((8 + 2 * O, 2, ROWS, 128), f32)
    mid = pltpu.VMEM((4 + 2 * O, ROWS, 128), f32)
    anywhere = pl.BlockSpec(memory_space=pl.ANY)
    out = jax.ShapeDtypeStruct(pressure_rhs.shape, f32)
    return pl.pallas_call(
        functools.partial(kernel, count_x, count_y),
        out_shape=(out, out),
        in_specs=[anywhere] * 7,
        out_specs=(anywhere, anywhere),
        scratch_shapes=[
            pltpu.VMEM((5, 8 + 2 * O, 2, ROWS, 128), f32),
            *[fine] * 10,
            pltpu.VMEM((4, 4 + 2 * O, ROWS, 128), f32),
            *[mid] * 11,
            pltpu.VMEM((8, ROWS, 128), f32),
            pltpu.VMEM((8, 2, ROWS, 128), f32),
            pltpu.VMEM((4, 16, 8, 64), f32),
            pltpu.VMEM((16, 8, 128), f32),
            pltpu.VMEM((6, 8, 128), f32),
            pltpu.VMEM((6, ROWS, 128), f32),
            pltpu.VMEM((5, 64, 128), f32),
            pltpu.VMEM((6, 64, 128), f32),
            pltpu.VMEM((6, 64, 128), f32),
            pltpu.SemaphoreType.DMA((16,)),
            pltpu.SemaphoreType.DMA((96,)),
            pltpu.SemaphoreType.DMA((96,)),
        ],
        compiler_params=pltpu.CompilerParams(
            collective_id=0, has_side_effects=True, vmem_limit_bytes=56 * 1024 * 1024
        ),
    )(pressure_rhs, storage_fine, mobility_fine, storage_mid, mobility_mid, storage_coarse, mobility_coarse)


def solution(mesh):
    placed = (
        P("gx", "gy", None),
        P("gx", "gy", None),
        P(None, "gx", "gy", None),
        P("gx", "gy", None),
        P(None, "gx", "gy", None),
        P("gx", "gy", None),
        P(None, "gx", "gy", None),
    )
    return jax.shard_map(
        local,
        mesh=mesh,
        in_specs=placed,
        out_specs=(P("gx", "gy", None), P("gx", "gy", None)),
        check_vma=False,
    )
```

time: 283 us -> 42.9 us (0.15)
  the two profiles are of different devices: /device:TPU:231 before, /device:TPU:1 now
where the time goes in v1:
time: 42.9 us; the launch traced here: 42.7 us
  Pallas kernels  39.9 us (93%)
  local copies, waits for them, and re-layouts  2.14 us (5%)
  between operations  0.65 us (2%)
    pallas_call x1, Pallas kernels, local(): pl.pallas_call(functools.partial(kernel, count_x, count_y), out_shape=(ou...  39.9 us
    unnamed x4, local copies, waits for them, and re-layouts  2.14 us

profile of v1, /device:TPU:1, one launch (start us, length us, event | category | flops | bytes accessed | tf_op | source)
XLA Modules:
  0.0 42.7 jit_solution(6835454185696219303)
XLA Ops:
  0.6 39.9 %shard_map.86 = (f32[8,8,256]{2,1,0:T(8,128)}, f32[8,8,256]{2,1,0:T(8,128)}) custom-call(f32[8,8,256]{2,1,0:T(8,128)} %rhs_h.1, f32[8,8,256]{2,1,0:T(8,128)} %store_f_h.1, f32[3,8,8,256]{3,2,1,0:T(8,128)} %mob_f_h.1, f32[4,4,128]{2,1,0:T(4,128)} %store_m_h.1, f32[3,4,4,128]{3,2,1,0:T(4,128)} %mob_m_h.1, f32[2,2,64]{2,1,0:T(2,128)} %store_c_h.1, ...), custom_call_target="tpu_custom_call" | custom-call | tf_op jit(solution)/shard_map/pallas_call | solution.py:538
  40.6 0.0 copy-start
  40.6 1.5 %copy.11 = f32[8,8,256]{2,1,0:T(8,128)} copy(f32[8,8,256]{2,1,0:T(8,128)} %get-tuple-element.4) | data formatting | bytes 131072
  42.1 0.0 copy-done
  42.1 0.6 %copy.12 = f32[8,8,256]{2,1,0:T(8,128)} copy(f32[8,8,256]{2,1,0:T(8,128)S(1)} %copy-done) | data formatting | bytes 131072
Async XLA Ops:
  40.6 1.5 %copy-start = (f32[8,8,256]{2,1,0:T(8,128)S(1)}, f32[8,8,256]{2,1,0:T(8,128)}, u32[]{:S(2)}) copy-start(f32[8,8,256]{2,1,0:T(8,128)} %get-tuple-element.5) | copy-start | bytes 196612

commit v2 on v1

v2 whole, which is shorter than its diff:
```python
import functools

import jax
import jax.numpy as jnp
from jax import lax
from jax.experimental import pallas as pl
from jax.experimental.pallas import tpu as pltpu
from jax.sharding import PartitionSpec as P

KC = 6
GROUP = 8
REACH = 4
DAMPING = 2.0 / 3.0

MESH = pl.DeviceIdType.MESH

O = 4
ROWS = 16
OWN_C = slice(15, 17)
FINE_X, FINE_Y, COEF_X, COEF_Y, MID_IN, MID_F, FINE_V, COARSE_F, MID_V = range(9)
EXCHANGES = 9
NEIGHBOURS = ((1, 0), (-1, 0), (1, 1), (1, -1), (-1, 1), (-1, -1), (0, 1), (0, -1))


def reciprocal(values):
    guess = pl.reciprocal(values, approx=True)
    return guess * (2.0 - values * guess)


def harmonic(left, right):
    return 2.0 * left * right * reciprocal(left + right)


def next_of(values, axis):
    return pltpu.roll(values, values.shape[axis] - 1, axis)


def prev_of(values, axis):
    return pltpu.roll(values, 1, axis)


def swapped(values):
    return jnp.concatenate([values[1:2], values[0:1]], axis=0)


def next_z(values):
    moved = next_of(values, values.ndim - 1)
    if values.ndim == 2:
        return moved
    lane = lax.broadcasted_iota(jnp.int32, values.shape, 2)
    return jnp.where(lane == 127, swapped(moved), moved)


def prev_z(values):
    moved = prev_of(values, values.ndim - 1)
    if values.ndim == 2:
        return moved
    lane = lax.broadcasted_iota(jnp.int32, values.shape, 2)
    return jnp.where(lane == 0, swapped(moved), moved)


def next_y(values):
    return next_of(values, values.ndim - 2)


def prev_y(values):
    return prev_of(values, values.ndim - 2)


def one_hot(shape, test):
    row = lax.broadcasted_iota(jnp.int32, shape, 0)
    column = lax.broadcasted_iota(jnp.int32, shape, 1)
    return jnp.where(test(row, column), 1.0, 0.0).astype(jnp.bfloat16)


def thirds(values):
    head = values.astype(jnp.bfloat16)
    rest = values - head.astype(jnp.float32)
    middle = rest.astype(jnp.bfloat16)
    tail = (rest - middle.astype(jnp.float32)).astype(jnp.bfloat16)
    return [head, middle, tail]


def times_one_hot(values, matrix):
    rows = values.shape[0]
    product = jnp.dot(jnp.concatenate(thirds(values), axis=0), matrix, preferred_element_type=jnp.float32)
    return product[:rows] + product[rows : 2 * rows] + product[2 * rows :]


def source_span(step, n, width):
    return (n - width, n) if step > 0 else (0, width) if step < 0 else (0, n)


def target_span(step, n, width):
    return (O - width, O) if step > 0 else (O + n, O + n + width) if step < 0 else (O, O + n)


def weights_x(level, field, rows):
    wx = level[0]

    def body(x, _):
        wx[x] = harmonic(field[0, x], field[0, x + 1])
        return 0

    lax.fori_loop(*rows, body, 0, unroll=True)


def weights_yz(level, field, rows, keep_y, keep_z):
    wx, wyu, wyd, wzu, wzd, diag, damp = level

    def body(x, _):
        second = field[1, x]
        third = field[2, x]
        up_y = harmonic(second, next_y(second)) * keep_y
        up_z = harmonic(third, next_z(third)) * keep_z
        wyu[x] = up_y
        wyd[x] = prev_y(up_y)
        wzu[x] = up_z
        wzd[x] = prev_z(up_z)
        return 0

    lax.fori_loop(*rows, body, 0, unroll=True)


def diagonals(level, field, rows):
    wx, wyu, wyd, wzu, wzd, diag, damp = level

    def body(x, _):
        total = field[3, x] + (wx[x] + wx[x - 1]) + (wyu[x] + wyd[x]) + (wzu[x] + wzd[x])
        diag[x] = total
        damp[x] = DAMPING * reciprocal(total)
        return 0

    lax.fori_loop(*rows, body, 0, unroll=True)


def row_residual(level, source, field, x):
    wx, wyu, wyd, wzu, wzd, diag, damp = level
    v = field[x]
    left = source[x] - diag[x] * v
    left = left + (wx[x] * field[x + 1] + wx[x - 1] * field[x - 1])
    left = left + (wyu[x] * next_y(v) + wyd[x] * prev_y(v))
    left = left + (wzu[x] * next_z(v) + wzd[x] * prev_z(v))
    return left


def sweep(level, source, field, result, rows):
    damp = level[6]

    def body(x, _):
        result[x] = field[x] + damp[x] * row_residual(level, source, field, x)
        return 0

    lax.fori_loop(rows[0], rows[1], body, 0, unroll=True)


def start_sweep(level, source, result, rows):
    damp = level[6]

    def body(x, _):
        result[x] = damp[x] * source[x]
        return 0

    lax.fori_loop(rows[0], rows[1], body, 0, unroll=True)


def kernel(
    count_x,
    count_y,
    rhs_h,
    store_f_h,
    mob_f_h,
    store_m_h,
    mob_m_h,
    store_c_h,
    mob_c_h,
    pressure,
    residual,
    f_in,
    f_wx,
    f_wyu,
    f_wyd,
    f_wzu,
    f_wzd,
    f_diag,
    f_damp,
    f_a,
    f_b,
    f_x,
    m_in,
    m_src,
    m_wx,
    m_wyu,
    m_wyd,
    m_wzu,
    m_wzd,
    m_diag,
    m_damp,
    m_a,
    m_b,
    m_y,
    m_fold,
    f_spread,
    c_coef,
    c_src,
    c_ext,
    c_spread,
    c_weights,
    c_alpha,
    c_gamma,
    meter,
    local_sem,
    send_sem,
    recv_sem,
):
    gx = lax.axis_index("gx")
    gy = lax.axis_index("gy")

    def beside(sx, sy):
        return {
            "gx": lax.rem(gx + (sx + count_x), count_x),
            "gy": lax.rem(gy + (sy + count_y), count_y),
        }

    c_coef[:, 6:8] = jnp.ones((4, 2, 32, 64), jnp.float32)
    c_src[6:8] = jnp.zeros((2, 32, 128), jnp.float32)

    partners = NEIGHBOURS + tuple((0, e) for e in range(-REACH, REACH + 1) if abs(e) > 1)
    barrier = pltpu.get_barrier_semaphore()
    for step in partners:
        pl.semaphore_signal(barrier, inc=1, device_id=beside(*step), device_id_type=MESH)

    locals_ = []

    def bring(source, target):
        copy = pltpu.make_async_copy(source, target, local_sem.at[len(locals_)])
        copy.start()
        locals_.append(copy)
        return copy

    def push(at, source, target, step):
        pltpu.make_async_remote_copy(
            src_ref=source,
            dst_ref=target,
            send_sem=send_sem.at[at],
            recv_sem=recv_sem.at[at],
            device_id=beside(*step),
            device_id_type=MESH,
        ).start()
        rows = 1
        for size in source.shape[:-1]:
            rows = rows * size
        rows_of[at] = rows_of.get(at, 0) + rows

    rows_of = {}

    def all_of(at):
        if at == COEF_X:
            return c_coef.at[:, 0:4, 0:2, :]
        if at == COEF_Y:
            return c_coef.at[:, 0:6, 0:16, :]
        return meter.at[0 : rows_of[at], :]

    def received(at):
        pltpu.make_async_copy(all_of(at), all_of(at), recv_sem.at[at]).wait()

    def sent(at):
        pltpu.make_async_copy(all_of(at), all_of(at), send_sem.at[at]).wait()

    own8 = slice(O, O + 8)
    own4 = slice(O, O + 4)
    fine_in = []
    for half in range(2):
        z = slice(128 * half, 128 * half + 128)
        fine_in.append(bring(mob_f_h.at[:, :, :, z], f_in.at[0:3, own8, half, own8, :]))
        fine_in.append(bring(store_f_h.at[:, :, z], f_in.at[3, own8, half, own8, :]))
        fine_in.append(bring(rhs_h.at[:, :, z], f_in.at[4, own8, half, own8, :]))
    coarse_in = [
        bring(store_c_h, c_coef.at[0, 2:4, OWN_C, :]),
        bring(mob_c_h, c_coef.at[1:4, 2:4, OWN_C, :]),
    ]
    mid_in = [
        bring(mob_m_h, m_in.at[0:3, own4, own4, :]),
        bring(store_m_h, m_in.at[3, own4, own4, :]),
    ]
    f_src = f_in.at[4]

    def spans(sx, sy, n, wide_x, wide_y):
        ax, ay = source_span(sx, n, wide_x), source_span(sy, n, wide_y)
        return (
            slice(ax[0] + O, ax[1] + O),
            slice(ay[0] + O, ay[1] + O),
            slice(*target_span(sx, n, wide_x)),
            slice(*target_span(sy, n, wide_y)),
        )

    faces_x = [step for step in NEIGHBOURS if step[1] == 0]
    faces_y = [step for step in NEIGHBOURS if step[0] == 0]
    corners = [step for step in NEIGHBOURS if step[0] != 0 and step[1] != 0]

    for copy in fine_in:
        copy.wait()
    pl.semaphore_wait(barrier, len(partners))

    def push_fine(at, fields, step, wide):
        ax, ay, bx, by = spans(*step, 8, wide, wide)
        push(at, f_in.at[fields, ax, :, ay, :], f_in.at[fields, bx, :, by, :], step)

    for step in faces_x:
        push_fine(FINE_X, slice(0, 1), step, 3)
        push_fine(FINE_X, slice(1, 5), step, 2)
    for step in corners:
        push_fine(FINE_X, slice(0, 5), step, 2)
    for step in faces_y:
        push_fine(FINE_Y, slice(0, 5), step, 3)

    for copy in coarse_in:
        copy.wait()
    for sx, sy in faces_x:
        own = c_coef.at[:, 2:4, OWN_C, :]
        push(COEF_X, own, c_coef.at[:, 2 - 2 * sx : 4 - 2 * sx, OWN_C, :], (sx, sy))

    for copy in mid_in:
        copy.wait()
    for step in NEIGHBOURS:
        wide = 3 if step in corners else 4
        ax, ay, bx, by = spans(*step, 4, wide, wide)
        push(MID_IN, m_in.at[:, ax, ay, :], m_in.at[:, bx, by, :], step)

    one = jnp.float32(1.0)
    nil = jnp.float32(0.0)
    keep_x = (jnp.where(gx == 0, nil, one), jnp.where(gx == count_x - 1, nil, one))

    def keep_yz(own, shape):
        row = lax.broadcasted_iota(jnp.int32, shape, len(shape) - 2)
        column = lax.broadcasted_iota(jnp.int32, shape, len(shape) - 1)
        if len(shape) == 3:
            column = column + 128 * lax.broadcasted_iota(jnp.int32, shape, 0)
        columns = 128 * (len(shape) - 1)
        end = jnp.where(gy == 0, O - 1, -1)
        other = jnp.where(gy == count_y - 1, O + own - 1, -1)
        keep_y = jnp.where((row == end) | (row == other), 0.0, 1.0)
        keep_z = jnp.where(column == columns - 1, 0.0, 1.0)
        return keep_y, keep_z

    half_f = one_hot((256, 128), lambda row, column: row // 2 == column)
    half_m = one_hot((64, 128), lambda row, column: row == column // 2)

    fine = (f_wx, f_wyu, f_wyd, f_wzu, f_wzd, f_diag, f_damp)
    keep_y, keep_z = keep_yz(8, (2, ROWS, 128))
    received(FINE_Y)
    weights_yz(fine, f_in, (O, O + 8), keep_y, keep_z)
    weights_x(fine, f_in, (O, O + 7))
    diagonals(fine, f_in, (O + 1, O + 7))
    start_sweep(fine, f_src, f_a, (O + 1, O + 7))
    received(COEF_X)
    for e in range(-REACH, REACH + 1):
        if e != 0:
            target = c_coef.at[:, 0:6, OWN_C.start - 2 * e : OWN_C.stop - 2 * e, :]
            push(COEF_Y, c_coef.at[:, 0:6, OWN_C, :], target, (0, e))
    received(FINE_X)
    for rows in ((O - 3, O), (O + 7, O + 10)):
        weights_x(fine, f_in, rows)
    f_wx[O - 1] = f_wx[O - 1] * keep_x[0]
    f_wx[O + 7] = f_wx[O + 7] * keep_x[1]
    for rows in ((O - 2, O), (O + 8, O + 10)):
        weights_yz(fine, f_in, rows, keep_y, keep_z)
    for rows in ((O - 2, O + 1), (O + 7, O + 10)):
        diagonals(fine, f_in, rows)
        start_sweep(fine, f_src, f_a, rows)
    sweep(fine, f_src, f_a, f_b, (O - 1, O + 9))

    def folded(x, _):
        first = row_residual(fine, f_src, f_b, O + 2 * x)
        f_spread[x] = first + row_residual(fine, f_src, f_b, O + 2 * x + 1)
        return 0

    lax.fori_loop(0, 4, folded, 0, unroll=True)
    halves = [f_spread[0:4, half].reshape(4 * ROWS, 128) for half in range(2)]
    m_fold[0:4] = times_one_hot(jnp.concatenate(halves, axis=1), half_f).reshape(4, ROWS, 128)

    def pairs(x, _):
        even = m_fold[x, pl.ds(O, 4, stride=2), :]
        m_src[O + x, O : O + 4, :] = even + m_fold[x, pl.ds(O + 1, 4, stride=2), :]
        return 0

    lax.fori_loop(0, 4, pairs, 0, unroll=True)

    for sx, sy in NEIGHBOURS:
        wide = 2 if sx != 0 and sy != 0 else 3
        ax, ay, bx, by = spans(sx, sy, 4, wide, wide)
        push(MID_F, m_src.at[ax, ay, :], m_src.at[bx, by, :], (sx, sy))

    def keep_fine(x, _):
        f_x[x, :, O : O + 8, :] = f_b[x, :, O : O + 8, :]
        return 0

    lax.fori_loop(O, O + 8, keep_fine, 0, unroll=True)
    for sx, sy in NEIGHBOURS:
        wide = 2 if sx != 0 and sy != 0 else 3
        ax, ay, bx, by = spans(sx, sy, 8, wide, wide)
        push(FINE_V, f_x.at[ax, :, ay, :], f_x.at[bx, :, by, :], (sx, sy))

    mid = (m_wx, m_wyu, m_wyd, m_wzu, m_wzd, m_diag, m_damp)
    keep_y, keep_z = keep_yz(4, (ROWS, 128))
    received(MID_IN)
    weights_x(mid, m_in, (O - 4, O + 7))
    m_wx[O - 1] = m_wx[O - 1] * keep_x[0]
    m_wx[O + 3] = m_wx[O + 3] * keep_x[1]
    weights_yz(mid, m_in, (O - 3, O + 7), keep_y, keep_z)
    diagonals(mid, m_in, (O - 3, O + 7))

    received(COEF_Y)
    coef = [c_coef[k, :, 8:24, :].reshape(128, 64).T for k in range(4)]
    second_prev = c_coef[2, :, 7:23, :].reshape(128, 64).T
    second_next = c_coef[2, :, 9:25, :].reshape(128, 64).T
    column = lax.broadcasted_iota(jnp.int32, (64, 128), 1)
    level_row = lax.broadcasted_iota(jnp.int32, (64, 128), 0)
    cells = 2 * count_y
    cell = 2 * gy + lax.rem(column, 16) + (cells - 7)
    block = 2 * GROUP
    offset = 4 + cells - (cells // block) * block
    shut_up = (lax.rem(cell + 1 - offset + 2 * block, block) == 0) | (lax.rem(cell + 1, cells) == 0)
    shut_down = (lax.rem(cell - offset + 2 * block, block) == 0) | (lax.rem(cell, cells) == 0)
    up_x = jnp.where(lax.rem(column, 32) < 16, harmonic(coef[1], pltpu.roll(coef[1], 112, 1)), 0.0)
    down_x = pltpu.roll(up_x, 16, 1)
    up_y = jnp.where(shut_up, 0.0, harmonic(coef[2], second_next))
    down_y = jnp.where(shut_down, 0.0, harmonic(second_prev, coef[2]))
    up_z = jnp.where(level_row == 63, 0.0, harmonic(coef[3], next_of(coef[3], 0)))
    down_z = prev_of(up_z, 0)
    c_weights[0] = up_x
    c_weights[1] = down_x
    c_weights[2] = up_y
    c_weights[3] = down_y
    main = coef[0] + (up_x + down_x) + (up_y + down_y) + (up_z + down_z)
    low, high = -down_z, -up_z
    for step in range(6):
        far = 1 << step
        inverse = reciprocal(main)
        alpha = -low * pltpu.roll(inverse, far, 0)
        gamma = -high * pltpu.roll(inverse, 64 - far, 0)
        c_alpha[step] = alpha
        c_gamma[step] = gamma
        main = main + alpha * pltpu.roll(high, far, 0) + gamma * pltpu.roll(low, 64 - far, 0)
        low, high = alpha * pltpu.roll(low, far, 0), gamma * pltpu.roll(high, 64 - far, 0)
    c_weights[4] = reciprocal(main)

    def lines(values):
        for step in range(6):
            far = 1 << step
            lower = pltpu.roll(values, far, 0)
            upper = pltpu.roll(values, 64 - far, 0)
            values = values + c_alpha[step] * lower + c_gamma[step] * upper
        return values * c_weights[4]

    for at in (FINE_X, FINE_Y, COEF_X, COEF_Y, MID_IN):
        sent(at)

    received(MID_F)
    start_sweep(mid, m_src, m_a, (O - 2, O + 6))
    sweep(mid, m_src, m_a, m_b, (O - 1, O + 5))
    for ix in range(2):
        fold = row_residual(mid, m_src, m_b, O + 2 * ix) + row_residual(mid, m_src, m_b, O + 2 * ix + 1)
        for iy in range(2):
            first = O + 2 * iy
            at = OWN_C.start + iy
            c_src[2 + ix, at : at + 1, :] = fold[first : first + 1] + fold[first + 1 : first + 2]
    for e in sorted(range(-REACH, REACH + 1), key=lambda e: -abs(e)):
        for g in (1, -1, 0):
            if (g, e) != (0, 0):
                target = c_src.at[2 - 2 * g : 4 - 2 * g, OWN_C.start - 2 * e : OWN_C.stop - 2 * e, :]
                push(COARSE_F, c_src.at[2:4, OWN_C, :], target, (g, e))

    def keep_mid(x, _):
        m_y[x, O : O + 4, :] = m_b[x, O : O + 4, :]
        return 0

    lax.fori_loop(O, O + 4, keep_mid, 0, unroll=True)
    for sx, sy in NEIGHBOURS:
        wide = 3 if sx != 0 and sy != 0 else 4
        ax, ay, bx, by = spans(sx, sy, 4, wide, wide)
        push(MID_V, m_y.at[ax, ay, :], m_y.at[bx, by, :], (sx, sy))
    for at in (MID_F, FINE_V):
        sent(at)

    received(COARSE_F)
    source = lax.dot_general(
        jnp.concatenate([half_m] * 3, axis=1),
        jnp.concatenate(thirds(c_src[:, 8:24, :].reshape(128, 128)), axis=1),
        (((1,), (1,)), ((), ())),
        preferred_element_type=jnp.float32,
    )

    def turn(_, z):
        pushed = source + (c_weights[0] * pltpu.roll(z, 112, 1) + c_weights[1] * pltpu.roll(z, 16, 1))
        pushed = pushed + (c_weights[2] * next_of(z, 1) + c_weights[3] * prev_of(z, 1))
        return lines(pushed)

    z = lax.fori_loop(0, KC - 1, turn, lines(source))
    c_ext[...] = times_one_hot(z.T[0:96], half_m).reshape(6, 16, 128)

    received(MID_V)

    def raise_mid(x, _):
        rows = c_ext[x, 5:13, :]
        c_spread[x, pl.ds(0, 8, stride=2), :] = rows
        c_spread[x, pl.ds(1, 8, stride=2), :] = rows
        doubled = c_spread[x]
        m_a[2 * x] = m_y[2 * x] + doubled
        m_a[2 * x + 1] = m_y[2 * x + 1] + doubled
        return 0

    lax.fori_loop(0, 6, raise_mid, 0, unroll=True)
    sweep(mid, m_src, m_a, m_b, (O - 3, O + 7))
    sweep(mid, m_src, m_b, m_a, (O - 2, O + 6))

    def raise_rows(x, _):
        rows = m_a[O - 2 + x, O - 2 : O + 6, :]
        m_fold[x, pl.ds(0, 8, stride=2), :] = rows
        m_fold[x, pl.ds(1, 8, stride=2), :] = rows
        return 0

    lax.fori_loop(0, 8, raise_rows, 0, unroll=True)
    double_f = one_hot((128, 256), lambda row, column: row == column // 2)
    doubled_z = times_one_hot(m_fold[...].reshape(8 * ROWS, 128), double_f)
    for half in range(2):
        f_spread[:, half] = doubled_z[:, 128 * half : 128 * half + 128].reshape(8, ROWS, 128)
    received(FINE_V)

    def raise_fine(x, _):
        f_a[2 * x] = f_x[2 * x] + f_spread[x]
        f_a[2 * x + 1] = f_x[2 * x + 1] + f_spread[x]
        return 0

    lax.fori_loop(0, 8, raise_fine, 0, unroll=True)
    sweep(fine, f_src, f_a, f_b, (O - 2, O + 10))
    sweep(fine, f_src, f_b, f_a, (O - 1, O + 9))

    def last(x, _):
        left = row_residual(fine, f_src, f_a, x)
        own = f_a[x]
        for half in range(2):
            columns = slice(128 * half, 128 * half + 128)
            pressure[x - O, :, columns] = own[half, O : O + 8]
            residual[x - O, :, columns] = left[half, O : O + 8]
        return 0

    lax.fori_loop(O, O + 8, last, 0, unroll=True)
    for at in (COARSE_F, MID_V):
        sent(at)


def publish(pressure, residual, pressure_h, residual_h, sem):
    copies = [
        pltpu.make_async_copy(pressure, pressure_h, sem.at[0]),
        pltpu.make_async_copy(residual, residual_h, sem.at[1]),
    ]
    for copy in copies:
        copy.start()
    for copy in copies:
        copy.wait()


def local(pressure_rhs, storage_fine, mobility_fine, storage_mid, mobility_mid, storage_coarse, mobility_coarse):
    count_x = lax.axis_size("gx")
    count_y = lax.axis_size("gy")
    f32 = jnp.float32
    fine = pltpu.VMEM((8 + 2 * O, 2, ROWS, 128), f32)
    mid = pltpu.VMEM((4 + 2 * O, ROWS, 128), f32)
    in_hbm = pl.BlockSpec(memory_space=pltpu.HBM)
    in_vmem = pl.BlockSpec(memory_space=pltpu.VMEM)
    arrays = (pressure_rhs, storage_fine, mobility_fine, storage_mid, mobility_mid, storage_coarse, mobility_coarse)
    result = pl.pallas_call(
        functools.partial(kernel, count_x, count_y),
        out_shape=(pltpu.VMEM(pressure_rhs.shape, f32),) * 2,
        in_specs=[in_hbm] * 7,
        out_specs=(in_vmem, in_vmem),
        scratch_shapes=[
            pltpu.VMEM((5, 8 + 2 * O, 2, ROWS, 128), f32),
            *[fine] * 10,
            pltpu.VMEM((4, 4 + 2 * O, ROWS, 128), f32),
            *[mid] * 11,
            pltpu.VMEM((8, ROWS, 128), f32),
            pltpu.VMEM((8, 2, ROWS, 128), f32),
            pltpu.VMEM((4, 8, 32, 64), f32),
            pltpu.VMEM((8, 32, 128), f32),
            pltpu.VMEM((6, 16, 128), f32),
            pltpu.VMEM((6, ROWS, 128), f32),
            pltpu.VMEM((5, 64, 128), f32),
            pltpu.VMEM((6, 64, 128), f32),
            pltpu.VMEM((6, 64, 128), f32),
            pltpu.VMEM((1024, 128), f32),
            pltpu.SemaphoreType.DMA((16,)),
            pltpu.SemaphoreType.DMA((EXCHANGES,)),
            pltpu.SemaphoreType.DMA((EXCHANGES,)),
        ],
        compiler_params=pltpu.CompilerParams(
            collective_id=0, has_side_effects=True, vmem_limit_bytes=32 * 1024 * 1024
        ),
    )(*[pltpu.with_memory_space_constraint(array, pltpu.HBM) for array in arrays])
    out = jax.ShapeDtypeStruct(pressure_rhs.shape, f32)
    return pl.pallas_call(
        publish,
        out_shape=(out, out),
        in_specs=[in_vmem] * 2,
        out_specs=(in_hbm, in_hbm),
        scratch_shapes=[pltpu.SemaphoreType.DMA((2,))],
        compiler_params=pltpu.CompilerParams(vmem_limit_bytes=16 * 1024 * 1024),
    )(*result)


def solution(mesh):
    placed = (
        P("gx", "gy", None),
        P("gx", "gy", None),
        P(None, "gx", "gy", None),
        P("gx", "gy", None),
        P(None, "gx", "gy", None),
        P("gx", "gy", None),
        P(None, "gx", "gy", None),
    )
    return jax.shard_map(
        local,
        mesh=mesh,
        in_specs=placed,
        out_specs=(P("gx", "gy", None), P("gx", "gy", None)),
        check_vma=False,
    )
```

time: 42.9 us -> 36.9 us (0.86)
  Pallas kernels: 39.9 us -> 36.1 us
  local copies, waits for them, and re-layouts: 2.14 us -> 0 us
    pallas_call x1 -> x2, Pallas kernels: 39.9 us -> 36.1 us  [the longest x1 35.4 us: local(): pl.pallas_call(functools.partial(kernel, count_x, count_y), out_shape=(pl...]
    unnamed x4 -> x0, local copies, waits for them, and re-layouts: 2.14 us -> none
where the time goes in v2:
time: 36.9 us; the launch traced here: 36.7 us
  Pallas kernels  36.1 us (98%)
  between operations  0.64 us (2%)
    pallas_call x1, Pallas kernels, local(): pl.pallas_call(functools.partial(kernel, count_x, count_y), out_shape=(pl...  35.4 us

profile of v2, /device:TPU:1, one launch (start us, length us, event | category | flops | bytes accessed | tf_op | source)
XLA Modules:
  0.0 36.7 jit_solution(11008810616065682031)
XLA Ops:
  0.6 35.4 %shard_map.86 = (f32[8,8,256]{2,1,0:T(8,128)S(1)}, f32[8,8,256]{2,1,0:T(8,128)S(1)}) custom-call(f32[8,8,256]{2,1,0:T(8,128)} %rhs_h.1, f32[8,8,256]{2,1,0:T(8,128)} %store_f_h.1, f32[3,8,8,256]{3,2,1,0:T(8,128)} %mob_f_h.1, f32[4,4,128]{2,1,0:T(4,128)} %store_m_h.1, f32[3,4,4,128]{3,2,1,0:T(4,128)} %mob_m_h.1, f32[2,2,64]{2,1,0:T(2,128)} %store_c_h.1, ...), custom_call_target="tpu_custom_call" | custom-call | tf_op jit(solution)/shard_map/pallas_call | solution.py:573
  36.1 0.7 %shard_map.87 = (f32[8,8,256]{2,1,0:T(8,128)}, f32[8,8,256]{2,1,0:T(8,128)}) custom-call(f32[8,8,256]{2,1,0:T(8,128)S(1)} %get-tuple-element.4.pressure, f32[8,8,256]{2,1,0:T(8,128)S(1)} %get-tuple-element.5.residual), custom_call_target="tpu_custom_call" | custom-call | tf_op jit(solution)/shard_map/pallas_call | solution.py:602

commit v3 on v2

--- a/solution.py
+++ b/solution.py
@@ -73,18 +73,22 @@
     return jnp.where(test(row, column), 1.0, 0.0).astype(jnp.bfloat16)
 
 
-def thirds(values):
+def pieces(values):
     head = values.astype(jnp.bfloat16)
-    rest = values - head.astype(jnp.float32)
-    middle = rest.astype(jnp.bfloat16)
-    tail = (rest - middle.astype(jnp.float32)).astype(jnp.bfloat16)
-    return [head, middle, tail]
+    return [head, (values - head.astype(jnp.float32)).astype(jnp.bfloat16)]
 
 
 def times_one_hot(values, matrix):
     rows = values.shape[0]
-    product = jnp.dot(jnp.concatenate(thirds(values), axis=0), matrix, preferred_element_type=jnp.float32)
-    return product[:rows] + product[rows : 2 * rows] + product[2 * rows :]
+    product = jnp.dot(jnp.concatenate(pieces(values), axis=0), matrix, preferred_element_type=jnp.float32)
+    return product[:rows] + product[rows:]
+
+
+def total(terms):
+    while len(terms) > 1:
+        pairs = [terms[i] + terms[i + 1] for i in range(0, len(terms) - 1, 2)]
+        terms = pairs + terms[len(terms) - len(terms) % 2 :]
+    return terms[0]
 
 
 def source_span(step, n, width):
@@ -206,8 +210,8 @@
     c_ext,
     c_spread,
     c_weights,
-    c_alpha,
-    c_gamma,
+    c_bands,
+    c_inverse,
     meter,
     local_sem,
     send_sem,
@@ -306,19 +310,20 @@
         ax, ay, bx, by = spans(*step, 8, wide, wide)
         push(at, f_in.at[fields, ax, :, ay, :], f_in.at[fields, bx, :, by, :], step)
 
-    for step in faces_x:
-        push_fine(FINE_X, slice(0, 1), step, 3)
-        push_fine(FINE_X, slice(1, 5), step, 2)
-    for step in corners:
-        push_fine(FINE_X, slice(0, 5), step, 2)
-    for step in faces_y:
-        push_fine(FINE_Y, slice(0, 5), step, 3)
-
     for copy in coarse_in:
         copy.wait()
     for sx, sy in faces_x:
         own = c_coef.at[:, 2:4, OWN_C, :]
         push(COEF_X, own, c_coef.at[:, 2 - 2 * sx : 4 - 2 * sx, OWN_C, :], (sx, sy))
+
+    for step in faces_x:
+        push_fine(FINE_X, slice(0, 1), step, 3)
+        push_fine(FINE_X, slice(1, 5), step, 2)
+    for step in corners:
+        push_fine(FINE_X, slice(0, 2), step, 2)
+        push_fine(FINE_X, slice(2, 5), step, 1)
+    for step in faces_y:
+        push_fine(FINE_Y, slice(0, 5), step, 3)
 
     for copy in mid_in:
         copy.wait()
@@ -344,7 +349,7 @@
         return keep_y, keep_z
 
     half_f = one_hot((256, 128), lambda row, column: row // 2 == column)
-    half_m = one_hot((64, 128), lambda row, column: row == column // 2)
+    fold_c = one_hot((64, 128), lambda row, column: row // 8 + 8 * (row % 8) == column // 2)
 
     fine = (f_wx, f_wyu, f_wyd, f_wzu, f_wzd, f_diag, f_damp)
     keep_y, keep_z = keep_yz(8, (2, ROWS, 128))
@@ -428,30 +433,9 @@
     down_y = jnp.where(shut_down, 0.0, harmonic(second_prev, coef[2]))
     up_z = jnp.where(level_row == 63, 0.0, harmonic(coef[3], next_of(coef[3], 0)))
     down_z = prev_of(up_z, 0)
-    c_weights[0] = up_x
-    c_weights[1] = down_x
-    c_weights[2] = up_y
-    c_weights[3] = down_y
     main = coef[0] + (up_x + down_x) + (up_y + down_y) + (up_z + down_z)
-    low, high = -down_z, -up_z
-    for step in range(6):
-        far = 1 << step
-        inverse = reciprocal(main)
-        alpha = -low * pltpu.roll(inverse, far, 0)
-        gamma = -high * pltpu.roll(inverse, 64 - far, 0)
-        c_alpha[step] = alpha
-        c_gamma[step] = gamma
-        main = main + alpha * pltpu.roll(high, far, 0) + gamma * pltpu.roll(low, 64 - far, 0)
-        low, high = alpha * pltpu.roll(low, far, 0), gamma * pltpu.roll(high, 64 - far, 0)
-    c_weights[4] = reciprocal(main)
-
-    def lines(values):
-        for step in range(6):
-            far = 1 << step
-            lower = pltpu.roll(values, far, 0)
-            upper = pltpu.roll(values, 64 - far, 0)
-            values = values + c_alpha[step] * lower + c_gamma[step] * upper
-        return values * c_weights[4]
+    for at, band in enumerate((up_x, down_x, up_y, down_y, -down_z, main, -up_z)):
+        c_bands[at] = band
 
     for at in (FINE_X, FINE_Y, COEF_X, COEF_Y, MID_IN):
         sent(at)
@@ -480,24 +464,105 @@
         wide = 3 if sx != 0 and sy != 0 else 4
         ax, ay, bx, by = spans(sx, sy, 4, wide, wide)
         push(MID_V, m_y.at[ax, ay, :], m_y.at[bx, by, :], (sx, sy))
+
+    def registers(at):
+        return [c_bands[at, pl.ds(place, 8, stride=8), :] for place in range(8)]
+
+    for at in range(4):
+        for place, values in enumerate(registers(at)):
+            c_weights[at, place] = values
+    low, main, high = (registers(at) for at in (4, 5, 6))
+    ahead, back = [reciprocal(main[0])], {6: reciprocal(main[6])}
+    upto, onfrom = [main[0]], {6: main[6]}
+    for i in range(1, 7):
+        upto.append(main[i] - low[i] * high[i - 1] * ahead[i - 1])
+        ahead.append(reciprocal(upto[i]))
+        j = 6 - i
+        onfrom[j] = main[j] - high[j] * low[j + 1] * back[j + 1]
+        back[j] = reciprocal(onfrom[j])
+    rise = [-high[i] * ahead[i] for i in range(7)]
+    fall = [-low[i] * back[i] for i in range(7)]
+    inverse = {}
+    for j in range(7):
+        inverse[j, j] = reciprocal(upto[j] + onfrom[j] - main[j])
+        for i in range(j - 1, -1, -1):
+            inverse[i, j] = rise[i] * inverse[i + 1, j]
+        for i in range(j + 1, 7):
+            inverse[i, j] = fall[i] * inverse[i - 1, j]
+    from_last = [inverse[i, 0] * low[0] for i in range(7)]
+    from_own = [inverse[i, 6] * high[6] for i in range(7)]
+
+    def turned(values, by):
+        return pltpu.roll(values, by % 8, 0) if by % 8 else values
+
+    face_main = main[7] - low[7] * from_own[6] - high[7] * turned(from_last[0], -1)
+    face_low = -low[7] * from_last[6]
+    face_high = -high[7] * turned(from_own[0], -1)
+    spread_by = {0: jnp.ones((8, 128), jnp.float32)}
+    for far in (1, 2, 4):
+        over = reciprocal(face_main)
+        alpha = -face_low * turned(over, far)
+        gamma = -face_high * turned(over, -far)
+        face_main = face_main + alpha * turned(face_high, far) + gamma * turned(face_low, -far)
+        face_low, face_high = alpha * turned(face_low, far), gamma * turned(face_high, -far)
+        wider = dict(spread_by)
+        for by, values in spread_by.items():
+            for step, factor in ((far, alpha), (-far, gamma)):
+                term = factor * turned(values, step)
+                key = (by + step) % 8
+                wider[key] = wider[key] + term if key in wider else term
+        spread_by = wider
+    over = reciprocal(face_main)
+    own_by = [over * spread_by[by] for by in range(8)]
+    next_by = [own_by[(by + 1) % 8] * turned(high[7], by + 1) for by in range(8)]
+    for i in range(7):
+        for j in range(7):
+            c_inverse[7 * i + j] = inverse[i, j]
+        c_inverse[49 + i] = from_last[i]
+        c_inverse[56 + i] = from_own[i]
+    for by in range(8):
+        c_inverse[64 + by] = own_by[by]
+        c_inverse[72 + by] = next_by[by]
+        c_inverse[80 + by] = turned(own_by[by - 1], 1)
+        c_inverse[88 + by] = turned(next_by[by - 1], 1)
+    c_inverse[63] = low[7]
+
+    def lines(values):
+        inner = [total([c_inverse[7 * i + j] * values[j] for j in range(7)]) for i in range(7)]
+        face = values[7] - c_inverse[63] * inner[6]
+        faces = [turned(face, by) for by in range(8)]
+        firsts = [turned(inner[0], by) for by in range(8)]
+
+        def interface(at):
+            terms = [c_inverse[at + by] * faces[by] for by in range(8)]
+            return total(terms) - total([c_inverse[at + 8 + by] * firsts[by] for by in range(8)])
+
+        here, before = interface(64), interface(80)
+        return tuple(inner[i] - (c_inverse[49 + i] * before + c_inverse[56 + i] * here) for i in range(7)) + (here,)
+
     for at in (MID_F, FINE_V):
         sent(at)
 
     received(COARSE_F)
     source = lax.dot_general(
-        jnp.concatenate([half_m] * 3, axis=1),
-        jnp.concatenate(thirds(c_src[:, 8:24, :].reshape(128, 128)), axis=1),
+        jnp.concatenate([fold_c] * 2, axis=1),
+        jnp.concatenate(pieces(c_src[:, 8:24, :].reshape(128, 128)), axis=1),
         (((1,), (1,)), ((), ())),
         preferred_element_type=jnp.float32,
     )
+    sources = [source[8 * place : 8 * place + 8] for place in range(8)]
 
     def turn(_, z):
-        pushed = source + (c_weights[0] * pltpu.roll(z, 112, 1) + c_weights[1] * pltpu.roll(z, 16, 1))
-        pushed = pushed + (c_weights[2] * next_of(z, 1) + c_weights[3] * prev_of(z, 1))
+        pushed = []
+        for place in range(8):
+            own = z[place]
+            along_x = c_weights[0, place] * pltpu.roll(own, 112, 1) + c_weights[1, place] * pltpu.roll(own, 16, 1)
+            along_y = c_weights[2, place] * next_of(own, 1) + c_weights[3, place] * prev_of(own, 1)
+            pushed.append(sources[place] + (along_x + along_y))
         return lines(pushed)
 
-    z = lax.fori_loop(0, KC - 1, turn, lines(source))
-    c_ext[...] = times_one_hot(z.T[0:96], half_m).reshape(6, 16, 128)
+    z = lax.fori_loop(0, KC - 1, turn, lines(sources))
+    c_ext[...] = times_one_hot(jnp.concatenate(z, axis=0).T[0:96], fold_c).reshape(6, 16, 128)
 
     received(MID_V)
 
@@ -586,9 +651,9 @@
             pltpu.VMEM((8, 32, 128), f32),
             pltpu.VMEM((6, 16, 128), f32),
             pltpu.VMEM((6, ROWS, 128), f32),
-            pltpu.VMEM((5, 64, 128), f32),
-            pltpu.VMEM((6, 64, 128), f32),
-            pltpu.VMEM((6, 64, 128), f32),
+            pltpu.VMEM((4, 8, 8, 128), f32),
+            pltpu.VMEM((7, 64, 128), f32),
+            pltpu.VMEM((97, 8, 128), f32),
             pltpu.VMEM((1024, 128), f32),
             pltpu.SemaphoreType.DMA((16,)),
             pltpu.SemaphoreType.DMA((EXCHANGES,)),

time: 36.9 us -> 35.2 us (0.954)
  Pallas kernels: 36.1 us -> 34.4 us
    pallas_call x1, Pallas kernels: 35.4 us -> 33.8 us  [local(): pl.pallas_call(functools.partial(kernel, count_x, count_y), out_shape=(pl...]
where the time goes in v3:
time: 35.2 us; the launch traced here: 35.1 us
  Pallas kernels  34.4 us (98%)
  between operations  0.64 us (2%)
    pallas_call x1, Pallas kernels, local(): pl.pallas_call(functools.partial(kernel, count_x, count_y), out_shape=(pl...  33.8 us

profile of v3, /device:TPU:1, one launch (start us, length us, event | category | flops | bytes accessed | tf_op | source)
XLA Modules:
  0.0 35.1 jit_solution(3901285293019812577)
XLA Ops:
  0.6 33.8 %shard_map.86 = (f32[8,8,256]{2,1,0:T(8,128)S(1)}, f32[8,8,256]{2,1,0:T(8,128)S(1)}) custom-call(f32[8,8,256]{2,1,0:T(8,128)} %rhs_h.1, f32[8,8,256]{2,1,0:T(8,128)} %store_f_h.1, f32[3,8,8,256]{3,2,1,0:T(8,128)} %mob_f_h.1, f32[4,4,128]{2,1,0:T(4,128)} %store_m_h.1, f32[3,4,4,128]{3,2,1,0:T(4,128)} %mob_m_h.1, f32[2,2,64]{2,1,0:T(2,128)} %store_c_h.1, ...), custom_call_target="tpu_custom_call" | custom-call | tf_op jit(solution)/shard_map/pallas_call | solution.py:638
  34.4 0.7 %shard_map.87 = (f32[8,8,256]{2,1,0:T(8,128)}, f32[8,8,256]{2,1,0:T(8,128)}) custom-call(f32[8,8,256]{2,1,0:T(8,128)S(1)} %get-tuple-element.4.pressure, f32[8,8,256]{2,1,0:T(8,128)S(1)} %get-tuple-element.5.residual), custom_call_target="tpu_custom_call" | custom-call | tf_op jit(solution)/shard_map/pallas_call | solution.py:667

commit v4 on v3

--- a/solution.py
+++ b/solution.py
@@ -106,7 +106,7 @@
         wx[x] = harmonic(field[0, x], field[0, x + 1])
         return 0
 
-    lax.fori_loop(*rows, body, 0, unroll=True)
+    lax.fori_loop(*rows, body, 0)
 
 
 def weights_yz(level, field, rows, keep_y, keep_z):
@@ -123,7 +123,7 @@
         wzd[x] = prev_z(up_z)
         return 0
 
-    lax.fori_loop(*rows, body, 0, unroll=True)
+    lax.fori_loop(*rows, body, 0)
 
 
 def diagonals(level, field, rows):
@@ -135,7 +135,7 @@
         damp[x] = DAMPING * reciprocal(total)
         return 0
 
-    lax.fori_loop(*rows, body, 0, unroll=True)
+    lax.fori_loop(*rows, body, 0)
 
 
 def row_residual(level, source, field, x):
@@ -155,7 +155,7 @@
         result[x] = field[x] + damp[x] * row_residual(level, source, field, x)
         return 0
 
-    lax.fori_loop(rows[0], rows[1], body, 0, unroll=True)
+    lax.fori_loop(rows[0], rows[1], body, 0)
 
 
 def start_sweep(level, source, result, rows):
@@ -165,7 +165,7 @@
         result[x] = damp[x] * source[x]
         return 0
 
-    lax.fori_loop(rows[0], rows[1], body, 0, unroll=True)
+    lax.fori_loop(rows[0], rows[1], body, 0)
 
 
 def kernel(
@@ -220,19 +220,25 @@
     gx = lax.axis_index("gx")
     gy = lax.axis_index("gy")
 
+    def stepped(at, step, count):
+        to = at + step
+        if step > 0:
+            return jnp.where(to >= count, to - count, to)
+        return jnp.where(to < 0, to + count, to) if step < 0 else at
+
+    along_gx = {step: stepped(gx, step, count_x) for step in (-1, 0, 1)}
+    along_gy = {step: stepped(gy, step, count_y) for step in range(-REACH, REACH + 1)}
+
     def beside(sx, sy):
-        return {
-            "gx": lax.rem(gx + (sx + count_x), count_x),
-            "gy": lax.rem(gy + (sy + count_y), count_y),
-        }
-
-    c_coef[:, 6:8] = jnp.ones((4, 2, 32, 64), jnp.float32)
-    c_src[6:8] = jnp.zeros((2, 32, 128), jnp.float32)
+        return {"gx": along_gx[sx], "gy": along_gy[sy]}
 
     partners = NEIGHBOURS + tuple((0, e) for e in range(-REACH, REACH + 1) if abs(e) > 1)
     barrier = pltpu.get_barrier_semaphore()
     for step in partners:
         pl.semaphore_signal(barrier, inc=1, device_id=beside(*step), device_id_type=MESH)
+
+    c_coef[:, 6:8] = jnp.ones((4, 2, 32, 64), jnp.float32)
+    c_src[6:8] = jnp.zeros((2, 32, 128), jnp.float32)
 
     locals_ = []
 
@@ -380,7 +386,7 @@
         f_spread[x] = first + row_residual(fine, f_src, f_b, O + 2 * x + 1)
         return 0
 
-    lax.fori_loop(0, 4, folded, 0, unroll=True)
+    lax.fori_loop(0, 4, folded, 0)
     halves = [f_spread[0:4, half].reshape(4 * ROWS, 128) for half in range(2)]
     m_fold[0:4] = times_one_hot(jnp.concatenate(halves, axis=1), half_f).reshape(4, ROWS, 128)
 
@@ -389,7 +395,7 @@
         m_src[O + x, O : O + 4, :] = even + m_fold[x, pl.ds(O + 1, 4, stride=2), :]
         return 0
 
-    lax.fori_loop(0, 4, pairs, 0, unroll=True)
+    lax.fori_loop(0, 4, pairs, 0)
 
     for sx, sy in NEIGHBOURS:
         wide = 2 if sx != 0 and sy != 0 else 3
@@ -400,7 +406,7 @@
         f_x[x, :, O : O + 8, :] = f_b[x, :, O : O + 8, :]
         return 0
 
-    lax.fori_loop(O, O + 8, keep_fine, 0, unroll=True)
+    lax.fori_loop(O, O + 8, keep_fine, 0)
     for sx, sy in NEIGHBOURS:
         wide = 2 if sx != 0 and sy != 0 else 3
         ax, ay, bx, by = spans(sx, sy, 8, wide, wide)
@@ -459,7 +465,7 @@
         m_y[x, O : O + 4, :] = m_b[x, O : O + 4, :]
         return 0
 
-    lax.fori_loop(O, O + 4, keep_mid, 0, unroll=True)
+    lax.fori_loop(O, O + 4, keep_mid, 0)
     for sx, sy in NEIGHBOURS:
         wide = 3 if sx != 0 and sy != 0 else 4
         ax, ay, bx, by = spans(sx, sy, 4, wide, wide)
@@ -561,7 +567,7 @@
             pushed.append(sources[place] + (along_x + along_y))
         return lines(pushed)
 
-    z = lax.fori_loop(0, KC - 1, turn, lines(sources))
+    z = lax.fori_loop(0, KC, turn, tuple(jnp.zeros((8, 128), jnp.float32) for _ in range(8)))
     c_ext[...] = times_one_hot(jnp.concatenate(z, axis=0).T[0:96], fold_c).reshape(6, 16, 128)
 
     received(MID_V)
@@ -575,7 +581,7 @@
         m_a[2 * x + 1] = m_y[2 * x + 1] + doubled
         return 0
 
-    lax.fori_loop(0, 6, raise_mid, 0, unroll=True)
+    lax.fori_loop(0, 6, raise_mid, 0)
     sweep(mid, m_src, m_a, m_b, (O - 3, O + 7))
     sweep(mid, m_src, m_b, m_a, (O - 2, O + 6))
 
@@ -585,7 +591,7 @@
         m_fold[x, pl.ds(1, 8, stride=2), :] = rows
         return 0
 
-    lax.fori_loop(0, 8, raise_rows, 0, unroll=True)
+    lax.fori_loop(0, 8, raise_rows, 0)
     double_f = one_hot((128, 256), lambda row, column: row == column // 2)
     doubled_z = times_one_hot(m_fold[...].reshape(8 * ROWS, 128), double_f)
     for half in range(2):
@@ -597,7 +603,7 @@
         f_a[2 * x + 1] = f_x[2 * x + 1] + f_spread[x]
         return 0
 
-    lax.fori_loop(0, 8, raise_fine, 0, unroll=True)
+    lax.fori_loop(0, 8, raise_fine, 0)
     sweep(fine, f_src, f_a, f_b, (O - 2, O + 10))
     sweep(fine, f_src, f_b, f_a, (O - 1, O + 9))
 
@@ -610,7 +616,7 @@
             residual[x - O, :, columns] = left[half, O : O + 8]
         return 0
 
-    lax.fori_loop(O, O + 8, last, 0, unroll=True)
+    lax.fori_loop(O, O + 8, last, 0)
     for at in (COARSE_F, MID_V):
         sent(at)
 

time: 35.2 us -> 41 us (1.16)
  Pallas kernels: 34.4 us -> 40.2 us
    pallas_call x1, Pallas kernels: 33.8 us -> 39.5 us  [local(): pl.pallas_call(functools.partial(kernel, count_x, count_y), out_shape=(pl...]
where the time goes in v4:
time: 41 us; the launch traced here: 40.8 us
  Pallas kernels  40.2 us (98%)
  between operations  0.64 us (2%)
    pallas_call x1, Pallas kernels, local(): pl.pallas_call(functools.partial(kernel, count_x, count_y), out_shape=(pl...  39.5 us

profile of v4, /device:TPU:1, one launch (start us, length us, event | category | flops | bytes accessed | tf_op | source)
XLA Modules:
  0.0 40.8 jit_solution(9132390518549558976)
XLA Ops:
  0.6 39.5 %shard_map.86 = (f32[8,8,256]{2,1,0:T(8,128)S(1)}, f32[8,8,256]{2,1,0:T(8,128)S(1)}) custom-call(f32[8,8,256]{2,1,0:T(8,128)} %rhs_h.1, f32[8,8,256]{2,1,0:T(8,128)} %store_f_h.1, f32[3,8,8,256]{3,2,1,0:T(8,128)} %mob_f_h.1, f32[4,4,128]{2,1,0:T(4,128)} %store_m_h.1, f32[3,4,4,128]{3,2,1,0:T(4,128)} %mob_m_h.1, f32[2,2,64]{2,1,0:T(2,128)} %store_c_h.1, ...), custom_call_target="tpu_custom_call" | custom-call | tf_op jit(solution)/shard_map/pallas_call | solution.py:644
  40.1 0.7 %shard_map.87 = (f32[8,8,256]{2,1,0:T(8,128)}, f32[8,8,256]{2,1,0:T(8,128)}) custom-call(f32[8,8,256]{2,1,0:T(8,128)S(1)} %get-tuple-element.4.pressure, f32[8,8,256]{2,1,0:T(8,128)S(1)} %get-tuple-element.5.residual), custom_call_target="tpu_custom_call" | custom-call | tf_op jit(solution)/shard_map/pallas_call | solution.py:673

commit v5 on v3

--- a/solution.py
+++ b/solution.py
@@ -15,7 +15,8 @@
 MESH = pl.DeviceIdType.MESH
 
 O = 4
-ROWS = 16
+OP = 2
+M0, M2, STORE, SOURCE, M1 = range(5)
 OWN_C = slice(15, 17)
 FINE_X, FINE_Y, COEF_X, COEF_Y, MID_IN, MID_F, FINE_V, COARSE_F, MID_V = range(9)
 EXCHANGES = 9
@@ -39,32 +40,30 @@
     return pltpu.roll(values, 1, axis)
 
 
-def swapped(values):
-    return jnp.concatenate([values[1:2], values[0:1]], axis=0)
+def next_paired(values, axis, pairs):
+    first, second = lax.slice_in_dim(values, 0, 1, axis=axis), lax.slice_in_dim(values, 1, 2, axis=axis)
+    return jnp.concatenate([second, next_of(first, pairs)], axis=axis)
+
+
+def prev_paired(values, axis, pairs):
+    first, second = lax.slice_in_dim(values, 0, 1, axis=axis), lax.slice_in_dim(values, 1, 2, axis=axis)
+    return jnp.concatenate([prev_of(second, pairs), first], axis=axis)
+
+
+def next_y(values):
+    return next_paired(values, 0, values.ndim - 2)
+
+
+def prev_y(values):
+    return prev_paired(values, 0, values.ndim - 2)
 
 
 def next_z(values):
-    moved = next_of(values, values.ndim - 1)
-    if values.ndim == 2:
-        return moved
-    lane = lax.broadcasted_iota(jnp.int32, values.shape, 2)
-    return jnp.where(lane == 127, swapped(moved), moved)
+    return next_paired(values, 1, 3) if values.ndim == 4 else next_of(values, 2)
 
 
 def prev_z(values):
-    moved = prev_of(values, values.ndim - 1)
-    if values.ndim == 2:
-        return moved
-    lane = lax.broadcasted_iota(jnp.int32, values.shape, 2)
-    return jnp.where(lane == 0, swapped(moved), moved)
-
-
-def next_y(values):
-    return next_of(values, values.ndim - 2)
-
-
-def prev_y(values):
-    return prev_of(values, values.ndim - 2)
+    return prev_paired(values, 1, 3) if values.ndim == 4 else prev_of(values, 2)
 
 
 def one_hot(shape, test):
@@ -73,15 +72,18 @@
     return jnp.where(test(row, column), 1.0, 0.0).astype(jnp.bfloat16)
 
 
-def pieces(values):
-    head = values.astype(jnp.bfloat16)
-    return [head, (values - head.astype(jnp.float32)).astype(jnp.bfloat16)]
-
-
-def times_one_hot(values, matrix):
+def pieces(values, count):
+    parts = []
+    for _ in range(count - 1):
+        parts.append(values.astype(jnp.bfloat16))
+        values = values - parts[-1].astype(jnp.float32)
+    return parts + [values.astype(jnp.bfloat16)]
+
+
+def times_one_hot(values, matrix, count):
     rows = values.shape[0]
-    product = jnp.dot(jnp.concatenate(pieces(values), axis=0), matrix, preferred_element_type=jnp.float32)
-    return product[:rows] + product[rows:]
+    product = jnp.dot(jnp.concatenate(pieces(values, count), axis=0), matrix, preferred_element_type=jnp.float32)
+    return total([product[at * rows : (at + 1) * rows] for at in range(count)])
 
 
 def total(terms):
@@ -91,30 +93,32 @@
     return terms[0]
 
 
-def source_span(step, n, width):
-    return (n - width, n) if step > 0 else (0, width) if step < 0 else (0, n)
-
-
-def target_span(step, n, width):
-    return (O - width, O) if step > 0 else (O + n, O + n + width) if step < 0 else (O, O + n)
-
-
-def weights_x(level, field, rows):
+def source_span(step, first, n, width):
+    return slice(first + n - width, first + n) if step > 0 else slice(first, first + (width if step < 0 else n))
+
+
+def target_span(step, first, n, width):
+    if step > 0:
+        return slice(first - width, first)
+    return slice(first + n, first + n + width) if step < 0 else slice(first, first + n)
+
+
+def weights_x(level, mob, rows):
     wx = level[0]
 
     def body(x, _):
-        wx[x] = harmonic(field[0, x], field[0, x + 1])
+        wx[x] = harmonic(mob[0][x], mob[0][x + 1])
         return 0
 
     lax.fori_loop(*rows, body, 0, unroll=True)
 
 
-def weights_yz(level, field, rows, keep_y, keep_z):
+def weights_yz(level, mob, rows, keep_y, keep_z):
     wx, wyu, wyd, wzu, wzd, diag, damp = level
 
     def body(x, _):
-        second = field[1, x]
-        third = field[2, x]
+        second = mob[1][x]
+        third = mob[2][x]
         up_y = harmonic(second, next_y(second)) * keep_y
         up_z = harmonic(third, next_z(third)) * keep_z
         wyu[x] = up_y
@@ -126,13 +130,13 @@
     lax.fori_loop(*rows, body, 0, unroll=True)
 
 
-def diagonals(level, field, rows):
+def diagonals(level, store, rows):
     wx, wyu, wyd, wzu, wzd, diag, damp = level
 
     def body(x, _):
-        total = field[3, x] + (wx[x] + wx[x - 1]) + (wyu[x] + wyd[x]) + (wzu[x] + wzd[x])
-        diag[x] = total
-        damp[x] = DAMPING * reciprocal(total)
+        all_of_it = store[x] + (wx[x] + wx[x - 1]) + (wyu[x] + wyd[x]) + (wzu[x] + wzd[x])
+        diag[x] = all_of_it
+        damp[x] = DAMPING * reciprocal(all_of_it)
         return 0
 
     lax.fori_loop(*rows, body, 0, unroll=True)
@@ -180,6 +184,8 @@
     mob_c_h,
     pressure,
     residual,
+    f_stage,
+    f_mixed,
     f_in,
     f_wx,
     f_wyu,
@@ -204,11 +210,10 @@
     m_b,
     m_y,
     m_fold,
-    f_spread,
+    f_rows,
     c_coef,
     c_src,
     c_ext,
-    c_spread,
     c_weights,
     c_bands,
     c_inverse,
@@ -220,19 +225,25 @@
     gx = lax.axis_index("gx")
     gy = lax.axis_index("gy")
 
+    def stepped(at, step, count):
+        to = at + step
+        if step > 0:
+            return jnp.where(to >= count, to - count, to)
+        return jnp.where(to < 0, to + count, to) if step < 0 else at
+
+    along_gx = {step: stepped(gx, step, count_x) for step in (-1, 0, 1)}
+    along_gy = {step: stepped(gy, step, count_y) for step in range(-REACH, REACH + 1)}
+
     def beside(sx, sy):
-        return {
-            "gx": lax.rem(gx + (sx + count_x), count_x),
-            "gy": lax.rem(gy + (sy + count_y), count_y),
-        }
-
-    c_coef[:, 6:8] = jnp.ones((4, 2, 32, 64), jnp.float32)
-    c_src[6:8] = jnp.zeros((2, 32, 128), jnp.float32)
+        return {"gx": along_gx[sx], "gy": along_gy[sy]}
 
     partners = NEIGHBOURS + tuple((0, e) for e in range(-REACH, REACH + 1) if abs(e) > 1)
     barrier = pltpu.get_barrier_semaphore()
     for step in partners:
         pl.semaphore_signal(barrier, inc=1, device_id=beside(*step), device_id_type=MESH)
+
+    c_coef[:, 6:8] = jnp.ones((4, 2, 32, 64), jnp.float32)
+    c_src[6:8] = jnp.zeros((2, 32, 128), jnp.float32)
 
     locals_ = []
 
@@ -271,44 +282,58 @@
     def sent(at):
         pltpu.make_async_copy(all_of(at), all_of(at), send_sem.at[at]).wait()
 
-    own8 = slice(O, O + 8)
-    own4 = slice(O, O + 4)
-    fine_in = []
-    for half in range(2):
-        z = slice(128 * half, 128 * half + 128)
-        fine_in.append(bring(mob_f_h.at[:, :, :, z], f_in.at[0:3, own8, half, own8, :]))
-        fine_in.append(bring(store_f_h.at[:, :, z], f_in.at[3, own8, half, own8, :]))
-        fine_in.append(bring(rhs_h.at[:, :, z], f_in.at[4, own8, half, own8, :]))
+    own8, pairs8 = slice(O, O + 8), slice(OP, OP + 4)
+    own4, pairs4 = slice(O, O + 4), slice(OP, OP + 2)
+    fine_in = [
+        bring(mob_f_h, f_stage.at[0:3]),
+        bring(store_f_h, f_stage.at[3]),
+        bring(rhs_h, f_stage.at[4]),
+    ]
     coarse_in = [
         bring(store_c_h, c_coef.at[0, 2:4, OWN_C, :]),
         bring(mob_c_h, c_coef.at[1:4, 2:4, OWN_C, :]),
     ]
-    mid_in = [
-        bring(mob_m_h, m_in.at[0:3, own4, own4, :]),
-        bring(store_m_h, m_in.at[3, own4, own4, :]),
-    ]
-    f_src = f_in.at[4]
+    mid_in = []
+    for y in range(4):
+        parity, pair = y % 2, OP + y // 2
+        mid_in.append(bring(mob_m_h.at[:, :, y, :], m_in.at[0:3, own4, parity, pair, :]))
+        mid_in.append(bring(store_m_h.at[:, y, :], m_in.at[3, own4, parity, pair, :]))
+    f_src = f_in.at[SOURCE]
 
     def spans(sx, sy, n, wide_x, wide_y):
-        ax, ay = source_span(sx, n, wide_x), source_span(sy, n, wide_y)
         return (
-            slice(ax[0] + O, ax[1] + O),
-            slice(ay[0] + O, ay[1] + O),
-            slice(*target_span(sx, n, wide_x)),
-            slice(*target_span(sy, n, wide_y)),
+            source_span(sx, O, n, wide_x),
+            source_span(sy, OP, n // 2, wide_y),
+            target_span(sx, O, n, wide_x),
+            target_span(sy, OP, n // 2, wide_y),
         )
 
     faces_x = [step for step in NEIGHBOURS if step[1] == 0]
     faces_y = [step for step in NEIGHBOURS if step[0] == 0]
     corners = [step for step in NEIGHBOURS if step[0] != 0 and step[1] != 0]
 
+    apart = one_hot((256, 256), lambda row, column: row == 2 * (column % 128) + column // 128)
     for copy in fine_in:
         copy.wait()
+    sorted_z = times_one_hot(f_stage[...].reshape(320, 256), apart, 3)
+    for half in range(2):
+        f_mixed[half] = sorted_z[:, 128 * half : 128 * half + 128].reshape(40, 8, 128)
+
+    def sort_y(x, _):
+        for at, to in enumerate((M0, M1, M2, STORE, SOURCE)):
+            for parity in range(2):
+                for half in range(2):
+                    rows = f_mixed[half, 8 * at + x, pl.ds(parity, 4, stride=2), :]
+                    f_in[to, O + x, parity, half, pairs8] = rows
+        return 0
+
+    lax.fori_loop(0, 8, sort_y, 0, unroll=True)
     pl.semaphore_wait(barrier, len(partners))
 
-    def push_fine(at, fields, step, wide):
-        ax, ay, bx, by = spans(*step, 8, wide, wide)
-        push(at, f_in.at[fields, ax, :, ay, :], f_in.at[fields, bx, :, by, :], step)
+    def push_fine(at, first, last, step, wide_x, wide_y):
+        fields = slice(first, last + 1)
+        ax, ay, bx, by = spans(*step, 8, wide_x, wide_y)
+        push(at, f_in.at[fields, ax, :, :, ay, :], f_in.at[fields, bx, :, :, by, :], step)
 
     for copy in coarse_in:
         copy.wait()
@@ -317,46 +342,47 @@
         push(COEF_X, own, c_coef.at[:, 2 - 2 * sx : 4 - 2 * sx, OWN_C, :], (sx, sy))
 
     for step in faces_x:
-        push_fine(FINE_X, slice(0, 1), step, 3)
-        push_fine(FINE_X, slice(1, 5), step, 2)
+        push_fine(FINE_X, M0, M0, step, 3, 1)
+        push_fine(FINE_X, M2, M1, step, 2, 1)
     for step in corners:
-        push_fine(FINE_X, slice(0, 2), step, 2)
-        push_fine(FINE_X, slice(2, 5), step, 1)
+        push_fine(FINE_X, M0, M0, step, 2, 1)
+        push_fine(FINE_X, M1, M1, step, 2, 1)
+        push_fine(FINE_X, M2, SOURCE, step, 1, 1)
     for step in faces_y:
-        push_fine(FINE_Y, slice(0, 5), step, 3)
+        push_fine(FINE_Y, M0, SOURCE, step, 1, 1)
+        push_fine(FINE_Y, M1, M1, step, 1, 2)
 
     for copy in mid_in:
         copy.wait()
     for step in NEIGHBOURS:
-        wide = 3 if step in corners else 4
-        ax, ay, bx, by = spans(*step, 4, wide, wide)
-        push(MID_IN, m_in.at[:, ax, ay, :], m_in.at[:, bx, by, :], step)
+        ax, ay, bx, by = spans(*step, 4, 3 if step in corners else 4, 2)
+        push(MID_IN, m_in.at[:, ax, :, ay, :], m_in.at[:, bx, :, by, :], step)
 
     one = jnp.float32(1.0)
     nil = jnp.float32(0.0)
     keep_x = (jnp.where(gx == 0, nil, one), jnp.where(gx == count_x - 1, nil, one))
 
     def keep_yz(own, shape):
-        row = lax.broadcasted_iota(jnp.int32, shape, len(shape) - 2)
-        column = lax.broadcasted_iota(jnp.int32, shape, len(shape) - 1)
-        if len(shape) == 3:
-            column = column + 128 * lax.broadcasted_iota(jnp.int32, shape, 0)
-        columns = 128 * (len(shape) - 1)
-        end = jnp.where(gy == 0, O - 1, -1)
-        other = jnp.where(gy == count_y - 1, O + own - 1, -1)
-        keep_y = jnp.where((row == end) | (row == other), 0.0, 1.0)
-        keep_z = jnp.where(column == columns - 1, 0.0, 1.0)
-        return keep_y, keep_z
-
-    half_f = one_hot((256, 128), lambda row, column: row // 2 == column)
+        def index(axis):
+            return lax.broadcasted_iota(jnp.int32, shape, axis)
+
+        parity, pair, lane = index(0), index(len(shape) - 2), index(len(shape) - 1)
+        end = jnp.where(gy == 0, OP - 1, -1)
+        other = jnp.where(gy == count_y - 1, OP + own // 2 - 1, -1)
+        keep_y = jnp.where((parity == 1) & ((pair == end) | (pair == other)), 0.0, 1.0)
+        last_z = (lane == 127) if len(shape) == 3 else (lane == 127) & (index(1) == 1)
+        return keep_y, jnp.where(last_z, 0.0, 1.0)
+
     fold_c = one_hot((64, 128), lambda row, column: row // 8 + 8 * (row % 8) == column // 2)
 
     fine = (f_wx, f_wyu, f_wyd, f_wzu, f_wzd, f_diag, f_damp)
-    keep_y, keep_z = keep_yz(8, (2, ROWS, 128))
+    f_mob = (f_in.at[M0], f_in.at[M1], f_in.at[M2])
+    f_store = f_in.at[STORE]
+    keep_y, keep_z = keep_yz(8, (2, 2, 8, 128))
     received(FINE_Y)
-    weights_yz(fine, f_in, (O, O + 8), keep_y, keep_z)
-    weights_x(fine, f_in, (O, O + 7))
-    diagonals(fine, f_in, (O + 1, O + 7))
+    weights_yz(fine, f_mob, (O, O + 8), keep_y, keep_z)
+    weights_x(fine, f_mob, (O, O + 7))
+    diagonals(fine, f_store, (O + 1, O + 7))
     start_sweep(fine, f_src, f_a, (O + 1, O + 7))
     received(COEF_X)
     for e in range(-REACH, REACH + 1):
@@ -365,55 +391,46 @@
             push(COEF_Y, c_coef.at[:, 0:6, OWN_C, :], target, (0, e))
     received(FINE_X)
     for rows in ((O - 3, O), (O + 7, O + 10)):
-        weights_x(fine, f_in, rows)
+        weights_x(fine, f_mob, rows)
     f_wx[O - 1] = f_wx[O - 1] * keep_x[0]
     f_wx[O + 7] = f_wx[O + 7] * keep_x[1]
     for rows in ((O - 2, O), (O + 8, O + 10)):
-        weights_yz(fine, f_in, rows, keep_y, keep_z)
+        weights_yz(fine, f_mob, rows, keep_y, keep_z)
     for rows in ((O - 2, O + 1), (O + 7, O + 10)):
-        diagonals(fine, f_in, rows)
+        diagonals(fine, f_store, rows)
         start_sweep(fine, f_src, f_a, rows)
     sweep(fine, f_src, f_a, f_b, (O - 1, O + 9))
 
     def folded(x, _):
-        first = row_residual(fine, f_src, f_b, O + 2 * x)
-        f_spread[x] = first + row_residual(fine, f_src, f_b, O + 2 * x + 1)
+        both = row_residual(fine, f_src, f_b, O + 2 * x) + row_residual(fine, f_src, f_b, O + 2 * x + 1)
+        m_fold[x] = (both[0, 0] + both[0, 1]) + (both[1, 0] + both[1, 1])
+        for parity in range(2):
+            m_src[O + x, parity, pairs4] = m_fold[x, pl.ds(OP + parity, 2, stride=2), :]
         return 0
 
     lax.fori_loop(0, 4, folded, 0, unroll=True)
-    halves = [f_spread[0:4, half].reshape(4 * ROWS, 128) for half in range(2)]
-    m_fold[0:4] = times_one_hot(jnp.concatenate(halves, axis=1), half_f).reshape(4, ROWS, 128)
-
-    def pairs(x, _):
-        even = m_fold[x, pl.ds(O, 4, stride=2), :]
-        m_src[O + x, O : O + 4, :] = even + m_fold[x, pl.ds(O + 1, 4, stride=2), :]
-        return 0
-
-    lax.fori_loop(0, 4, pairs, 0, unroll=True)
-
-    for sx, sy in NEIGHBOURS:
-        wide = 2 if sx != 0 and sy != 0 else 3
-        ax, ay, bx, by = spans(sx, sy, 4, wide, wide)
-        push(MID_F, m_src.at[ax, ay, :], m_src.at[bx, by, :], (sx, sy))
+    for step in NEIGHBOURS:
+        ax, ay, bx, by = spans(*step, 4, 2 if step in corners else 3, 1 if step in corners else 2)
+        push(MID_F, m_src.at[ax, :, ay, :], m_src.at[bx, :, by, :], step)
 
     def keep_fine(x, _):
-        f_x[x, :, O : O + 8, :] = f_b[x, :, O : O + 8, :]
+        f_x[x, :, :, pairs8] = f_b[x, :, :, pairs8]
         return 0
 
     lax.fori_loop(O, O + 8, keep_fine, 0, unroll=True)
-    for sx, sy in NEIGHBOURS:
-        wide = 2 if sx != 0 and sy != 0 else 3
-        ax, ay, bx, by = spans(sx, sy, 8, wide, wide)
-        push(FINE_V, f_x.at[ax, :, ay, :], f_x.at[bx, :, by, :], (sx, sy))
+    for step in NEIGHBOURS:
+        ax, ay, bx, by = spans(*step, 8, 2 if step in corners else 3, 1 if step in corners else 2)
+        push(FINE_V, f_x.at[ax, :, :, ay, :], f_x.at[bx, :, :, by, :], step)
 
     mid = (m_wx, m_wyu, m_wyd, m_wzu, m_wzd, m_diag, m_damp)
-    keep_y, keep_z = keep_yz(4, (ROWS, 128))
+    m_mob = (m_in.at[0], m_in.at[1], m_in.at[2])
+    keep_y, keep_z = keep_yz(4, (2, 8, 128))
     received(MID_IN)
-    weights_x(mid, m_in, (O - 4, O + 7))
+    weights_x(mid, m_mob, (O - 4, O + 7))
     m_wx[O - 1] = m_wx[O - 1] * keep_x[0]
     m_wx[O + 3] = m_wx[O + 3] * keep_x[1]
-    weights_yz(mid, m_in, (O - 3, O + 7), keep_y, keep_z)
-    diagonals(mid, m_in, (O - 3, O + 7))
+    weights_yz(mid, m_mob, (O - 3, O + 7), keep_y, keep_z)
+    diagonals(mid, m_in.at[3], (O - 3, O + 7))
 
     received(COEF_Y)
     coef = [c_coef[k, :, 8:24, :].reshape(128, 64).T for k in range(4)]
@@ -445,10 +462,7 @@
     sweep(mid, m_src, m_a, m_b, (O - 1, O + 5))
     for ix in range(2):
         fold = row_residual(mid, m_src, m_b, O + 2 * ix) + row_residual(mid, m_src, m_b, O + 2 * ix + 1)
-        for iy in range(2):
-            first = O + 2 * iy
-            at = OWN_C.start + iy
-            c_src[2 + ix, at : at + 1, :] = fold[first : first + 1] + fold[first + 1 : first + 2]
+        c_src[2 + ix, OWN_C, :] = (fold[0] + fold[1])[pairs4]
     for e in sorted(range(-REACH, REACH + 1), key=lambda e: -abs(e)):
         for g in (1, -1, 0):
             if (g, e) != (0, 0):
@@ -456,14 +470,13 @@
                 push(COARSE_F, c_src.at[2:4, OWN_C, :], target, (g, e))
 
     def keep_mid(x, _):
-        m_y[x, O : O + 4, :] = m_b[x, O : O + 4, :]
+        m_y[x, :, pairs4] = m_b[x, :, pairs4]
         return 0
 
     lax.fori_loop(O, O + 4, keep_mid, 0, unroll=True)
-    for sx, sy in NEIGHBOURS:
-        wide = 3 if sx != 0 and sy != 0 else 4
-        ax, ay, bx, by = spans(sx, sy, 4, wide, wide)
-        push(MID_V, m_y.at[ax, ay, :], m_y.at[bx, by, :], (sx, sy))
+    for step in NEIGHBOURS:
+        ax, ay, bx, by = spans(*step, 4, 3 if step in corners else 4, 2)
+        push(MID_V, m_y.at[ax, :, ay, :], m_y.at[bx, :, by, :], step)
 
     def registers(at):
         return [c_bands[at, pl.ds(place, 8, stride=8), :] for place in range(8)]
@@ -546,7 +559,7 @@
     received(COARSE_F)
     source = lax.dot_general(
         jnp.concatenate([fold_c] * 2, axis=1),
-        jnp.concatenate(pieces(c_src[:, 8:24, :].reshape(128, 128)), axis=1),
+        jnp.concatenate(pieces(c_src[:, 8:24, :].reshape(128, 128), 2), axis=1),
         (((1,), (1,)), ((), ())),
         preferred_element_type=jnp.float32,
     )
@@ -562,55 +575,59 @@
         return lines(pushed)
 
     z = lax.fori_loop(0, KC - 1, turn, lines(sources))
-    c_ext[...] = times_one_hot(jnp.concatenate(z, axis=0).T[0:96], fold_c).reshape(6, 16, 128)
+    c_ext[...] = times_one_hot(jnp.concatenate(z, axis=0).T[0:96], fold_c, 2).reshape(6, 16, 128)
 
     received(MID_V)
 
     def raise_mid(x, _):
         rows = c_ext[x, 5:13, :]
-        c_spread[x, pl.ds(0, 8, stride=2), :] = rows
-        c_spread[x, pl.ds(1, 8, stride=2), :] = rows
-        doubled = c_spread[x]
-        m_a[2 * x] = m_y[2 * x] + doubled
-        m_a[2 * x + 1] = m_y[2 * x + 1] + doubled
+        for along in range(2):
+            for parity in range(2):
+                m_a[2 * x + along, parity] = m_y[2 * x + along, parity] + rows
         return 0
 
     lax.fori_loop(0, 6, raise_mid, 0, unroll=True)
     sweep(mid, m_src, m_a, m_b, (O - 3, O + 7))
     sweep(mid, m_src, m_b, m_a, (O - 2, O + 6))
 
-    def raise_rows(x, _):
-        rows = m_a[O - 2 + x, O - 2 : O + 6, :]
-        m_fold[x, pl.ds(0, 8, stride=2), :] = rows
-        m_fold[x, pl.ds(1, 8, stride=2), :] = rows
-        return 0
-
-    lax.fori_loop(0, 8, raise_rows, 0, unroll=True)
-    double_f = one_hot((128, 256), lambda row, column: row == column // 2)
-    doubled_z = times_one_hot(m_fold[...].reshape(8 * ROWS, 128), double_f)
-    for half in range(2):
-        f_spread[:, half] = doubled_z[:, 128 * half : 128 * half + 128].reshape(8, ROWS, 128)
     received(FINE_V)
 
     def raise_fine(x, _):
-        f_a[2 * x] = f_x[2 * x] + f_spread[x]
-        f_a[2 * x + 1] = f_x[2 * x + 1] + f_spread[x]
+        for parity in range(2):
+            m_fold[x, pl.ds(parity, 4, stride=2), :] = m_a[O - 2 + x, parity, 1:5]
+        rows = m_fold[x]
+        for along in range(2):
+            for parity in range(2):
+                for half in range(2):
+                    at = (2 * x + along, parity, half)
+                    f_a[at] = f_x[at] + rows
         return 0
 
     lax.fori_loop(0, 8, raise_fine, 0, unroll=True)
     sweep(fine, f_src, f_a, f_b, (O - 2, O + 10))
     sweep(fine, f_src, f_b, f_a, (O - 1, O + 9))
 
+    together = one_hot((256, 256), lambda row, column: column == 2 * (row % 128) + row // 128)
+
+    def in_order(field, result):
+        def sort_back(x, _):
+            for parity in range(2):
+                for half in range(2):
+                    f_rows[half, x, pl.ds(parity, 8, stride=2), :] = field[O + x, parity, half]
+            return 0
+
+        lax.fori_loop(0, 8, sort_back, 0, unroll=True)
+        halves = [f_rows[half, :, O : O + 8, :].reshape(64, 128) for half in range(2)]
+        result[...] = times_one_hot(jnp.concatenate(halves, axis=1), together, 3).reshape(8, 8, 256)
+
+    in_order(f_a, pressure)
+
     def last(x, _):
-        left = row_residual(fine, f_src, f_a, x)
-        own = f_a[x]
-        for half in range(2):
-            columns = slice(128 * half, 128 * half + 128)
-            pressure[x - O, :, columns] = own[half, O : O + 8]
-            residual[x - O, :, columns] = left[half, O : O + 8]
+        f_b[x] = row_residual(fine, f_src, f_a, x)
         return 0
 
     lax.fori_loop(O, O + 8, last, 0, unroll=True)
+    in_order(f_b, residual)
     for at in (COARSE_F, MID_V):
         sent(at)
 
@@ -630,8 +647,8 @@
     count_x = lax.axis_size("gx")
     count_y = lax.axis_size("gy")
     f32 = jnp.float32
-    fine = pltpu.VMEM((8 + 2 * O, 2, ROWS, 128), f32)
-    mid = pltpu.VMEM((4 + 2 * O, ROWS, 128), f32)
+    fine = pltpu.VMEM((8 + 2 * O, 2, 2, 8, 128), f32)
+    mid = pltpu.VMEM((4 + 2 * O, 2, 8, 128), f32)
     in_hbm = pl.BlockSpec(memory_space=pltpu.HBM)
     in_vmem = pl.BlockSpec(memory_space=pltpu.VMEM)
     arrays = (pressure_rhs, storage_fine, mobility_fine, storage_mid, mobility_mid, storage_coarse, mobility_coarse)
@@ -641,16 +658,17 @@
         in_specs=[in_hbm] * 7,
         out_specs=(in_vmem, in_vmem),
         scratch_shapes=[
-            pltpu.VMEM((5, 8 + 2 * O, 2, ROWS, 128), f32),
+            pltpu.VMEM((5, 8, 8, 256), f32),
+            pltpu.VMEM((2, 40, 8, 128), f32),
+            pltpu.VMEM((5, 8 + 2 * O, 2, 2, 8, 128), f32),
             *[fine] * 10,
-            pltpu.VMEM((4, 4 + 2 * O, ROWS, 128), f32),
+            pltpu.VMEM((4, 4 + 2 * O, 2, 8, 128), f32),
             *[mid] * 11,
-            pltpu.VMEM((8, ROWS, 128), f32),
-            pltpu.VMEM((8, 2, ROWS, 128), f32),
+            pltpu.VMEM((8, 8, 128), f32),
+            pltpu.VMEM((2, 8, 16, 128), f32),
             pltpu.VMEM((4, 8, 32, 64), f32),
             pltpu.VMEM((8, 32, 128), f32),
             pltpu.VMEM((6, 16, 128), f32),
-            pltpu.VMEM((6, ROWS, 128), f32),
             pltpu.VMEM((4, 8, 8, 128), f32),
             pltpu.VMEM((7, 64, 128), f32),
             pltpu.VMEM((97, 8, 128), f32),

time: 35.2 us -> 35 us (level)
  no operation moved by 1% of the time
where the time goes in v5:
time: 35 us; the launch traced here: 34.8 us
  Pallas kernels  34.2 us (98%)
  between operations  0.64 us (2%)
    pallas_call x1, Pallas kernels, local(): pl.pallas_call(functools.partial(kernel, count_x, count_y), out_shape=(pl...  33.5 us

profile of v5, /device:TPU:1, one launch (start us, length us, event | category | flops | bytes accessed | tf_op | source)
XLA Modules:
  0.0 34.8 jit_solution(16146169394638580066)
XLA Ops:
  0.6 33.5 %shard_map.86 = (f32[8,8,256]{2,1,0:T(8,128)S(1)}, f32[8,8,256]{2,1,0:T(8,128)S(1)}) custom-call(f32[8,8,256]{2,1,0:T(8,128)} %rhs_h.1, f32[8,8,256]{2,1,0:T(8,128)} %store_f_h.1, f32[3,8,8,256]{3,2,1,0:T(8,128)} %mob_f_h.1, f32[4,4,128]{2,1,0:T(4,128)} %store_m_h.1, f32[3,4,4,128]{3,2,1,0:T(4,128)} %mob_m_h.1, f32[2,2,64]{2,1,0:T(2,128)} %store_c_h.1, ...), custom_call_target="tpu_custom_call" | custom-call | tf_op jit(solution)/shard_map/pallas_call | solution.py:655
  34.1 0.7 %shard_map.87 = (f32[8,8,256]{2,1,0:T(8,128)}, f32[8,8,256]{2,1,0:T(8,128)}) custom-call(f32[8,8,256]{2,1,0:T(8,128)S(1)} %get-tuple-element.4.pressure, f32[8,8,256]{2,1,0:T(8,128)S(1)} %get-tuple-element.5.residual), custom_call_target="tpu_custom_call" | custom-call | tf_op jit(solution)/shard_map/pallas_call | solution.py:685

commit v6 on v5

--- a/solution.py
+++ b/solution.py
@@ -218,6 +218,8 @@
     c_bands,
     c_inverse,
     meter,
+    spare,
+    c_spare,
     local_sem,
     send_sem,
     recv_sem,
@@ -237,10 +239,24 @@
     def beside(sx, sy):
         return {"gx": along_gx[sx], "gy": along_gy[sy]}
 
-    partners = NEIGHBOURS + tuple((0, e) for e in range(-REACH, REACH + 1) if abs(e) > 1)
+    def ahead_of(sx):
+        return gx < count_x - 1 if sx > 0 else gx > 0
+
     barrier = pltpu.get_barrier_semaphore()
-    for step in partners:
-        pl.semaphore_signal(barrier, inc=1, device_id=beside(*step), device_id_type=MESH)
+
+    def greet(steps):
+        for step in steps:
+            pl.semaphore_signal(barrier, inc=1, device_id=beside(*step), device_id_type=MESH)
+
+    for side in (1, -1):
+
+        @pl.when(ahead_of(side))
+        def _():
+            greet([step for step in NEIGHBOURS if step[0] == side])
+
+    straight = [(0, e) for e in range(-REACH, REACH + 1) if e != 0]
+    greet(straight)
+    partners = len(straight) + jnp.where(gx > 0, 3, 0) + jnp.where(gx < count_x - 1, 3, 0)
 
     c_coef[:, 6:8] = jnp.ones((4, 2, 32, 64), jnp.float32)
     c_src[6:8] = jnp.zeros((2, 32, 128), jnp.float32)
@@ -253,20 +269,55 @@
         locals_.append(copy)
         return copy
 
-    def push(at, source, target, step):
-        pltpu.make_async_remote_copy(
-            src_ref=source,
-            dst_ref=target,
-            send_sem=send_sem.at[at],
-            recv_sem=recv_sem.at[at],
-            device_id=beside(*step),
-            device_id_type=MESH,
-        ).start()
-        rows = 1
-        for size in source.shape[:-1]:
-            rows = rows * size
-        rows_of[at] = rows_of.get(at, 0) + rows
-
+    def exchange(at, messages):
+        sizes = []
+        for source, _, _ in messages:
+            rows = 1
+            for size in source.shape[:-1]:
+                rows = rows * size
+            sizes.append(rows)
+        rows_of[at] = rows_of.get(at, 0) + sum(sizes)
+
+        def send(side):
+            for source, target, step in messages:
+                if step[0] == side:
+                    pltpu.make_async_remote_copy(
+                        src_ref=source,
+                        dst_ref=target,
+                        send_sem=send_sem.at[at],
+                        recv_sem=recv_sem.at[at],
+                        device_id=beside(*step),
+                        device_id_type=MESH,
+                    ).start()
+
+        for side in (1, -1):
+            rows = sum(size for size, message in zip(sizes, messages) if message[2][0] == side)
+            if rows == 0:
+                continue
+            first = spent[0]
+            spent[0] += rows
+
+            @pl.when(ahead_of(side))
+            def _():
+                send(side)
+
+            @pl.when(jnp.logical_not(ahead_of(side)))
+            def _():
+                if at == COEF_X:
+                    pltpu.make_async_copy(c_coef.at[:, 2:4, OWN_C, :], c_spare, send_sem.at[at]).start()
+                else:
+                    spare_to = spare.at[first : first + rows, :]
+                    pltpu.make_async_copy(meter.at[0:rows, :], spare_to, send_sem.at[at]).start()
+
+            @pl.when(jnp.logical_not(ahead_of(-side)))
+            def _():
+                for source, target, step in messages:
+                    if step[0] == side:
+                        pltpu.make_async_copy(source, target, recv_sem.at[at]).start()
+
+        send(0)
+
+    spent = [0]
     rows_of = {}
 
     def all_of(at):
@@ -328,35 +379,41 @@
         return 0
 
     lax.fori_loop(0, 8, sort_y, 0, unroll=True)
-    pl.semaphore_wait(barrier, len(partners))
-
-    def push_fine(at, first, last, step, wide_x, wide_y):
+    pl.semaphore_wait(barrier, partners)
+
+    def part(first, last, step, wide_x, wide_y):
         fields = slice(first, last + 1)
         ax, ay, bx, by = spans(*step, 8, wide_x, wide_y)
-        push(at, f_in.at[fields, ax, :, :, ay, :], f_in.at[fields, bx, :, :, by, :], step)
+        return (f_in.at[fields, ax, :, :, ay, :], f_in.at[fields, bx, :, :, by, :], step)
 
     for copy in coarse_in:
         copy.wait()
-    for sx, sy in faces_x:
-        own = c_coef.at[:, 2:4, OWN_C, :]
-        push(COEF_X, own, c_coef.at[:, 2 - 2 * sx : 4 - 2 * sx, OWN_C, :], (sx, sy))
-
+    exchange(
+        COEF_X,
+        [
+            (c_coef.at[:, 2:4, OWN_C, :], c_coef.at[:, 2 - 2 * sx : 4 - 2 * sx, OWN_C, :], (sx, sy))
+            for sx, sy in faces_x
+        ],
+    )
+
+    messages = []
     for step in faces_x:
-        push_fine(FINE_X, M0, M0, step, 3, 1)
-        push_fine(FINE_X, M2, M1, step, 2, 1)
+        messages += [part(M0, M0, step, 3, 1), part(M2, M1, step, 2, 1)]
     for step in corners:
-        push_fine(FINE_X, M0, M0, step, 2, 1)
-        push_fine(FINE_X, M1, M1, step, 2, 1)
-        push_fine(FINE_X, M2, SOURCE, step, 1, 1)
+        messages += [part(M0, M0, step, 2, 1), part(M1, M1, step, 2, 1), part(M2, SOURCE, step, 1, 1)]
+    exchange(FINE_X, messages)
+    messages = []
     for step in faces_y:
-        push_fine(FINE_Y, M0, SOURCE, step, 1, 1)
-        push_fine(FINE_Y, M1, M1, step, 1, 2)
+        messages += [part(M0, SOURCE, step, 1, 1), part(M1, M1, step, 1, 2)]
+    exchange(FINE_Y, messages)
 
     for copy in mid_in:
         copy.wait()
+    messages = []
     for step in NEIGHBOURS:
         ax, ay, bx, by = spans(*step, 4, 3 if step in corners else 4, 2)
-        push(MID_IN, m_in.at[:, ax, :, ay, :], m_in.at[:, bx, :, by, :], step)
+        messages.append((m_in.at[:, ax, :, ay, :], m_in.at[:, bx, :, by, :], step))
+    exchange(MID_IN, messages)
 
     one = jnp.float32(1.0)
     nil = jnp.float32(0.0)
@@ -385,10 +442,11 @@
     diagonals(fine, f_store, (O + 1, O + 7))
     start_sweep(fine, f_src, f_a, (O + 1, O + 7))
     received(COEF_X)
-    for e in range(-REACH, REACH + 1):
-        if e != 0:
-            target = c_coef.at[:, 0:6, OWN_C.start - 2 * e : OWN_C.stop - 2 * e, :]
-            push(COEF_Y, c_coef.at[:, 0:6, OWN_C, :], target, (0, e))
+    messages = []
+    for step in straight:
+        target = c_coef.at[:, 0:6, OWN_C.start - 2 * step[1] : OWN_C.stop - 2 * step[1], :]
+        messages.append((c_coef.at[:, 0:6, OWN_C, :], target, step))
+    exchange(COEF_Y, messages)
     received(FINE_X)
     for rows in ((O - 3, O), (O + 7, O + 10)):
         weights_x(fine, f_mob, rows)
@@ -409,18 +467,22 @@
         return 0
 
     lax.fori_loop(0, 4, folded, 0, unroll=True)
+    messages = []
     for step in NEIGHBOURS:
         ax, ay, bx, by = spans(*step, 4, 2 if step in corners else 3, 1 if step in corners else 2)
-        push(MID_F, m_src.at[ax, :, ay, :], m_src.at[bx, :, by, :], step)
+        messages.append((m_src.at[ax, :, ay, :], m_src.at[bx, :, by, :], step))
+    exchange(MID_F, messages)
 
     def keep_fine(x, _):
         f_x[x, :, :, pairs8] = f_b[x, :, :, pairs8]
         return 0
 
     lax.fori_loop(O, O + 8, keep_fine, 0, unroll=True)
+    messages = []
     for step in NEIGHBOURS:
         ax, ay, bx, by = spans(*step, 8, 2 if step in corners else 3, 1 if step in corners else 2)
-        push(FINE_V, f_x.at[ax, :, :, ay, :], f_x.at[bx, :, :, by, :], step)
+        messages.append((f_x.at[ax, :, :, ay, :], f_x.at[bx, :, :, by, :], step))
+    exchange(FINE_V, messages)
 
     mid = (m_wx, m_wyu, m_wyd, m_wzu, m_wzd, m_diag, m_damp)
     m_mob = (m_in.at[0], m_in.at[1], m_in.at[2])
@@ -463,20 +525,24 @@
     for ix in range(2):
         fold = row_residual(mid, m_src, m_b, O + 2 * ix) + row_residual(mid, m_src, m_b, O + 2 * ix + 1)
         c_src[2 + ix, OWN_C, :] = (fold[0] + fold[1])[pairs4]
+    messages = []
     for e in sorted(range(-REACH, REACH + 1), key=lambda e: -abs(e)):
         for g in (1, -1, 0):
             if (g, e) != (0, 0):
                 target = c_src.at[2 - 2 * g : 4 - 2 * g, OWN_C.start - 2 * e : OWN_C.stop - 2 * e, :]
-                push(COARSE_F, c_src.at[2:4, OWN_C, :], target, (g, e))
+                messages.append((c_src.at[2:4, OWN_C, :], target, (g, e)))
+    exchange(COARSE_F, messages)
 
     def keep_mid(x, _):
         m_y[x, :, pairs4] = m_b[x, :, pairs4]
         return 0
 
     lax.fori_loop(O, O + 4, keep_mid, 0, unroll=True)
+    messages = []
     for step in NEIGHBOURS:
         ax, ay, bx, by = spans(*step, 4, 3 if step in corners else 4, 2)
-        push(MID_V, m_y.at[ax, :, ay, :], m_y.at[bx, :, by, :], step)
+        messages.append((m_y.at[ax, :, ay, :], m_y.at[bx, :, by, :], step))
+    exchange(MID_V, messages)
 
     def registers(at):
         return [c_bands[at, pl.ds(place, 8, stride=8), :] for place in range(8)]
@@ -673,6 +739,8 @@
             pltpu.VMEM((7, 64, 128), f32),
             pltpu.VMEM((97, 8, 128), f32),
             pltpu.VMEM((1024, 128), f32),
+            pltpu.VMEM((4096, 128), f32),
+            pltpu.VMEM((4, 2, 2, 64), f32),
             pltpu.SemaphoreType.DMA((16,)),
             pltpu.SemaphoreType.DMA((EXCHANGES,)),
             pltpu.SemaphoreType.DMA((EXCHANGES,)),

time: 35 us -> 31.4 us (0.90)
  the two profiles are of different devices: /device:TPU:1 before, /device:TPU:6 now
where the time goes in v6:
time: 31.4 us; the launch traced here: 31.3 us
  Pallas kernels  30.7 us (98%)
  between operations  0.64 us (2%)
    pallas_call x1, Pallas kernels, local(): pl.pallas_call(functools.partial(kernel, count_x, count_y), out_shape=(pl...  30 us
    pallas_call x1, Pallas kernels, local(): pl.pallas_call(publish, out_shape=(out, out), in_specs=[in_vmem] * 2, out...  0.67 us

profile of v6, /device:TPU:6, one launch (start us, length us, event | category | flops | bytes accessed | tf_op | source)
XLA Modules:
  0.0 31.3 jit_solution(201732105544830355)
XLA Ops:
  0.6 30.0 %shard_map.86 = (f32[8,8,256]{2,1,0:T(8,128)S(1)}, f32[8,8,256]{2,1,0:T(8,128)S(1)}) custom-call(f32[8,8,256]{2,1,0:T(8,128)} %rhs_h.1, f32[8,8,256]{2,1,0:T(8,128)} %store_f_h.1, f32[3,8,8,256]{3,2,1,0:T(8,128)} %mob_f_h.1, f32[4,4,128]{2,1,0:T(4,128)} %store_m_h.1, f32[3,4,4,128]{3,2,1,0:T(4,128)} %mob_m_h.1, f32[2,2,64]{2,1,0:T(2,128)} %store_c_h.1, ...), custom_call_target="tpu_custom_call" | custom-call | tf_op jit(solution)/shard_map/pallas_call | solution.py:721
  30.6 0.7 %shard_map.87 = (f32[8,8,256]{2,1,0:T(8,128)}, f32[8,8,256]{2,1,0:T(8,128)}) custom-call(f32[8,8,256]{2,1,0:T(8,128)S(1)} %get-tuple-element.4.pressure, f32[8,8,256]{2,1,0:T(8,128)S(1)} %get-tuple-element.5.residual), custom_call_target="tpu_custom_call" | custom-call | tf_op jit(solution)/shard_map/pallas_call | solution.py:753

commit v7 on v6

--- a/solution.py
+++ b/solution.py
@@ -211,6 +211,7 @@
     m_y,
     m_fold,
     f_rows,
+    together,
     c_coef,
     c_src,
     c_ext,
@@ -366,7 +367,7 @@
     apart = one_hot((256, 256), lambda row, column: row == 2 * (column % 128) + column // 128)
     for copy in fine_in:
         copy.wait()
-    sorted_z = times_one_hot(f_stage[...].reshape(320, 256), apart, 3)
+    sorted_z = times_one_hot(f_stage[...].reshape(320, 256), apart, 2)
     for half in range(2):
         f_mixed[half] = sorted_z[:, 128 * half : 128 * half + 128].reshape(40, 8, 128)
 
@@ -407,14 +408,6 @@
         messages += [part(M0, SOURCE, step, 1, 1), part(M1, M1, step, 1, 2)]
     exchange(FINE_Y, messages)
 
-    for copy in mid_in:
-        copy.wait()
-    messages = []
-    for step in NEIGHBOURS:
-        ax, ay, bx, by = spans(*step, 4, 3 if step in corners else 4, 2)
-        messages.append((m_in.at[:, ax, :, ay, :], m_in.at[:, bx, :, by, :], step))
-    exchange(MID_IN, messages)
-
     one = jnp.float32(1.0)
     nil = jnp.float32(0.0)
     keep_x = (jnp.where(gx == 0, nil, one), jnp.where(gx == count_x - 1, nil, one))
@@ -430,6 +423,7 @@
         last_z = (lane == 127) if len(shape) == 3 else (lane == 127) & (index(1) == 1)
         return keep_y, jnp.where(last_z, 0.0, 1.0)
 
+    together[...] = one_hot((256, 256), lambda row, column: column == 2 * (row % 128) + row // 128)
     fold_c = one_hot((64, 128), lambda row, column: row // 8 + 8 * (row % 8) == column // 2)
 
     fine = (f_wx, f_wyu, f_wyd, f_wzu, f_wzd, f_diag, f_damp)
@@ -441,6 +435,14 @@
     weights_x(fine, f_mob, (O, O + 7))
     diagonals(fine, f_store, (O + 1, O + 7))
     start_sweep(fine, f_src, f_a, (O + 1, O + 7))
+    for copy in mid_in:
+        copy.wait()
+    messages = []
+    for step in NEIGHBOURS:
+        ax, ay, bx, by = spans(*step, 4, 3 if step in corners else 4, 2)
+        messages.append((m_in.at[:, ax, :, ay, :], m_in.at[:, bx, :, by, :], step))
+    exchange(MID_IN, messages)
+
     received(COEF_X)
     messages = []
     for step in straight:
@@ -673,7 +675,6 @@
     sweep(fine, f_src, f_a, f_b, (O - 2, O + 10))
     sweep(fine, f_src, f_b, f_a, (O - 1, O + 9))
 
-    together = one_hot((256, 256), lambda row, column: column == 2 * (row % 128) + row // 128)
 
     def in_order(field, result):
         def sort_back(x, _):
@@ -684,7 +685,7 @@
 
         lax.fori_loop(0, 8, sort_back, 0, unroll=True)
         halves = [f_rows[half, :, O : O + 8, :].reshape(64, 128) for half in range(2)]
-        result[...] = times_one_hot(jnp.concatenate(halves, axis=1), together, 3).reshape(8, 8, 256)
+        result[...] = times_one_hot(jnp.concatenate(halves, axis=1), together[...], 2).reshape(8, 8, 256)
 
     in_order(f_a, pressure)
 
@@ -732,6 +733,7 @@
             *[mid] * 11,
             pltpu.VMEM((8, 8, 128), f32),
             pltpu.VMEM((2, 8, 16, 128), f32),
+            pltpu.VMEM((256, 256), jnp.bfloat16),
             pltpu.VMEM((4, 8, 32, 64), f32),
             pltpu.VMEM((8, 32, 128), f32),
             pltpu.VMEM((6, 16, 128), f32),

time: 31.4 us -> 31.8 us (1.013)
  no operation moved by 1% of the time
where the time goes in v7:
time: 31.8 us; the launch traced here: 31.4 us
  Pallas kernels  30.8 us (97%)
  between operations  0.64 us (2%)
    pallas_call x1, Pallas kernels, local(): pl.pallas_call(functools.partial(kernel, count_x, count_y), out_shape=(pl...  30.1 us
    pallas_call x1, Pallas kernels, local(): pl.pallas_call(publish, out_shape=(out, out), in_specs=[in_vmem] * 2, out...  0.67 us

profile of v7, /device:TPU:6, one launch (start us, length us, event | category | flops | bytes accessed | tf_op | source)
XLA Modules:
  0.0 31.4 jit_solution(4609836821427953578)
XLA Ops:
  0.6 30.1 %shard_map.86 = (f32[8,8,256]{2,1,0:T(8,128)S(1)}, f32[8,8,256]{2,1,0:T(8,128)S(1)}) custom-call(f32[8,8,256]{2,1,0:T(8,128)} %rhs_h.1, f32[8,8,256]{2,1,0:T(8,128)} %store_f_h.1, f32[3,8,8,256]{3,2,1,0:T(8,128)} %mob_f_h.1, f32[4,4,128]{2,1,0:T(4,128)} %store_m_h.1, f32[3,4,4,128]{3,2,1,0:T(4,128)} %mob_m_h.1, f32[2,2,64]{2,1,0:T(2,128)} %store_c_h.1, ...), custom_call_target="tpu_custom_call" | custom-call | tf_op jit(solution)/shard_map/pallas_call | solution.py:722
  30.8 0.7 %shard_map.87 = (f32[8,8,256]{2,1,0:T(8,128)}, f32[8,8,256]{2,1,0:T(8,128)}) custom-call(f32[8,8,256]{2,1,0:T(8,128)S(1)} %get-tuple-element.4.pressure, f32[8,8,256]{2,1,0:T(8,128)S(1)} %get-tuple-element.5.residual), custom_call_target="tpu_custom_call" | custom-call | tf_op jit(solution)/shard_map/pallas_call | solution.py:755

commit v8 on v6

--- a/solution.py
+++ b/solution.py
@@ -211,6 +211,7 @@
     m_y,
     m_fold,
     f_rows,
+    together,
     c_coef,
     c_src,
     c_ext,
@@ -366,7 +367,7 @@
     apart = one_hot((256, 256), lambda row, column: row == 2 * (column % 128) + column // 128)
     for copy in fine_in:
         copy.wait()
-    sorted_z = times_one_hot(f_stage[...].reshape(320, 256), apart, 3)
+    sorted_z = times_one_hot(f_stage[...].reshape(320, 256), apart, 2)
     for half in range(2):
         f_mixed[half] = sorted_z[:, 128 * half : 128 * half + 128].reshape(40, 8, 128)
 
@@ -381,10 +382,10 @@
     lax.fori_loop(0, 8, sort_y, 0, unroll=True)
     pl.semaphore_wait(barrier, partners)
 
-    def part(first, last, step, wide_x, wide_y):
+    def part(first, last, step, wide_x, wide_y, parity=slice(0, 2)):
         fields = slice(first, last + 1)
         ax, ay, bx, by = spans(*step, 8, wide_x, wide_y)
-        return (f_in.at[fields, ax, :, :, ay, :], f_in.at[fields, bx, :, :, by, :], step)
+        return (f_in.at[fields, ax, parity, :, ay, :], f_in.at[fields, bx, parity, :, by, :], step)
 
     for copy in coarse_in:
         copy.wait()
@@ -400,7 +401,8 @@
     for step in faces_x:
         messages += [part(M0, M0, step, 3, 1), part(M2, M1, step, 2, 1)]
     for step in corners:
-        messages += [part(M0, M0, step, 2, 1), part(M1, M1, step, 2, 1), part(M2, SOURCE, step, 1, 1)]
+        nearest = slice(1, 2) if step[1] > 0 else slice(0, 1)
+        messages += [part(M0, M0, step, 2, 1), part(M1, M1, step, 2, 1), part(M2, SOURCE, step, 1, 1, nearest)]
     exchange(FINE_X, messages)
     messages = []
     for step in faces_y:
@@ -430,6 +432,7 @@
         last_z = (lane == 127) if len(shape) == 3 else (lane == 127) & (index(1) == 1)
         return keep_y, jnp.where(last_z, 0.0, 1.0)
 
+    together[...] = one_hot((256, 256), lambda row, column: column == 2 * (row % 128) + row // 128)
     fold_c = one_hot((64, 128), lambda row, column: row // 8 + 8 * (row % 8) == column // 2)
 
     fine = (f_wx, f_wyu, f_wyd, f_wzu, f_wzd, f_diag, f_damp)
@@ -447,6 +450,7 @@
         target = c_coef.at[:, 0:6, OWN_C.start - 2 * step[1] : OWN_C.stop - 2 * step[1], :]
         messages.append((c_coef.at[:, 0:6, OWN_C, :], target, step))
     exchange(COEF_Y, messages)
+    sweep(fine, f_src, f_a, f_b, (O + 2, O + 6))
     received(FINE_X)
     for rows in ((O - 3, O), (O + 7, O + 10)):
         weights_x(fine, f_mob, rows)
@@ -457,7 +461,8 @@
     for rows in ((O - 2, O + 1), (O + 7, O + 10)):
         diagonals(fine, f_store, rows)
         start_sweep(fine, f_src, f_a, rows)
-    sweep(fine, f_src, f_a, f_b, (O - 1, O + 9))
+    for rows in ((O - 1, O + 2), (O + 6, O + 9)):
+        sweep(fine, f_src, f_a, f_b, rows)
 
     def folded(x, _):
         both = row_residual(fine, f_src, f_b, O + 2 * x) + row_residual(fine, f_src, f_b, O + 2 * x + 1)
@@ -493,6 +498,34 @@
     m_wx[O + 3] = m_wx[O + 3] * keep_x[1]
     weights_yz(mid, m_mob, (O - 3, O + 7), keep_y, keep_z)
     diagonals(mid, m_in.at[3], (O - 3, O + 7))
+
+    for at in (FINE_X, FINE_Y, COEF_X, MID_IN):
+        sent(at)
+
+    received(MID_F)
+    start_sweep(mid, m_src, m_a, (O - 2, O + 6))
+    sweep(mid, m_src, m_a, m_b, (O - 1, O + 5))
+    for ix in range(2):
+        fold = row_residual(mid, m_src, m_b, O + 2 * ix) + row_residual(mid, m_src, m_b, O + 2 * ix + 1)
+        c_src[2 + ix, OWN_C, :] = (fold[0] + fold[1])[pairs4]
+    messages = []
+    for e in sorted(range(-REACH, REACH + 1), key=lambda e: -abs(e)):
+        for g in (1, -1, 0):
+            if (g, e) != (0, 0):
+                target = c_src.at[2 - 2 * g : 4 - 2 * g, OWN_C.start - 2 * e : OWN_C.stop - 2 * e, :]
+                messages.append((c_src.at[2:4, OWN_C, :], target, (g, e)))
+    exchange(COARSE_F, messages)
+
+    def keep_mid(x, _):
+        m_y[x, :, pairs4] = m_b[x, :, pairs4]
+        return 0
+
+    lax.fori_loop(O, O + 4, keep_mid, 0, unroll=True)
+    messages = []
+    for step in NEIGHBOURS:
+        ax, ay, bx, by = spans(*step, 4, 3 if step in corners else 4, 2)
+        messages.append((m_y.at[ax, :, ay, :], m_y.at[bx, :, by, :], step))
+    exchange(MID_V, messages)
 
     received(COEF_Y)
     coef = [c_coef[k, :, 8:24, :].reshape(128, 64).T for k in range(4)]
@@ -515,34 +548,6 @@
     main = coef[0] + (up_x + down_x) + (up_y + down_y) + (up_z + down_z)
     for at, band in enumerate((up_x, down_x, up_y, down_y, -down_z, main, -up_z)):
         c_bands[at] = band
-
-    for at in (FINE_X, FINE_Y, COEF_X, COEF_Y, MID_IN):
-        sent(at)
-
-    received(MID_F)
-    start_sweep(mid, m_src, m_a, (O - 2, O + 6))
-    sweep(mid, m_src, m_a, m_b, (O - 1, O + 5))
-    for ix in range(2):
-        fold = row_residual(mid, m_src, m_b, O + 2 * ix) + row_residual(mid, m_src, m_b, O + 2 * ix + 1)
-        c_src[2 + ix, OWN_C, :] = (fold[0] + fold[1])[pairs4]
-    messages = []
-    for e in sorted(range(-REACH, REACH + 1), key=lambda e: -abs(e)):
-        for g in (1, -1, 0):
-            if (g, e) != (0, 0):
-                target = c_src.at[2 - 2 * g : 4 - 2 * g, OWN_C.start - 2 * e : OWN_C.stop - 2 * e, :]
-                messages.append((c_src.at[2:4, OWN_C, :], target, (g, e)))
-    exchange(COARSE_F, messages)
-
-    def keep_mid(x, _):
-        m_y[x, :, pairs4] = m_b[x, :, pairs4]
-        return 0
-
-    lax.fori_loop(O, O + 4, keep_mid, 0, unroll=True)
-    messages = []
-    for step in NEIGHBOURS:
-        ax, ay, bx, by = spans(*step, 4, 3 if step in corners else 4, 2)
-        messages.append((m_y.at[ax, :, ay, :], m_y.at[bx, :, by, :], step))
-    exchange(MID_V, messages)
 
     def registers(at):
         return [c_bands[at, pl.ds(place, 8, stride=8), :] for place in range(8)]
@@ -619,7 +624,7 @@
         here, before = interface(64), interface(80)
         return tuple(inner[i] - (c_inverse[49 + i] * before + c_inverse[56 + i] * here) for i in range(7)) + (here,)
 
-    for at in (MID_F, FINE_V):
+    for at in (COEF_Y, MID_F, FINE_V):
         sent(at)
 
     received(COARSE_F)
@@ -673,7 +678,6 @@
     sweep(fine, f_src, f_a, f_b, (O - 2, O + 10))
     sweep(fine, f_src, f_b, f_a, (O - 1, O + 9))
 
-    together = one_hot((256, 256), lambda row, column: column == 2 * (row % 128) + row // 128)
 
     def in_order(field, result):
         def sort_back(x, _):
@@ -684,7 +688,7 @@
 
         lax.fori_loop(0, 8, sort_back, 0, unroll=True)
         halves = [f_rows[half, :, O : O + 8, :].reshape(64, 128) for half in range(2)]
-        result[...] = times_one_hot(jnp.concatenate(halves, axis=1), together, 3).reshape(8, 8, 256)
+        result[...] = times_one_hot(jnp.concatenate(halves, axis=1), together[...], 2).reshape(8, 8, 256)
 
     in_order(f_a, pressure)
 
@@ -732,6 +736,7 @@
             *[mid] * 11,
             pltpu.VMEM((8, 8, 128), f32),
             pltpu.VMEM((2, 8, 16, 128), f32),
+            pltpu.VMEM((256, 256), jnp.bfloat16),
             pltpu.VMEM((4, 8, 32, 64), f32),
             pltpu.VMEM((8, 32, 128), f32),
             pltpu.VMEM((6, 16, 128), f32),

time: 31.4 us -> 31.3 us (level)
  no operation moved by 1% of the time
where the time goes in v8:
time: 31.3 us; the launch traced here: 31.2 us
  Pallas kernels  30.5 us (97%)
  between operations  0.64 us (2%)
    pallas_call x1, Pallas kernels, local(): pl.pallas_call(functools.partial(kernel, count_x, count_y), out_shape=(pl...  29.8 us
    pallas_call x1, Pallas kernels, local(): pl.pallas_call(publish, out_shape=(out, out), in_specs=[in_vmem] * 2, out...  0.67 us

profile of v8, /device:TPU:6, one launch (start us, length us, event | category | flops | bytes accessed | tf_op | source)
XLA Modules:
  0.0 31.2 jit_solution(1334045925231231795)
XLA Ops:
  0.6 29.8 %shard_map.86 = (f32[8,8,256]{2,1,0:T(8,128)S(1)}, f32[8,8,256]{2,1,0:T(8,128)S(1)}) custom-call(f32[8,8,256]{2,1,0:T(8,128)} %rhs_h.1, f32[8,8,256]{2,1,0:T(8,128)} %store_f_h.1, f32[3,8,8,256]{3,2,1,0:T(8,128)} %mob_f_h.1, f32[4,4,128]{2,1,0:T(4,128)} %store_m_h.1, f32[3,4,4,128]{3,2,1,0:T(4,128)} %mob_m_h.1, f32[2,2,64]{2,1,0:T(2,128)} %store_c_h.1, ...), custom_call_target="tpu_custom_call" | custom-call | tf_op jit(solution)/shard_map/pallas_call | solution.py:725
  30.5 0.7 %shard_map.87 = (f32[8,8,256]{2,1,0:T(8,128)}, f32[8,8,256]{2,1,0:T(8,128)}) custom-call(f32[8,8,256]{2,1,0:T(8,128)S(1)} %get-tuple-element.4.pressure, f32[8,8,256]{2,1,0:T(8,128)S(1)} %get-tuple-element.5.residual), custom_call_target="tpu_custom_call" | custom-call | tf_op jit(solution)/shard_map/pallas_call | solution.py:758

commit v9 on v8

--- a/solution.py
+++ b/solution.py
@@ -51,19 +51,31 @@
 
 
 def next_y(values):
-    return next_paired(values, 0, values.ndim - 2)
+    return next_paired(values, 1, values.ndim - 2)
 
 
 def prev_y(values):
-    return prev_paired(values, 0, values.ndim - 2)
+    return prev_paired(values, 1, values.ndim - 2)
 
 
 def next_z(values):
-    return next_paired(values, 1, 3) if values.ndim == 4 else next_of(values, 2)
+    return next_paired(values, 2, 4) if values.ndim == 5 else next_of(values, 3)
 
 
 def prev_z(values):
-    return prev_paired(values, 1, 3) if values.ndim == 4 else prev_of(values, 2)
+    return prev_paired(values, 2, 4) if values.ndim == 5 else prev_of(values, 3)
+
+
+def blocks(level, rows):
+    first, last = rows
+    most = 4 if len(level[0].shape) == 5 else 6
+    count = -(-(last - first) // most)
+    edges = [first + (last - first) * at // count for at in range(count + 1)]
+    return [slice(*pair) for pair in zip(edges[:-1], edges[1:])]
+
+
+def moved(rows, by):
+    return slice(rows.start + by, rows.stop + by)
 
 
 def one_hot(shape, test):
@@ -104,72 +116,50 @@
 
 
 def weights_x(level, mob, rows):
-    wx = level[0]
-
-    def body(x, _):
-        wx[x] = harmonic(mob[0][x], mob[0][x + 1])
-        return 0
-
-    lax.fori_loop(*rows, body, 0, unroll=True)
+    for x in blocks(level, rows):
+        level[0][x] = harmonic(mob[0][x], mob[0][moved(x, 1)])
 
 
 def weights_yz(level, mob, rows, keep_y, keep_z):
     wx, wyu, wyd, wzu, wzd, diag, damp = level
-
-    def body(x, _):
+    for x in blocks(level, rows):
         second = mob[1][x]
-        third = mob[2][x]
         up_y = harmonic(second, next_y(second)) * keep_y
-        up_z = harmonic(third, next_z(third)) * keep_z
         wyu[x] = up_y
         wyd[x] = prev_y(up_y)
+        third = mob[2][x]
+        up_z = harmonic(third, next_z(third)) * keep_z
         wzu[x] = up_z
         wzd[x] = prev_z(up_z)
-        return 0
-
-    lax.fori_loop(*rows, body, 0, unroll=True)
 
 
 def diagonals(level, store, rows):
     wx, wyu, wyd, wzu, wzd, diag, damp = level
-
-    def body(x, _):
-        all_of_it = store[x] + (wx[x] + wx[x - 1]) + (wyu[x] + wyd[x]) + (wzu[x] + wzd[x])
+    for x in blocks(level, rows):
+        all_of_it = store[x] + (wx[x] + wx[moved(x, -1)]) + (wyu[x] + wyd[x]) + (wzu[x] + wzd[x])
         diag[x] = all_of_it
         damp[x] = DAMPING * reciprocal(all_of_it)
-        return 0
-
-    lax.fori_loop(*rows, body, 0, unroll=True)
-
-
-def row_residual(level, source, field, x):
+
+
+def residual_of(level, source, field, x):
     wx, wyu, wyd, wzu, wzd, diag, damp = level
     v = field[x]
     left = source[x] - diag[x] * v
-    left = left + (wx[x] * field[x + 1] + wx[x - 1] * field[x - 1])
+    left = left + (wx[x] * field[moved(x, 1)] + wx[moved(x, -1)] * field[moved(x, -1)])
     left = left + (wyu[x] * next_y(v) + wyd[x] * prev_y(v))
-    left = left + (wzu[x] * next_z(v) + wzd[x] * prev_z(v))
-    return left
+    return left + (wzu[x] * next_z(v) + wzd[x] * prev_z(v))
 
 
 def sweep(level, source, field, result, rows):
     damp = level[6]
-
-    def body(x, _):
-        result[x] = field[x] + damp[x] * row_residual(level, source, field, x)
-        return 0
-
-    lax.fori_loop(rows[0], rows[1], body, 0, unroll=True)
+    for x in blocks(level, rows):
+        result[x] = field[x] + damp[x] * residual_of(level, source, field, x)
 
 
 def start_sweep(level, source, result, rows):
     damp = level[6]
-
-    def body(x, _):
+    for x in blocks(level, rows):
         result[x] = damp[x] * source[x]
-        return 0
-
-    lax.fori_loop(rows[0], rows[1], body, 0, unroll=True)
 
 
 def kernel(
@@ -464,14 +454,14 @@
     for rows in ((O - 1, O + 2), (O + 6, O + 9)):
         sweep(fine, f_src, f_a, f_b, rows)
 
-    def folded(x, _):
-        both = row_residual(fine, f_src, f_b, O + 2 * x) + row_residual(fine, f_src, f_b, O + 2 * x + 1)
-        m_fold[x] = (both[0, 0] + both[0, 1]) + (both[1, 0] + both[1, 1])
+    for x in blocks(fine, (O, O + 8)):
+        left = residual_of(fine, f_src, f_b, x)
+        for pair in range(2):
+            both = left[2 * pair] + left[2 * pair + 1]
+            m_fold[(x.start - O) // 2 + pair] = (both[0, 0] + both[0, 1]) + (both[1, 0] + both[1, 1])
+    for x in range(4):
         for parity in range(2):
             m_src[O + x, parity, pairs4] = m_fold[x, pl.ds(OP + parity, 2, stride=2), :]
-        return 0
-
-    lax.fori_loop(0, 4, folded, 0, unroll=True)
     messages = []
     for step in NEIGHBOURS:
         ax, ay, bx, by = spans(*step, 4, 2 if step in corners else 3, 1 if step in corners else 2)
@@ -505,8 +495,9 @@
     received(MID_F)
     start_sweep(mid, m_src, m_a, (O - 2, O + 6))
     sweep(mid, m_src, m_a, m_b, (O - 1, O + 5))
+    left = residual_of(mid, m_src, m_b, own4)
     for ix in range(2):
-        fold = row_residual(mid, m_src, m_b, O + 2 * ix) + row_residual(mid, m_src, m_b, O + 2 * ix + 1)
+        fold = left[2 * ix] + left[2 * ix + 1]
         c_src[2 + ix, OWN_C, :] = (fold[0] + fold[1])[pairs4]
     messages = []
     for e in sorted(range(-REACH, REACH + 1), key=lambda e: -abs(e)):
@@ -692,11 +683,8 @@
 
     in_order(f_a, pressure)
 
-    def last(x, _):
-        f_b[x] = row_residual(fine, f_src, f_a, x)
-        return 0
-
-    lax.fori_loop(O, O + 8, last, 0, unroll=True)
+    for x in blocks(fine, (O, O + 8)):
+        f_b[x] = residual_of(fine, f_src, f_a, x)
     in_order(f_b, residual)
     for at in (COARSE_F, MID_V):
         sent(at)

time: 31.3 us -> 31.3 us (level)
  no operation moved by 1% of the time
where the time goes in v9:
time: 31.3 us; the launch traced here: 31.2 us
  Pallas kernels  30.5 us (97%)
  between operations  0.64 us (2%)
    pallas_call x1, Pallas kernels, local(): pl.pallas_call(functools.partial(kernel, count_x, count_y), out_shape=(pl...  29.9 us
    pallas_call x1, Pallas kernels, local(): pl.pallas_call(publish, out_shape=(out, out), in_specs=[in_vmem] * 2, out...  0.67 us

profile of v9, /device:TPU:6, one launch (start us, length us, event | category | flops | bytes accessed | tf_op | source)
XLA Modules:
  0.0 31.2 jit_solution(1523853280491294451)
XLA Ops:
  0.6 29.9 %shard_map.86 = (f32[8,8,256]{2,1,0:T(8,128)S(1)}, f32[8,8,256]{2,1,0:T(8,128)S(1)}) custom-call(f32[8,8,256]{2,1,0:T(8,128)} %rhs_h.1, f32[8,8,256]{2,1,0:T(8,128)} %store_f_h.1, f32[3,8,8,256]{3,2,1,0:T(8,128)} %mob_f_h.1, f32[4,4,128]{2,1,0:T(4,128)} %store_m_h.1, f32[3,4,4,128]{3,2,1,0:T(4,128)} %mob_m_h.1, f32[2,2,64]{2,1,0:T(2,128)} %store_c_h.1, ...), custom_call_target="tpu_custom_call" | custom-call | tf_op jit(solution)/shard_map/pallas_call | solution.py:713
  30.5 0.7 %shard_map.87 = (f32[8,8,256]{2,1,0:T(8,128)}, f32[8,8,256]{2,1,0:T(8,128)}) custom-call(f32[8,8,256]{2,1,0:T(8,128)S(1)} %get-tuple-element.4.pressure, f32[8,8,256]{2,1,0:T(8,128)S(1)} %get-tuple-element.5.residual), custom_call_target="tpu_custom_call" | custom-call | tf_op jit(solution)/shard_map/pallas_call | solution.py:746

commit v10 on v9

--- a/solution.py
+++ b/solution.py
@@ -402,9 +402,22 @@
     for copy in mid_in:
         copy.wait()
     messages = []
-    for step in NEIGHBOURS:
-        ax, ay, bx, by = spans(*step, 4, 3 if step in corners else 4, 2)
-        messages.append((m_in.at[:, ax, :, ay, :], m_in.at[:, bx, :, by, :], step))
+
+    def mid_part(first, last, step, wide_x, wide_y, beyond_y=0):
+        fields = slice(first, last + 1)
+        ax, ay, bx, by = spans(*step, 4, wide_x, wide_y)
+        if beyond_y and step[1] > 0:
+            ay, by = slice(ay.start, ay.stop - beyond_y), slice(by.start, by.stop - beyond_y)
+        elif beyond_y:
+            ay, by = slice(ay.start + beyond_y, ay.stop), slice(by.start + beyond_y, by.stop)
+        return (m_in.at[fields, ax, :, ay, :], m_in.at[fields, bx, :, by, :], step)
+
+    for step in faces_x:
+        messages += [mid_part(0, 0, step, 4, 1), mid_part(1, 3, step, 3, 1)]
+    for step in corners:
+        messages += [mid_part(0, 1, step, 3, 1), mid_part(0, 1, step, 1, 2, 1), mid_part(2, 3, step, 2, 1)]
+    for step in faces_y:
+        messages.append(mid_part(0, 3, step, 4, 2))
     exchange(MID_IN, messages)
 
     one = jnp.float32(1.0)

time: 31.3 us -> 30.9 us (0.987)
  Pallas kernels: 30.5 us -> 30.1 us
    pallas_call x1, Pallas kernels: 29.9 us -> 29.4 us  [local(): pl.pallas_call(functools.partial(kernel, count_x, count_y), out_shape=(pl...]
where the time goes in v10:
time: 30.9 us; the launch traced here: 30.7 us
  Pallas kernels  30.1 us (97%)
  between operations  0.64 us (2%)
    pallas_call x1, Pallas kernels, local(): pl.pallas_call(functools.partial(kernel, count_x, count_y), out_shape=(pl...  29.4 us
    pallas_call x1, Pallas kernels, local(): pl.pallas_call(publish, out_shape=(out, out), in_specs=[in_vmem] * 2, out...  0.67 us

profile of v10, /device:TPU:6, one launch (start us, length us, event | category | flops | bytes accessed | tf_op | source)
XLA Modules:
  0.0 30.7 jit_solution(10577857089418976964)
XLA Ops:
  0.6 29.4 %shard_map.86 = (f32[8,8,256]{2,1,0:T(8,128)S(1)}, f32[8,8,256]{2,1,0:T(8,128)S(1)}) custom-call(f32[8,8,256]{2,1,0:T(8,128)} %rhs_h.1, f32[8,8,256]{2,1,0:T(8,128)} %store_f_h.1, f32[3,8,8,256]{3,2,1,0:T(8,128)} %mob_f_h.1, f32[4,4,128]{2,1,0:T(4,128)} %store_m_h.1, f32[3,4,4,128]{3,2,1,0:T(4,128)} %mob_m_h.1, f32[2,2,64]{2,1,0:T(2,128)} %store_c_h.1, ...), custom_call_target="tpu_custom_call" | custom-call | tf_op jit(solution)/shard_map/pallas_call | solution.py:726
  30.1 0.7 %shard_map.87 = (f32[8,8,256]{2,1,0:T(8,128)}, f32[8,8,256]{2,1,0:T(8,128)}) custom-call(f32[8,8,256]{2,1,0:T(8,128)S(1)} %get-tuple-element.4.pressure, f32[8,8,256]{2,1,0:T(8,128)S(1)} %get-tuple-element.5.residual), custom_call_target="tpu_custom_call" | custom-call | tf_op jit(solution)/shard_map/pallas_call | solution.py:759

commit v11 on v10

--- a/solution.py
+++ b/solution.py
@@ -18,8 +18,8 @@
 OP = 2
 M0, M2, STORE, SOURCE, M1 = range(5)
 OWN_C = slice(15, 17)
-FINE_X, FINE_Y, COEF_X, COEF_Y, MID_IN, MID_F, FINE_V, COARSE_F, MID_V = range(9)
-EXCHANGES = 9
+FINE_X, FINE_Y, COEF_X, COEF_Y, MID_IN, MID_F, FINE_V, COARSE_F, MID_V, MID_OUT = range(10)
+EXCHANGES = 10
 NEIGHBOURS = ((1, 0), (-1, 0), (1, 1), (1, -1), (-1, 1), (-1, -1), (0, 1), (0, -1))
 
 
@@ -188,6 +188,7 @@
     f_b,
     f_x,
     m_in,
+    m_wide,
     m_src,
     m_wx,
     m_wyu,
@@ -403,19 +404,29 @@
         copy.wait()
     messages = []
 
-    def mid_part(first, last, step, wide_x, wide_y, beyond_y=0):
+    def without(span, step, beyond):
+        return slice(span.start, span.stop - beyond) if step > 0 else slice(span.start + beyond, span.stop)
+
+    def mid_part(first, last, step, wide_x, wide_y, beyond_x=0, beyond_y=0):
         fields = slice(first, last + 1)
         ax, ay, bx, by = spans(*step, 4, wide_x, wide_y)
-        if beyond_y and step[1] > 0:
-            ay, by = slice(ay.start, ay.stop - beyond_y), slice(by.start, by.stop - beyond_y)
-        elif beyond_y:
-            ay, by = slice(ay.start + beyond_y, ay.stop), slice(by.start + beyond_y, by.stop)
-        return (m_in.at[fields, ax, :, ay, :], m_in.at[fields, bx, :, by, :], step)
-
+        if beyond_x:
+            ax, bx = without(ax, step[0], beyond_x), without(bx, step[0], beyond_x)
+        if beyond_y:
+            ay, by = without(ay, step[1], beyond_y), without(by, step[1], beyond_y)
+        landing = m_wide if beyond_x or beyond_y else m_in
+        if landing is m_wide:
+            late.append((fields, bx, slice(0, 2), by))
+        return (m_in.at[fields, ax, :, ay, :], landing.at[fields, bx, :, by, :], step)
+
+    late = []
+    outer = []
     for step in faces_x:
-        messages += [mid_part(0, 0, step, 4, 1), mid_part(1, 3, step, 3, 1)]
+        messages += [mid_part(0, 0, step, 3, 1), mid_part(1, 3, step, 2, 1)]
+        outer += [mid_part(0, 0, step, 4, 1, 3), mid_part(1, 3, step, 3, 1, 2)]
     for step in corners:
-        messages += [mid_part(0, 1, step, 3, 1), mid_part(0, 1, step, 1, 2, 1), mid_part(2, 3, step, 2, 1)]
+        messages += [mid_part(0, 1, step, 2, 1), mid_part(2, 3, step, 1, 1)]
+        outer += [mid_part(0, 1, step, 3, 1, 2), mid_part(0, 1, step, 1, 2, 0, 1), mid_part(2, 3, step, 2, 1, 1)]
     for step in faces_y:
         messages.append(mid_part(0, 3, step, 4, 2))
     exchange(MID_IN, messages)
@@ -480,6 +491,7 @@
         ax, ay, bx, by = spans(*step, 4, 2 if step in corners else 3, 1 if step in corners else 2)
         messages.append((m_src.at[ax, :, ay, :], m_src.at[bx, :, by, :], step))
     exchange(MID_F, messages)
+    exchange(MID_OUT, outer)
 
     def keep_fine(x, _):
         f_x[x, :, :, pairs8] = f_b[x, :, :, pairs8]
@@ -495,13 +507,16 @@
     mid = (m_wx, m_wyu, m_wyd, m_wzu, m_wzd, m_diag, m_damp)
     m_mob = (m_in.at[0], m_in.at[1], m_in.at[2])
     keep_y, keep_z = keep_yz(4, (2, 8, 128))
+
+    def mid_weights(reach):
+        weights_x(mid, m_mob, (O - 1 - reach, O + 4 + reach))
+        m_wx[O - 1] = m_wx[O - 1] * keep_x[0]
+        m_wx[O + 3] = m_wx[O + 3] * keep_x[1]
+        weights_yz(mid, m_mob, (O - reach, O + 4 + reach), keep_y, keep_z)
+        diagonals(mid, m_in.at[3], (O - reach, O + 4 + reach))
+
     received(MID_IN)
-    weights_x(mid, m_mob, (O - 4, O + 7))
-    m_wx[O - 1] = m_wx[O - 1] * keep_x[0]
-    m_wx[O + 3] = m_wx[O + 3] * keep_x[1]
-    weights_yz(mid, m_mob, (O - 3, O + 7), keep_y, keep_z)
-    diagonals(mid, m_in.at[3], (O - 3, O + 7))
-
+    mid_weights(2)
     for at in (FINE_X, FINE_Y, COEF_X, MID_IN):
         sent(at)
 
@@ -628,7 +643,11 @@
         here, before = interface(64), interface(80)
         return tuple(inner[i] - (c_inverse[49 + i] * before + c_inverse[56 + i] * here) for i in range(7)) + (here,)
 
-    for at in (COEF_Y, MID_F, FINE_V):
+    received(MID_OUT)
+    for region in late:
+        m_in[region] = m_wide[region]
+    mid_weights(3)
+    for at in (COEF_Y, MID_F, FINE_V, MID_OUT):
         sent(at)
 
     received(COARSE_F)
@@ -733,6 +752,7 @@
             pltpu.VMEM((2, 40, 8, 128), f32),
             pltpu.VMEM((5, 8 + 2 * O, 2, 2, 8, 128), f32),
             *[fine] * 10,
+            pltpu.VMEM((4, 4 + 2 * O, 2, 8, 128), f32),
             pltpu.VMEM((4, 4 + 2 * O, 2, 8, 128), f32),
             *[mid] * 11,
             pltpu.VMEM((8, 8, 128), f32),

time: 30.9 us -> 30.8 us (level)
  no operation moved by 1% of the time
where the time goes in v11:
time: 30.8 us; the launch traced here: 30.5 us
  Pallas kernels  29.9 us (97%)
  between operations  0.64 us (2%)
    pallas_call x1, Pallas kernels, local(): pl.pallas_call(functools.partial(kernel, count_x, count_y), out_shape=(pl...  29.2 us
    pallas_call x1, Pallas kernels, local(): pl.pallas_call(publish, out_shape=(out, out), in_specs=[in_vmem] * 2, out...  0.67 us

profile of v11, /device:TPU:6, one launch (start us, length us, event | category | flops | bytes accessed | tf_op | source)
XLA Modules:
  0.0 30.5 jit_solution(17579132158022622830)
XLA Ops:
  0.6 29.2 %shard_map.86 = (f32[8,8,256]{2,1,0:T(8,128)S(1)}, f32[8,8,256]{2,1,0:T(8,128)S(1)}) custom-call(f32[8,8,256]{2,1,0:T(8,128)} %rhs_h.1, f32[8,8,256]{2,1,0:T(8,128)} %store_f_h.1, f32[3,8,8,256]{3,2,1,0:T(8,128)} %mob_f_h.1, f32[4,4,128]{2,1,0:T(4,128)} %store_m_h.1, f32[3,4,4,128]{3,2,1,0:T(4,128)} %mob_m_h.1, f32[2,2,64]{2,1,0:T(2,128)} %store_c_h.1, ...), custom_call_target="tpu_custom_call" | custom-call | tf_op jit(solution)/shard_map/pallas_call | solution.py:745
  29.8 0.7 %shard_map.87 = (f32[8,8,256]{2,1,0:T(8,128)}, f32[8,8,256]{2,1,0:T(8,128)}) custom-call(f32[8,8,256]{2,1,0:T(8,128)S(1)} %get-tuple-element.4.pressure, f32[8,8,256]{2,1,0:T(8,128)S(1)} %get-tuple-element.5.residual), custom_call_target="tpu_custom_call" | custom-call | tf_op jit(solution)/shard_map/pallas_call | solution.py:779

commit v12 on v10

--- a/solution.py
+++ b/solution.py
@@ -481,17 +481,6 @@
         messages.append((m_src.at[ax, :, ay, :], m_src.at[bx, :, by, :], step))
     exchange(MID_F, messages)
 
-    def keep_fine(x, _):
-        f_x[x, :, :, pairs8] = f_b[x, :, :, pairs8]
-        return 0
-
-    lax.fori_loop(O, O + 8, keep_fine, 0, unroll=True)
-    messages = []
-    for step in NEIGHBOURS:
-        ax, ay, bx, by = spans(*step, 8, 2 if step in corners else 3, 1 if step in corners else 2)
-        messages.append((f_x.at[ax, :, :, ay, :], f_x.at[bx, :, :, by, :], step))
-    exchange(FINE_V, messages)
-
     mid = (m_wx, m_wyu, m_wyd, m_wzu, m_wzd, m_diag, m_damp)
     m_mob = (m_in.at[0], m_in.at[1], m_in.at[2])
     keep_y, keep_z = keep_yz(4, (2, 8, 128))
@@ -530,6 +519,17 @@
         ax, ay, bx, by = spans(*step, 4, 3 if step in corners else 4, 2)
         messages.append((m_y.at[ax, :, ay, :], m_y.at[bx, :, by, :], step))
     exchange(MID_V, messages)
+
+    def keep_fine(x, _):
+        f_x[x, :, :, pairs8] = f_b[x, :, :, pairs8]
+        return 0
+
+    lax.fori_loop(O, O + 8, keep_fine, 0, unroll=True)
+    messages = []
+    for step in NEIGHBOURS:
+        ax, ay, bx, by = spans(*step, 8, 2 if step in corners else 3, 1 if step in corners else 2)
+        messages.append((f_x.at[ax, :, :, ay, :], f_x.at[bx, :, :, by, :], step))
+    exchange(FINE_V, messages)
 
     received(COEF_Y)
     coef = [c_coef[k, :, 8:24, :].reshape(128, 64).T for k in range(4)]
@@ -628,7 +628,7 @@
         here, before = interface(64), interface(80)
         return tuple(inner[i] - (c_inverse[49 + i] * before + c_inverse[56 + i] * here) for i in range(7)) + (here,)
 
-    for at in (COEF_Y, MID_F, FINE_V):
+    for at in (COEF_Y, MID_F):
         sent(at)
 
     received(COARSE_F)
@@ -699,7 +699,7 @@
     for x in blocks(fine, (O, O + 8)):
         f_b[x] = residual_of(fine, f_src, f_a, x)
     in_order(f_b, residual)
-    for at in (COARSE_F, MID_V):
+    for at in (COARSE_F, MID_V, FINE_V):
         sent(at)
 
 

time: 30.9 us -> 31 us (level)
  no operation moved by 1% of the time
where the time goes in v12:
time: 31 us; the launch traced here: 30.8 us
  Pallas kernels  30.2 us (97%)
  between operations  0.64 us (2%)
    pallas_call x1, Pallas kernels, local(): pl.pallas_call(functools.partial(kernel, count_x, count_y), out_shape=(pl...  29.5 us
    pallas_call x1, Pallas kernels, local(): pl.pallas_call(publish, out_shape=(out, out), in_specs=[in_vmem] * 2, out...  0.67 us

profile of v12, /device:TPU:6, one launch (start us, length us, event | category | flops | bytes accessed | tf_op | source)
XLA Modules:
  0.0 30.8 jit_solution(992818799833939142)
XLA Ops:
  0.6 29.5 %shard_map.86 = (f32[8,8,256]{2,1,0:T(8,128)S(1)}, f32[8,8,256]{2,1,0:T(8,128)S(1)}) custom-call(f32[8,8,256]{2,1,0:T(8,128)} %rhs_h.1, f32[8,8,256]{2,1,0:T(8,128)} %store_f_h.1, f32[3,8,8,256]{3,2,1,0:T(8,128)} %mob_f_h.1, f32[4,4,128]{2,1,0:T(4,128)} %store_m_h.1, f32[3,4,4,128]{3,2,1,0:T(4,128)} %mob_m_h.1, f32[2,2,64]{2,1,0:T(2,128)} %store_c_h.1, ...), custom_call_target="tpu_custom_call" | custom-call | tf_op jit(solution)/shard_map/pallas_call | solution.py:726
  30.2 0.7 %shard_map.87 = (f32[8,8,256]{2,1,0:T(8,128)}, f32[8,8,256]{2,1,0:T(8,128)}) custom-call(f32[8,8,256]{2,1,0:T(8,128)S(1)} %get-tuple-element.4.pressure, f32[8,8,256]{2,1,0:T(8,128)S(1)} %get-tuple-element.5.residual), custom_call_target="tpu_custom_call" | custom-call | tf_op jit(solution)/shard_map/pallas_call | solution.py:759
